TPU v7x, 32 devices: a whole 2x2x4 slice. The times are simulated.
32 devices in a mesh: groups: 2 (over y), expert: 4 (over z), tensor: 2 (over x), dp: 2 (over core).
Axes of the slice: x: 2, y: 2, z: 4, core: 2. Of those that a mesh axis runs over, the one named last changes fastest.
Arguments:
- activations: bfloat16 [512, 2048], P(('groups', 'expert', 'dp'), 'tensor'), parts along dimension 0, may hold values from -6 to 6
- out_grad: bfloat16 [512, 2048], P(('groups', 'expert', 'dp'), 'tensor'), parts along dimension 0, may hold values from -1.5 to 1.5
- expert_ids: int32 [512, 8], P(('groups', 'expert', 'dp')), parts along dimension 0, may hold values from 0 to 31, all different within a row; in each aligned block of 32 rows (0 to 31, 32 to 63, ...) at most 16 rows name the same one
- gate_probs: bfloat16 [512, 8], P(('groups', 'expert', 'dp')), parts along dimension 0, may hold values from 0.049804688 to 0.5
- w_gate: bfloat16 [32, 2048, 768], P('expert', None, 'tensor'), may hold values from -0.125 to 0.125
- w_up: bfloat16 [32, 2048, 768], P('expert', None, 'tensor'), may hold values from -0.125 to 0.125
- w_down: bfloat16 [32, 768, 2048], P('expert', 'tensor'), may hold values from -0.21875 to 0.21875
Outputs:
- grad_activations: bfloat16 [512, 2048], P(('groups', 'expert', 'dp'), 'tensor'), parts along dimension 0
- grad_probs: float32 [512, 8], P(('groups', 'expert', 'dp')), parts along dimension 0
- grad_gate: bfloat16 [64, 2048, 768], P(('groups', 'expert'), None, 'tensor'), parts along dimension 0
- grad_up: bfloat16 [64, 2048, 768], P(('groups', 'expert'), None, 'tensor'), parts along dimension 0
- grad_down: bfloat16 [64, 768, 2048], P(('groups', 'expert'), 'tensor'), parts along dimension 0
There are 2 independent parts, one for each index of `groups`. A program takes and returns all parts, laid end to end along the dimension named above; an argument that names none is the same for every part. Nothing has to cross between parts.
Inputs may be any that keep to these rules, and one draw needn't show every extreme that they name: `expert_ids`: among the 8 entries of a row, no expert appears twice. Among the 32 rows of one device, no expert appears in more than 16 rows, and in every draw some expert appears in exactly 16 of them.
All inputs are finite; a program needn't handle non-finite values.
Results may differ from a plain program's by a relative error of at most 0.009.
Values may be sent and summed in bfloat16 or wider, within the bound.
No kernel may reach another device: no remote copies, remote signals or barrier semaphores. Data moves between devices by JAX's collectives and lax.ppermute only.
A program may use at most 256 MiB of HBM per device.

v0:
```python
import jax
import jax.numpy as jnp
from jax import lax
from jax.sharding import PartitionSpec as P

D = 2048
TOP = 8
CAP = 16


def body(activations, out_grad, expert_ids, gate_probs, w_gate, w_up, w_down):
    expert_count = lax.axis_size("expert")
    local_count = w_gate.shape[0]
    experts = expert_count * local_count
    token_rows = expert_ids.shape[0]
    flat_ids = expert_ids.reshape(-1)
    onehot = (flat_ids[:, None] == jnp.arange(experts, dtype=jnp.int32)[None, :]).astype(jnp.int32)
    before = jnp.cumsum(onehot, axis=0) - onehot
    slot_index = jnp.sum(before * onehot, axis=1)
    position = (flat_ids * CAP + slot_index).reshape(token_rows, TOP)
    lane_index = jnp.arange(experts * CAP, dtype=jnp.int32)
    matches = position[None, :, :] == lane_index[:, None, None]
    placing = jnp.sum(matches.astype(jnp.int32), axis=2).astype(jnp.bfloat16)
    send_probs = jnp.sum(jnp.where(matches, gate_probs.astype(jnp.float32)[None], 0.0), axis=(1, 2))
    send_probs = send_probs.astype(jnp.bfloat16).reshape(experts, CAP)
    full_rows, full_grads = (
        lax.all_gather(activations, "tensor", axis=1, tiled=True),
        lax.all_gather(out_grad, "tensor", axis=1, tiled=True),
    )
    send_rows = (
        jnp.dot(placing, full_rows, preferred_element_type=jnp.float32)
        .astype(jnp.bfloat16)
        .reshape(experts, CAP, D)
    )
    send_grads = (
        jnp.dot(placing, full_grads, preferred_element_type=jnp.float32)
        .astype(jnp.bfloat16)
        .reshape(experts, CAP, D)
    )
    got_rows, got_grads, got_probs = (
        lax.all_to_all(send_rows, "expert", split_axis=0, concat_axis=0, tiled=True),
        lax.all_to_all(send_grads, "expert", split_axis=0, concat_axis=0, tiled=True),
        lax.all_to_all(send_probs, "expert", split_axis=0, concat_axis=0, tiled=True),
    )
    rows_in = got_rows.reshape(expert_count, local_count, CAP, D)
    grads_in = got_grads.reshape(expert_count, local_count, CAP, D)
    row_probs = got_probs.reshape(expert_count, local_count, CAP, 1).astype(jnp.float32)
    gate_pre = jnp.einsum("slcd,ldf->slcf", rows_in, w_gate, preferred_element_type=jnp.float32)
    up_pre = jnp.einsum("slcd,ldf->slcf", rows_in, w_up, preferred_element_type=jnp.float32)
    hidden_grad = jnp.einsum("slcd,lfd->slcf", grads_in, w_down, preferred_element_type=jnp.float32)
    sigma = jax.nn.sigmoid(gate_pre)
    activated = gate_pre * sigma
    hidden = activated * up_pre
    inner_part = jnp.sum(hidden * hidden_grad, axis=3)
    weighted = (row_probs * hidden).astype(jnp.bfloat16)
    scaled = row_probs * hidden_grad
    gate_grad = (scaled * up_pre * sigma * (1.0 + gate_pre * (1.0 - sigma))).astype(jnp.bfloat16)
    up_grad = (scaled * activated).astype(jnp.bfloat16)
    row_part = jnp.einsum("slcf,ldf->slcd", gate_grad, w_gate, preferred_element_type=jnp.float32)
    row_part = row_part + jnp.einsum(
        "slcf,ldf->slcd", up_grad, w_up, preferred_element_type=jnp.float32
    )
    gate_total = jnp.einsum(
        "slcd,slcf->ldf", rows_in, gate_grad, preferred_element_type=jnp.float32
    )
    up_total = jnp.einsum("slcd,slcf->ldf", rows_in, up_grad, preferred_element_type=jnp.float32)
    down_total = jnp.einsum(
        "slcf,slcd->lfd", weighted, grads_in, preferred_element_type=jnp.float32
    )
    lanes = experts * CAP
    own_part = lax.psum_scatter(
        row_part.astype(jnp.bfloat16), "tensor", scatter_dimension=3, tiled=True
    ).astype(jnp.float32)
    inner_sum = lax.psum(inner_part.astype(jnp.bfloat16), "tensor").astype(jnp.float32)
    quarter = own_part.shape[3]
    returned_rows, returned_inner = (
        lax.all_to_all(
            own_part.reshape(experts, CAP, quarter).astype(jnp.bfloat16),
            "expert",
            split_axis=0,
            concat_axis=0,
            tiled=True,
        ).astype(jnp.float32),
        lax.all_to_all(
            inner_sum.reshape(experts, CAP).astype(jnp.bfloat16),
            "expert",
            split_axis=0,
            concat_axis=0,
            tiled=True,
        ).astype(jnp.float32),
    )
    placing_wide = jnp.sum(matches.astype(jnp.int32), axis=2).astype(jnp.float32)
    token_grad = lax.dot_general(
        placing_wide,
        returned_rows.reshape(lanes, quarter),
        (((0,), (0,)), ((), ())),
        precision=lax.Precision.HIGHEST,
        preferred_element_type=jnp.float32,
    )
    grad_probs = jnp.sum(
        jnp.where(matches, returned_inner.reshape(lanes)[:, None, None], 0.0), axis=0
    )
    gate_sum, up_sum, down_sum = (
        lax.psum(gate_total.astype(jnp.bfloat16), "dp").astype(jnp.float32),
        lax.psum(up_total.astype(jnp.bfloat16), "dp").astype(jnp.float32),
        lax.psum(down_total.astype(jnp.bfloat16), "dp").astype(jnp.float32),
    )
    return (
        token_grad.astype(jnp.bfloat16),
        grad_probs,
        gate_sum.astype(jnp.bfloat16),
        up_sum.astype(jnp.bfloat16),
        down_sum.astype(jnp.bfloat16),
    )


def solution(mesh):
    in_specs = (
        P(("groups", "expert", "dp"), "tensor"),
        P(("groups", "expert", "dp"), "tensor"),
        P(("groups", "expert", "dp"), None),
        P(("groups", "expert", "dp"), None),
        P("expert", None, "tensor"),
        P("expert", None, "tensor"),
        P("expert", "tensor", None),
    )
    out_specs = (
        P(("groups", "expert", "dp"), "tensor"),
        P(("groups", "expert", "dp"), None),
        P(("groups", "expert"), None, "tensor"),
        P(("groups", "expert"), None, "tensor"),
        P(("groups", "expert"), "tensor", None),
    )
    return jax.shard_map(body, mesh=mesh, in_specs=in_specs, out_specs=out_specs, check_vma=False)
```

profile of v0, /device:TPU:0, one launch (start us, length us, event | category | flops | bytes accessed | tf_op | source)
XLA Modules:
  0.0 342.5 jit_solution(17029019497911361153)
XLA Ops:
  8.0 0.0 copy-start.3
  8.0 0.8 copy.68
  8.8 0.1 eq.42
  8.9 0.1 eq.38
  9.0 0.6 reduce-window.6
  9.6 0.2 slice_reduce_fusion
  9.8 0.1 fusion.42
  9.9 0.1 reduce_sum.52
  10.0 0.2 convert_reduce_fusion
  10.3 6.1 %all_gather.7 = bf16[32,2048]{1,0:T(8,128)(2,1)S(1)} all-gather(bf16[32,1024]{1,0:T(8,128)(2,1)} %param.7), channel_id=1, replica_groups=mesh['groups'=2,'expert'=4,'tensor'=2,'dp'=2] {'tensor'}, dimensions={1}, use_global_device_ids=true | all-gather | bytes 196608 | tf_op jit(solution)/shard_map/all_gather | solution.py:27
  16.4 2.1 convolution_convert_fusion
  18.4 5.4 %all-to-all-start.2 = ((bf16[32,16,2048]{2,1,0:T(8,128)(2,1)}), bf16[32,16,2048]{2,1,0:T(8,128)(2,1)S(1)}, u32[]{:S(2)}, u32[]{:S(2)}) async-start(bf16[32,16,2048]{2,1,0:T(8,128)(2,1)} %bitcast.85), calls=%async_computation.2 | async-start | bytes 4194304 | tf_op jit(solution)/shard_map/all_to_all | solution.py:41
  23.8 0.0 copy-done.3
  23.8 4.9 %all_gather.6 = bf16[32,2048]{1,0:T(8,128)(2,1)S(1)} all-gather(bf16[32,1024]{1,0:T(8,128)(2,1)S(1)} %copy-done.3), channel_id=1, replica_groups=mesh['groups'=2,'expert'=4,'tensor'=2,'dp'=2] {'tensor'}, dimensions={1}, use_global_device_ids=true | all-gather | bytes 196608 | tf_op jit(solution)/shard_map/all_gather | solution.py:28
  28.7 2.0 convolution_convert_fusion.1
  30.8 40.1 %all-to-all-done.2 = bf16[32,16,2048]{2,1,0:T(8,128)(2,1)S(1)} async-done(((bf16[32,16,2048]{2,1,0:T(8,128)(2,1)}), bf16[32,16,2048]{2,1,0:T(8,128)(2,1)S(1)}, u32[]{:S(2)}, u32[]{:S(2)}) %all-to-all-start.2) | async-done | bytes 2097184 | tf_op jit(solution)/shard_map/all_to_all | solution.py:41
  70.8 4.4 %all-to-all-start.1 = ((bf16[32,16,2048]{2,1,0:T(8,128)(2,1)}), bf16[32,16,2048]{2,1,0:T(8,128)(2,1)}, u32[]{:S(2)}, u32[]{:S(2)}) async-start(bf16[32,16,2048]{2,1,0:T(8,128)(2,1)} %bitcast.84), calls=%async_computation.1 | async-start | bytes 4194304 | tf_op jit(solution)/shard_map/all_to_all | solution.py:42
  75.3 6.6 %fusion.29 = f32[4,8,16,384]{3,2,0,1:T(8,128)S(1)} fusion(bf16[8,2048,384]{2,1,0:T(8,128)(2,1)} %param.11, bf16[4,8,16,2048]{3,2,1,0:T(8,128)(2,1)S(1)} %bitcast.78), kind=kOutput, calls=%fused_computation.23 | convolution fusion | flops 805306368 | bytes 15466496 | tf_op jit(solution)/shard_map/slcd,ldf->slcf/dot_general | solution.py:48
  81.9 7.4 %fusion.19 = f32[4,8,16,384]{3,2,0,1:T(8,128)} fusion(bf16[8,2048,384]{2,1,0:T(8,128)(2,1)} %param.12, bf16[4,8,16,2048]{3,2,1,0:T(8,128)(2,1)S(1)} %bitcast.79), kind=kOutput, calls=%fused_computation.21 | convolution fusion | flops 805306368 | bytes 15466496 | tf_op jit(solution)/shard_map/slcd,ldf->slcf/dot_general | solution.py:49
  89.3 33.7 %all-to-all-done.1 = bf16[32,16,2048]{2,1,0:T(8,128)(2,1)} async-done(((bf16[32,16,2048]{2,1,0:T(8,128)(2,1)}), bf16[32,16,2048]{2,1,0:T(8,128)(2,1)}, u32[]{:S(2)}, u32[]{:S(2)}) %all-to-all-start.1) | async-done | bytes 2097184 | tf_op jit(solution)/shard_map/all_to_all | solution.py:42
  123.0 0.0 copy-start.4
  123.0 10.2 %multiply_reduce_fusion = (bf16[4,8,16]{2,0,1:T(4,128)(2,1)S(1)}, f32[4,8,16,384]{3,2,0,1:T(8,128)}) fusion(f32[4,8,16,384]{3,2,0,1:T(8,128)} %fusion.19, f32[4,8,16,384]{3,2,0,1:T(8,128)S(1)} %fusion.29, bf16[8,384,2048]{2,1,0:T(8,128)(2,1)} %param.13, bf16[4,8,16,2048]{3,2,1,0:T(8,128)(2,1)} %bitcast.2), kind=kOutput, calls=%fused_computation.26 | convolution fusion | flops 806682112 | bytes 17040384 | tf_op jit(solution)/shard_map/slcd,lfd->slcf/dot_general | solution.py:50
  133.3 5.0 %psum.28 = bf16[4,8,16]{2,0,1:T(4,128)(2,1)S(1)} all-reduce(bf16[4,8,16]{2,0,1:T(4,128)(2,1)S(1)} %get-tuple-element.17), channel_id=1, replica_groups=mesh['groups'=2,'expert'=4,'tensor'=2,'dp'=2] {'tensor'}, use_global_device_ids=true, to_apply=%region_7.8 | all-reduce | flops 512 | bytes 2048 | tf_op jit(solution)/shard_map/psum | solution.py:74
  138.2 0.6 copy.78
  138.9 3.2 all-to-all-start.4
  142.1 0.0 reduce-scatter.2.cloned.1.call-start
  142.2 0.0 copy-done.4
  142.2 0.1 copy.72
  142.3 5.4 %all-to-all-done.4 = bf16[4,8,16]{2,1,0:T(8,128)(2,1)S(1)} async-done(((bf16[4,8,16]{2,1,0:T(8,128)(2,1)}), bf16[4,8,16]{2,1,0:T(8,128)(2,1)S(1)}, u32[]{:S(2)}, u32[]{:S(2)}) %all-to-all-start.4) | async-done | bytes 1056 | tf_op jit(solution)/shard_map/all_to_all | solution.py:84
  147.7 0.1 reshape.81
  147.8 0.2 select_reduce_fusion
  148.0 0.1 convert_element_type.101
  148.1 7.9 %all_to_all.27 = bf16[4,8,16]{2,1,0:T(8,128)(2,1)S(1)} all-to-all(bf16[4,8,16]{2,1,0:T(8,128)(2,1)S(1)} %convert_element_type.101), channel_id=1, replica_groups=mesh['groups'=2,'expert'=4,'tensor'=2,'dp'=2] {'expert'}, dimensions={0} | all-to-all | bytes 2048 | tf_op jit(solution)/shard_map/all_to_all | solution.py:43
  156.0 1.8 multiply_convert_fusion.1
  157.8 0.0 copy-start.1
  157.8 8.8 %fusion = f32[8,4,16,2048]{3,2,1,0:T(8,128)S(1)} fusion(bf16[4,8,16,384]{3,2,0,1:T(8,128)(2,1)S(1)} %get-tuple-element.16, bf16[8,2048,384]{2,1,0:T(8,128)(2,1)} %param.11), kind=kOutput, calls=%fused_computation.3 | convolution fusion | flops 805306368 | bytes 17170432 | tf_op jit(solution)/shard_map/slcf,ldf->slcd/dot_general | solution.py:59
  166.6 0.0 copy-done.1
  166.6 10.0 %fusion.12 = bf16[4,8,16,2048]{3,2,0,1:T(8,128)(2,1)} fusion(f32[8,4,16,2048]{3,2,1,0:T(8,128)S(1)} %fusion, bf16[4,8,16,384]{3,2,0,1:T(8,128)(2,1)S(1)} %get-tuple-element.15, bf16[8,2048,384]{2,1,0:T(8,128)(2,1)} %param.12), kind=kOutput, calls=%fused_computation.16 | convolution fusion | flops 807403520 | bytes 19267584 | tf_op jit(solution)/shard_map/slcf,ldf->slcd/dot_general | solution.py:60
  176.6 0.0 reduce-scatter.2.cloned.1.call-update
  176.6 0.0 all-reduce.3.cloned.1.call-start
  176.6 10.2 %bitcast_convert_fusion = bf16[8,384,2048]{2,1,0:T(8,128)(2,1)} fusion(bf16[4,8,16,2048]{3,2,1,0:T(8,128)(2,1)} %bitcast.2, f32[4,8,16]{2,0,1:T(4,128)S(1)} %copy.73, f32[4,8,16,384]{3,2,0,1:T(8,128)} %fusion.19, f32[4,8,16,384]{3,2,0,1:T(8,128)S(1)} %fusion.29), kind=kOutput, calls=%fused_computation | convolution fusion | flops 812974080 | bytes 16254976 | tf_op jit(solution)/shard_map/slcf,slcd->lfd/dot_general | solution.py:67
  186.8 0.0 copy-start.2
  186.8 6.6 %bitcast_convert_fusion.1 = bf16[8,2048,384]{2,1,0:T(8,128)(2,1)} fusion(bf16[4,8,16,2048]{3,2,1,0:T(8,128)(2,1)S(1)} %bitcast.80, bf16[4,8,16,384]{3,2,0,1:T(8,128)(2,1)S(1)} %get-tuple-element.15), kind=kOutput, calls=%fused_computation.1 | convolution fusion | flops 811597824 | bytes 15073280 | tf_op jit(solution)/shard_map/slcd,slcf->ldf/dot_general | solution.py:66
  193.4 0.0 copy-done.2
  193.4 6.6 %bitcast_convert_fusion.2 = bf16[8,2048,384]{2,1,0:T(8,128)(2,1)} fusion(bf16[4,8,16,2048]{3,2,1,0:T(8,128)(2,1)S(1)} %bitcast.81, bf16[4,8,16,384]{3,2,0,1:T(8,128)(2,1)S(1)} %copy-done.2), kind=kOutput, calls=%fused_computation.2 | convolution fusion | flops 811597824 | bytes 15073280 | tf_op jit(solution)/shard_map/slcd,slcf->ldf/dot_general | solution.py:63
  200.0 0.0 all-reduce.3.cloned.1.call-update
  200.1 6.8 %reduce-scatter.2.cloned.1.call-done = bf16[4,8,16,1024]{3,2,0,1:T(8,128)(2,1)} async-done(((bf16[4,8,16,2048]{3,2,0,1:T(8,128)(2,1)}), bf16[4,8,16,1024]{3,2,0,1:T(8,128)(2,1)}) %reduce-scatter.2.cloned.1.call-update) | async-done | bytes 1048592 | tf_op jit(solution)/shard_map/reduce_scatter | solution.py:71
  206.8 2.6 copy.77
  209.5 4.5 %all-to-all-start.3 = ((bf16[32,16,1024]{2,1,0:T(8,128)(2,1)}), bf16[32,16,1024]{2,1,0:T(8,128)(2,1)S(1)}, u32[]{:S(2)}, u32[]{:S(2)}) async-start(bf16[32,16,1024]{2,1,0:T(8,128)(2,1)} %bitcast.16), calls=%async_computation.4 | async-start | bytes 2097152 | tf_op jit(solution)/shard_map/all_to_all | solution.py:77
  214.0 0.7 copy.82
  214.7 24.8 %all-to-all-done.3 = bf16[32,16,1024]{2,1,0:T(8,128)(2,1)S(1)} async-done(((bf16[32,16,1024]{2,1,0:T(8,128)(2,1)}), bf16[32,16,1024]{2,1,0:T(8,128)(2,1)S(1)}, u32[]{:S(2)}, u32[]{:S(2)}) %all-to-all-start.3) | async-done | bytes 1048608 | tf_op jit(solution)/shard_map/all_to_all | solution.py:77
  239.5 1.2 convolution_convert_fusion.2
  240.7 68.5 %all-reduce.3.cloned.1.call-done = (bf16[8,2048,384]{2,1,0:T(8,128)(2,1)}, bf16[8,2048,384]{2,1,0:T(8,128)(2,1)}, bf16[8,384,2048]{2,1,0:T(8,128)(2,1)}) async-done(((bf16[8,2048,384]{2,1,0:T(8,128)(2,1)}, bf16[8,2048,384]{2,1,0:T(8,128)(2,1)}, bf16[8,384,2048]{2,1,0:T(8,128)(2,1)}), (bf16[8,2048,384]{2,1,0:T(8,128)(2,1)}, bf16[8,2048,384]{2,1,0:T(8,128)(2,1)}, ...) | async-done | bytes 37748752 | tf_op jit(solution)/shard_map/psum | solution.py:104
  309.2 0.0 copy-start
  309.2 0.0 slice-start
  309.2 0.0 slice-start.1
  309.2 12.3 %copy.112 = bf16[8,2048,384]{2,1,0:T(8,128)(2,1)} copy(bf16[8,2048,384]{2,1,0:T(8,128)(2,1)} %get-tuple-element.21) | data formatting | bytes 25165824
  321.5 0.0 copy-done
  321.5 0.0 slice-start.2
  321.5 6.4 %copy.113 = bf16[8,2048,384]{2,1,0:T(8,128)(2,1)} copy(bf16[8,2048,384]{2,1,0:T(8,128)(2,1)S(1)} %copy-done) | data formatting | bytes 25165824
  327.9 0.0 slice-done
  327.9 1.1 slice-done.1
  329.0 1.3 slice-done.2
  330.3 4.8 %copy.114 = bf16[8,384,2048]{2,1,0:T(8,128)(2,1)} copy(bf16[8,384,2048]{2,1,0:T(8,128)(2,1)S(1)} %bitcast.83) | data formatting | bytes 25165824
  (6 shorter events, 0.1 us)
Async XLA Ops:
  8.0 15.8 %copy-start.3 = (bf16[32,1024]{1,0:T(8,128)(2,1)S(1)}, bf16[32,1024]{1,0:T(8,128)(2,1)}, u32[]{:S(2)}) copy-start(bf16[32,1024]{1,0:T(8,128)(2,1)} %param.8) | copy-start | bytes 196612
  18.4 52.4 %all-to-all-start.2 = ((bf16[32,16,2048]{2,1,0:T(8,128)(2,1)}), bf16[32,16,2048]{2,1,0:T(8,128)(2,1)S(1)}, u32[]{:S(2)}, u32[]{:S(2)}) async-start(bf16[32,16,2048]{2,1,0:T(8,128)(2,1)} %bitcast.85), calls=%async_computation.2 | async-start | bytes 4194304 | tf_op jit(solution)/shard_map/all_to_all | solution.py:41
  70.8 52.2 %all-to-all-start.1 = ((bf16[32,16,2048]{2,1,0:T(8,128)(2,1)}), bf16[32,16,2048]{2,1,0:T(8,128)(2,1)}, u32[]{:S(2)}, u32[]{:S(2)}) async-start(bf16[32,16,2048]{2,1,0:T(8,128)(2,1)} %bitcast.84), calls=%async_computation.1 | async-start | bytes 4194304 | tf_op jit(solution)/shard_map/all_to_all | solution.py:42
  123.0 19.1 %copy-start.4 = (bf16[32,8]{0,1:T(8,128)(2,1)S(1)}, bf16[32,8]{0,1:T(8,128)(2,1)}, u32[]{:S(2)}) copy-start(bf16[32,8]{0,1:T(8,128)(2,1)} %param.10) | copy-start | bytes 1540
  138.9 8.8 %all-to-all-start.4 = ((bf16[4,8,16]{2,1,0:T(8,128)(2,1)}), bf16[4,8,16]{2,1,0:T(8,128)(2,1)S(1)}, u32[]{:S(2)}, u32[]{:S(2)}) async-start(bf16[4,8,16]{2,1,0:T(8,128)(2,1)} %copy.78), calls=%async_computation.5 | async-start | bytes 16384 | tf_op jit(solution)/shard_map/all_to_all | solution.py:84
  142.1 64.7 %reduce-scatter.2.cloned.1.call-start = ((), (), s32[]{:S(2)}) async-start(), calls=%async_computation.6 | async-start | bytes 3145728 | tf_op jit(solution)/shard_map/reduce_scatter | solution.py:71
  157.8 8.8 %copy-start.1 = (bf16[4,8,16,384]{3,2,0,1:T(8,128)(2,1)}, bf16[4,8,16,384]{3,2,0,1:T(8,128)(2,1)S(1)}, u32[]{:S(2)}) copy-start(bf16[4,8,16,384]{3,2,0,1:T(8,128)(2,1)S(1)} %get-tuple-element.16) | copy-start | bytes 1179652
  176.6 132.6 %all-reduce.3.cloned.1.call-start = ((), (), s32[]{:S(2)}) async-start(), calls=%async_computation.7 | async-start | bytes 75497472 | tf_op jit(solution)/shard_map/psum | solution.py:104
  186.8 6.6 %copy-start.2 = (bf16[4,8,16,384]{3,2,0,1:T(8,128)(2,1)S(1)}, bf16[4,8,16,384]{3,2,0,1:T(8,128)(2,1)}, u32[]{:S(2)}) copy-start(bf16[4,8,16,384]{3,2,0,1:T(8,128)(2,1)} %copy-done.1) | copy-start | bytes 1179652
  209.5 30.0 %all-to-all-start.3 = ((bf16[32,16,1024]{2,1,0:T(8,128)(2,1)}), bf16[32,16,1024]{2,1,0:T(8,128)(2,1)S(1)}, u32[]{:S(2)}, u32[]{:S(2)}) async-start(bf16[32,16,1024]{2,1,0:T(8,128)(2,1)} %bitcast.16), calls=%async_computation.4 | async-start | bytes 2097152 | tf_op jit(solution)/shard_map/all_to_all | solution.py:77
  309.2 12.3 %copy-start = (bf16[8,2048,384]{2,1,0:T(8,128)(2,1)S(1)}, bf16[8,2048,384]{2,1,0:T(8,128)(2,1)}, u32[]{:S(2)}) copy-start(bf16[8,2048,384]{2,1,0:T(8,128)(2,1)} %get-tuple-element.22) | copy-start | bytes 37748740
  309.2 18.7 %slice-start = ((s8[12582912]{0:T(1024)(128)(4,1)}), s8[4194304]{0:T(1024)(128)(4,1)S(1)}, s32[]{:S(2)}) async-start(s8[12582912]{0:T(1024)(128)(4,1)} %bitcast.82), calls=%async_computation.8 | async-start | bytes 8388608
  309.2 19.8 %slice-start.1 = ((s8[12582912]{0:T(1024)(128)(4,1)}), s8[4194304]{0:T(1024)(128)(4,1)S(1)}, s32[]{:S(2)}) async-start(s8[12582912]{0:T(1024)(128)(4,1)} %bitcast.82), calls=%async_computation.9 | async-start | bytes 8388608
  321.5 8.8 %slice-start.2 = ((s8[12582912]{0:T(1024)(128)(4,1)}), s8[4194304]{0:T(1024)(128)(4,1)S(1)}, s32[]{:S(2)}) async-start(s8[12582912]{0:T(1024)(128)(4,1)} %bitcast.82), calls=%async_computation.10 | async-start | bytes 8388608
Sparse Core Ops, SparseCore 0:
  176.7 30.0 reduce-scatter.1
Sparse Core Ops, SparseCore 1:
  200.1 109.0 all-reduce.2
where the time goes:
time: 343 us
  waiting for transfers between devices  179 us (52%)
  matrix products  71.7 us (21%)
  local copies, waits for them, and re-layouts  31.3 us (9%)
  blocking collectives  24 us (7%)
  starting transfers between devices  17.7 us (5%)
  between operations  15.6 us (5%)
    psum x1, waiting for transfers between devices, body(): lax.psum(gate_total.astype(jnp.bfloat16), 'dp').astype(jnp.float32)  68.5 us
    all_to_all x1, waiting for transfers between devices, body(): lax.all_to_all(send_rows, 'expert', split_axis=0, concat_axis=0, tiled=True)  40.1 us
    all_to_all x1, waiting for transfers between devices, body(): lax.all_to_all(send_grads, 'expert', split_axis=0, concat_axis=0, tiled=T...  33.7 us
    unnamed x21, local copies, waits for them, and re-layouts  27.4 us
    all_to_all x1, waiting for transfers between devices, body(): lax.all_to_all(own_part.reshape(experts, CAP, quarter).astype(jnp.bfloat1...  24.8 us
    dot_general x1, matrix products, body(): jnp.einsum('slcd,lfd->slcf', grads_in, w_down, preferred_element_type=jnp...  10.2 us
    dot_general x1, matrix products, body(): jnp.einsum('slcf,slcd->lfd', weighted, grads_in, preferred_element_type=j...  10.2 us
    dot_general x1, matrix products, body(): jnp.einsum('slcf,ldf->slcd', up_grad, w_up, preferred_element_type=jnp.fl...  9.95 us
  transfers between devices with their start and end apart: 6, of which 6 were waited for; matrix products, arithmetic and copies ran while one was open for 13% of the time, Pallas kernels for 0%

commit v1 on v0

--- a/solution.py
+++ b/solution.py
@@ -1,14 +1,211 @@
+import functools
+
 import jax
 import jax.numpy as jnp
 from jax import lax
+from jax.experimental import pallas as pl
+from jax.experimental.pallas import tpu as pltpu
 from jax.sharding import PartitionSpec as P
 
-D = 2048
-TOP = 8
+VMEM_BYTES = 56 * 1024 * 1024
 CAP = 16
-
-
-def body(activations, out_grad, expert_ids, gate_probs, w_gate, w_up, w_down):
+META = 128
+NT = (((1,), (1,)), ((), ()))
+
+
+def forward_kernel(places, parts, top, own, scalars, *refs):
+    shards = refs[: len(places)]
+    wg_ref, wu_ref, wd_ref = refs[len(places) : len(places) + 3]
+    outs = refs[len(places) + 3 :]
+    own_ref, other_ref, grads_ref, weighted_ref, xt_ref, og_ref, x_ref, meta_ref, acc_ref, inner_ref = outs
+    step = pl.program_id(0)
+    tensor, dp = scalars[1], scalars[2]
+    n_tensor, n_dp = parts
+    wide = x_ref.shape[1] // n_tensor
+    tokens = x_ref.shape[0]
+    share = tokens // n_dp
+
+    @pl.when(step == 0)
+    def _():
+        for shard, (row, side, half) in zip(shards, places):
+            rows = shard.shape[0]
+            at = pl.ds(pl.multiple_of(lax.rem(dp + half, n_dp) * share + row, rows), rows)
+            columns = pl.ds(pl.multiple_of(lax.rem(tensor + side, n_tensor) * wide, wide), wide)
+            x_ref[at, columns] = shard[:, :wide]
+            og_ref[at, columns] = shard[:, wide : 2 * wide]
+            if side == 0:
+                meta_ref[at, :] = shard[:, 2 * wide :].astype(jnp.float32)
+        xt_ref[...] = x_ref[...].T
+        inner_ref[...] = jnp.zeros_like(inner_ref)
+
+    rows, grads = x_ref[...], og_ref[...]
+    gate_pre = jnp.dot(rows, wg_ref[0], preferred_element_type=jnp.float32)
+    up_pre = jnp.dot(rows, wu_ref[0], preferred_element_type=jnp.float32)
+    hidden_grad = lax.dot_general(grads, wd_ref[0], NT, preferred_element_type=jnp.float32)
+    expert = scalars[3] + step
+    meta = meta_ref[...]
+    hit = meta[:, :top] == expert.astype(jnp.float32)
+    prob = jnp.sum(jnp.where(hit, meta[:, top : 2 * top], 0.0), axis=1, keepdims=True)
+    sigma = jax.nn.sigmoid(gate_pre)
+    activated = gate_pre * sigma
+    hidden = activated * up_pre
+    inner = jnp.sum(hidden * hidden_grad, axis=1, keepdims=True)
+    lane = lax.broadcasted_iota(jnp.int32, inner_ref.shape, 1)
+    inner_ref[...] = jnp.where(lane == expert, inner, inner_ref[...])
+    scaled = prob * hidden_grad
+    gate_grad = (scaled * up_pre * sigma * (1.0 + gate_pre * (1.0 - sigma))).astype(jnp.bfloat16)
+    up_grad = (scaled * activated).astype(jnp.bfloat16)
+    grads_ref[0, 0] = gate_grad
+    grads_ref[0, 1] = up_grad
+    weighted_ref[0] = (prob * hidden).T.astype(jnp.bfloat16)
+    row_part = lax.dot_general(gate_grad, wg_ref[0], NT, preferred_element_type=jnp.float32)
+    row_part = row_part + lax.dot_general(up_grad, wu_ref[0], NT, preferred_element_type=jnp.float32)
+
+    @pl.when(step == 0)
+    def _():
+        acc_ref[...] = row_part
+
+    @pl.when(step > 0)
+    def _():
+        acc_ref[...] += row_part
+
+    @pl.when(step == own - 1)
+    def _():
+        for half, target in ((0, own_ref), (1, other_ref)):
+            if target is None:
+                continue
+            at = pl.ds(pl.multiple_of(lax.rem(dp + half, n_dp) * share, share), share)
+            for side in range(n_tensor):
+                columns = pl.ds(pl.multiple_of(lax.rem(tensor + side, n_tensor) * wide, wide), wide)
+                target[side, :, :wide] = acc_ref[at, columns].astype(target.dtype)
+                target[side, :, wide:] = inner_ref[at, :].astype(jnp.bfloat16).astype(target.dtype)
+
+
+def forward(shards, places, scalars, w_gate, w_up, w_down, own, tokens, parts, top):
+    n_tensor, n_dp = parts
+    _, d, ff = w_gate.shape
+    share, wide = tokens // n_dp, d // n_tensor
+    whole = lambda shape: pl.BlockSpec(shape, lambda i, s: (0,) * len(shape))
+    weight = lambda shape: pl.BlockSpec((1, *shape), lambda i, s: (s[0] + i, 0, 0))
+    sums = (n_tensor, share, wide + META)
+    return pl.pallas_call(
+        functools.partial(forward_kernel, places, parts, top, own),
+        grid_spec=pltpu.PrefetchScalarGridSpec(
+            num_scalar_prefetch=1,
+            grid=(own,),
+            in_specs=[whole(s.shape) for s in shards] + [weight((d, ff)), weight((d, ff)), weight((ff, d))],
+            out_specs=[
+                whole(sums),
+                whole(sums),
+                pl.BlockSpec((1, 2, tokens, ff), lambda i, s: (i, 0, 0, 0)),
+                pl.BlockSpec((1, ff, tokens), lambda i, s: (i, 0, 0)),
+                whole((d, tokens)),
+                whole((tokens, d)),
+            ],
+            scratch_shapes=[
+                pltpu.VMEM((tokens, d), jnp.bfloat16),
+                pltpu.VMEM((tokens, META), jnp.float32),
+                pltpu.VMEM((tokens, d), jnp.float32),
+                pltpu.VMEM((tokens, META), jnp.float32),
+            ],
+        ),
+        out_shape=[
+            jax.ShapeDtypeStruct(sums, jnp.float32),
+            jax.ShapeDtypeStruct(sums, jnp.bfloat16),
+            jax.ShapeDtypeStruct((own, 2, tokens, ff), jnp.bfloat16),
+            jax.ShapeDtypeStruct((own, ff, tokens), jnp.bfloat16),
+            jax.ShapeDtypeStruct((d, tokens), jnp.bfloat16),
+            jax.ShapeDtypeStruct((tokens, d), jnp.bfloat16),
+        ],
+        compiler_params=pltpu.CompilerParams(vmem_limit_bytes=VMEM_BYTES),
+        cost_estimate=pl.CostEstimate(
+            flops=10 * own * tokens * d * ff, bytes_accessed=6 * own * d * ff + 8 * tokens * d, transcendentals=0
+        ),
+        name="routed_forward",
+    )(scalars, *shards, w_gate, w_up, w_down)
+
+
+def weight_kernel(scalars, xt_ref, og_ref, grads_ref, weighted_ref, *refs):
+    gate_ref, up_ref, down_ref = refs[-3:]
+    xt = xt_ref[...]
+    gate_ref[0] = jnp.dot(xt, grads_ref[0, 0], preferred_element_type=jnp.float32).astype(jnp.bfloat16)
+    up_ref[0] = jnp.dot(xt, grads_ref[0, 1], preferred_element_type=jnp.float32).astype(jnp.bfloat16)
+    down_ref[0] = jnp.dot(weighted_ref[0], og_ref[...], preferred_element_type=jnp.float32).astype(jnp.bfloat16)
+
+
+def weight_grads(scalars, xt, og, grads, weighted, local_count, into=None):
+    own, _, tokens, ff = grads.shape
+    d = xt.shape[0]
+    whole = lambda shape: pl.BlockSpec(shape, lambda i, s: (0,) * len(shape))
+    out = lambda shape: pl.BlockSpec((1, *shape), lambda i, s: (s[0] + i, 0, 0))
+    kept = [] if into is None else list(into)
+    shapes = [(d, ff), (d, ff), (ff, d)]
+    return pl.pallas_call(
+        weight_kernel,
+        grid_spec=pltpu.PrefetchScalarGridSpec(
+            num_scalar_prefetch=1,
+            grid=(own,),
+            in_specs=[
+                whole((d, tokens)),
+                whole((tokens, d)),
+                pl.BlockSpec((1, 2, tokens, ff), lambda i, s: (i, 0, 0, 0)),
+                pl.BlockSpec((1, ff, tokens), lambda i, s: (i, 0, 0)),
+            ]
+            + [pl.BlockSpec(memory_space=pl.ANY)] * len(kept),
+            out_specs=[out(s) for s in shapes],
+        ),
+        out_shape=[jax.ShapeDtypeStruct((local_count, *s), jnp.bfloat16) for s in shapes],
+        input_output_aliases={5 + i: i for i in range(len(kept))},
+        compiler_params=pltpu.CompilerParams(vmem_limit_bytes=VMEM_BYTES),
+        cost_estimate=pl.CostEstimate(
+            flops=6 * own * tokens * d * ff, bytes_accessed=6 * own * d * ff + 8 * tokens * d, transcendentals=0
+        ),
+        name="weight_grads",
+    )(scalars, xt, og, grads, weighted, *kept)
+
+
+def split_kernel(own_ref, got_ref, *out_refs):
+    rows, sides = out_refs[0].shape[0], own_ref.shape[0]
+    blocks = own_ref.shape[1] // rows
+    for side in range(sides):
+        for block in range(blocks):
+            at = pl.ds(block * rows, rows)
+            total = own_ref[side, at, :] + got_ref[side, at, :].astype(jnp.float32)
+            out_refs[side * blocks + block][...] = total.astype(out_refs[0].dtype)
+
+
+def finish_kernel(top, ids_ref, *refs):
+    parts, (grad_ref, probs_ref) = refs[:-2], refs[-2:]
+    total = parts[0][...].astype(jnp.float32)
+    for part in parts[1:]:
+        total = total + part[...].astype(jnp.float32)
+    wide = grad_ref.shape[1]
+    grad_ref[...] = total[:, :wide].astype(jnp.bfloat16)
+    inner = total[:, wide:]
+    ids = ids_ref[...]
+    lane = lax.broadcasted_iota(jnp.int32, inner.shape, 1)
+    for k in range(top):
+        picked = jnp.where(lane == ids[:, k : k + 1], inner, 0.0)
+        probs_ref[:, k : k + 1] = jnp.sum(picked, axis=1, keepdims=True)
+
+
+def shift(x, axis, by):
+    count = lax.axis_size(axis)
+    return lax.ppermute(x, axis, [(i, (i + by) % count) for i in range(count)])
+
+
+def shift_both(x, by, side):
+    n_expert, n_tensor = lax.axis_size("expert"), lax.axis_size("tensor")
+    pairs = [
+        (e * n_tensor + t, (e + by) % n_expert * n_tensor + (t + side) % n_tensor)
+        for e in range(n_expert)
+        for t in range(n_tensor)
+    ]
+    return lax.ppermute(x, ("expert", "tensor"), pairs)
+
+
+def general_body(activations, out_grad, expert_ids, gate_probs, w_gate, w_up, w_down):
+    d = activations.shape[1] * lax.axis_size("tensor")
     expert_count = lax.axis_size("expert")
     local_count = w_gate.shape[0]
     experts = expert_count * local_count
@@ -17,7 +214,7 @@
     onehot = (flat_ids[:, None] == jnp.arange(experts, dtype=jnp.int32)[None, :]).astype(jnp.int32)
     before = jnp.cumsum(onehot, axis=0) - onehot
     slot_index = jnp.sum(before * onehot, axis=1)
-    position = (flat_ids * CAP + slot_index).reshape(token_rows, TOP)
+    position = (flat_ids * CAP + slot_index).reshape(token_rows, expert_ids.shape[1])
     lane_index = jnp.arange(experts * CAP, dtype=jnp.int32)
     matches = position[None, :, :] == lane_index[:, None, None]
     placing = jnp.sum(matches.astype(jnp.int32), axis=2).astype(jnp.bfloat16)
@@ -30,20 +227,20 @@
     send_rows = (
         jnp.dot(placing, full_rows, preferred_element_type=jnp.float32)
         .astype(jnp.bfloat16)
-        .reshape(experts, CAP, D)
+        .reshape(experts, CAP, d)
     )
     send_grads = (
         jnp.dot(placing, full_grads, preferred_element_type=jnp.float32)
         .astype(jnp.bfloat16)
-        .reshape(experts, CAP, D)
+        .reshape(experts, CAP, d)
     )
     got_rows, got_grads, got_probs = (
         lax.all_to_all(send_rows, "expert", split_axis=0, concat_axis=0, tiled=True),
         lax.all_to_all(send_grads, "expert", split_axis=0, concat_axis=0, tiled=True),
         lax.all_to_all(send_probs, "expert", split_axis=0, concat_axis=0, tiled=True),
     )
-    rows_in = got_rows.reshape(expert_count, local_count, CAP, D)
-    grads_in = got_grads.reshape(expert_count, local_count, CAP, D)
+    rows_in = got_rows.reshape(expert_count, local_count, CAP, d)
+    grads_in = got_grads.reshape(expert_count, local_count, CAP, d)
     row_probs = got_probs.reshape(expert_count, local_count, CAP, 1).astype(jnp.float32)
     gate_pre = jnp.einsum("slcd,ldf->slcf", rows_in, w_gate, preferred_element_type=jnp.float32)
     up_pre = jnp.einsum("slcd,ldf->slcf", rows_in, w_up, preferred_element_type=jnp.float32)
@@ -114,6 +311,53 @@
     )
 
 
+def body(activations, out_grad, expert_ids, gate_probs, w_gate, w_up, w_down):
+    n_expert, n_tensor, n_dp = (lax.axis_size(a) for a in ("expert", "tensor", "dp"))
+    local_count, d, ff = w_gate.shape
+    rows, top = expert_ids.shape
+    tokens = rows * n_expert * n_dp
+    wide = d // n_tensor
+    own = local_count // n_dp
+    e, t, p = (lax.axis_index(a) for a in ("expert", "tensor", "dp"))
+    first = p * own
+    meta = jnp.concatenate([expert_ids.astype(jnp.bfloat16), gate_probs], axis=1)
+    meta = jnp.pad(meta, ((0, 0), (0, META - 2 * top)))
+    packed = jnp.concatenate([activations, out_grad, meta], axis=1)
+    shards, places = [], []
+    along = [packed] + [shift(packed, "expert", k) for k in range(1, n_expert)]
+    for side in range(n_tensor):
+        for k in range(n_expert):
+            shards.append(along[k] if side == 0 else shift(along[k], "tensor", 1))
+            places.append((k * rows, side, 0))
+    for i in range(n_expert * n_tensor):
+        shards.append(shift(shards[i], "dp", 1))
+        places.append((*places[i][:2], 1))
+    scalars = jnp.stack([first, t, p, e * local_count + first]).astype(jnp.int32)
+    own_sum, other_sum, grads, weighted, xt, og = forward(
+        shards, tuple(places), scalars, w_gate, w_up, w_down, own, tokens, (n_tensor, n_dp), top
+    )
+    from_other = shift(other_sum, "dp", 1)
+    piece = jax.ShapeDtypeStruct((rows, wide + META), jnp.bfloat16)
+    pieces = pl.pallas_call(
+        split_kernel, out_shape=[piece] * (n_expert * n_tensor), name="add_and_split"
+    )(own_sum, from_other)
+    got_grads, got_weighted = shift(grads, "dp", 1), shift(weighted, "dp", 1)
+    received = []
+    for side in range(n_tensor):
+        for k in range(n_expert):
+            part = pieces[side * n_expert + k]
+            received.append(part if side == k == 0 else shift_both(part, -k, side))
+    outputs = weight_grads(scalars, xt, og, grads, weighted, local_count)
+    other = jnp.stack([own - first, t]).astype(jnp.int32)
+    outputs = weight_grads(other, xt, og, got_grads, got_weighted, local_count, outputs)
+    grad, probs = pl.pallas_call(
+        functools.partial(finish_kernel, top),
+        out_shape=[jax.ShapeDtypeStruct((rows, wide), jnp.bfloat16), jax.ShapeDtypeStruct((rows, top), jnp.float32)],
+        name="sum_of_parts",
+    )(expert_ids, *received)
+    return (grad, probs, *outputs)
+
+
 def solution(mesh):
     in_specs = (
         P(("groups", "expert", "dp"), "tensor"),
@@ -131,4 +375,6 @@
         P(("groups", "expert"), None, "tensor"),
         P(("groups", "expert"), "tensor", None),
     )
-    return jax.shard_map(body, mesh=mesh, in_specs=in_specs, out_specs=out_specs, check_vma=False)
+    sizes = dict(mesh.shape)
+    compact = sizes["expert"] <= 4 and sizes["tensor"] == 2 and sizes["dp"] == 2
+    return jax.shard_map(body if compact else general_body, mesh=mesh, in_specs=in_specs, out_specs=out_specs, check_vma=False)

time: 343 us -> 102 us (0.30)
  waiting for transfers between devices: 179 us -> 26.6 us
  matrix products: 71.7 us -> 0 us
  Pallas kernels: 0 us -> 47.4 us
  local copies, waits for them, and re-layouts: 31.3 us -> 6.54 us
  blocking collectives: 24 us -> 0 us
  between operations: 15.6 us -> 0.94 us
    all_to_all x4 -> x0, waiting for transfers between devices: 104 us -> none  [the longest x1 40.1 us: body(): lax.all_to_all(send_rows, 'expert', split_axis=0, concat_axis=0, tiled=True)]
    dot_general x11 -> x0, matrix products: 71.7 us -> none  [the longest x1 10.2 us: body(): jnp.einsum('slcd,lfd->slcf', grads_in, w_down, preferred_element_type=jnp...]
    psum x1 -> x0, waiting for transfers between devices: 68.5 us -> none  [body(): lax.psum(gate_total.astype(jnp.bfloat16), 'dp').astype(jnp.float32)]
    pallas_call x0 -> x5, Pallas kernels: none -> 47.4 us  [the longest x2 22.8 us: weight_grads(): pl.pallas_call(weight_kernel, grid_spec=pltpu.PrefetchScalarGridSpec(num_...]
    ppermute x0 -> x25, waiting for transfers between devices: none -> 26.6 us  [the longest x18 20.4 us: shift(): return lax.ppermute(x, axis, [(i, (i + by) % count) for i in range(count)])]
    unnamed x21 -> x57, local copies, waits for them, and re-layouts: 27.4 us -> 6.45 us
    ppermute x0 -> x25, starting transfers between devices: none -> 17.7 us  [the longest x18 11.9 us: shift(): return lax.ppermute(x, axis, [(i, (i + by) % count) for i in range(count)])]
    all_to_all x4 -> x0, starting transfers between devices: 17.6 us -> none  [the longest x1 5.36 us: body(): lax.all_to_all(send_rows, 'expert', split_axis=0, concat_axis=0, tiled=True)]
  transfers between devices with their start and end apart: 6 -> 25, of which waited for: 6 -> 8; matrix products, arithmetic and copies ran while one was open for 13% -> 3% of each run, Pallas kernels for 0% -> 16%
where the time goes in v1:
time: 102 us
  Pallas kernels  47.4 us (46%)
  waiting for transfers between devices  26.6 us (26%)
  starting transfers between devices  17.7 us (17%)
  local copies, waits for them, and re-layouts  6.54 us (6%)
  other arithmetic  2.98 us (3%)
    pallas_call x2, Pallas kernels, weight_grads(): pl.pallas_call(weight_kernel, grid_spec=pltpu.PrefetchScalarGridSpec(num_...  22.8 us
    ppermute x18, waiting for transfers between devices, shift(): return lax.ppermute(x, axis, [(i, (i + by) % count) for i in range(count)])  20.4 us
    pallas_call x1, Pallas kernels, forward(): pl.pallas_call(functools.partial(forward_kernel, places, parts, top, own)...  20.1 us
    ppermute x18, starting transfers between devices, shift(): return lax.ppermute(x, axis, [(i, (i + by) % count) for i in range(count)])  11.9 us
    unnamed x57, local copies, waits for them, and re-layouts  6.45 us
    ppermute x7, waiting for transfers between devices, shift_both(): return lax.ppermute(x, ('expert', 'tensor'), pairs)  6.2 us
    ppermute x7, starting transfers between devices, shift_both(): return lax.ppermute(x, ('expert', 'tensor'), pairs)  5.77 us
    pallas_call x1, Pallas kernels, body(): pl.pallas_call(functools.partial(finish_kernel, top), out_shape=[jax.Shap...  2.27 us
  transfers between devices with their start and end apart: 25, of which 8 were waited for; matrix products, arithmetic and copies ran while one was open for 3% of the time, Pallas kernels for 16%

profile of v1, /device:TPU:0, one launch (start us, length us, event | category | flops | bytes accessed | tf_op | source)
XLA Modules:
  0.0 102.1 jit_solution(9405294669567857844)
XLA Ops:
  0.6 0.7 convert_element_type.5
  1.3 0.1 copy.19
  1.4 0.8 copy.20
  2.2 0.1 fusion.2
  2.3 0.9 pad_maximum_fusion.refs_0_
  3.2 0.0 copy-start.3
  3.2 3.0 %collective-permute-start.3 = (bf16[32,2176]{1,0:T(8,128)(2,1)S(1)}, bf16[32,2176]{1,0:T(8,128)(2,1)S(1)}, u32[]{:S(2)}, u32[]{:S(2)}) collective-permute-start(bf16[32,2176]{1,0:T(8,128)(2,1)S(1)} %pad_maximum_fusion.refs_0_), channel_id=1, source_target_pairs={{0,2},{2,0},{1,3},{3,1},{4,6},{6,4},{5,7},{7,5},{8,10},{10,8},{9,1... | collective-permute-start | bytes 417800 | tf_op jit(solution)/shard_map/ppermute | solution.py:194
  6.2 3.6 %collective-permute-start.2 = (bf16[32,2176]{1,0:T(8,128)(2,1)S(1)}, bf16[32,2176]{1,0:T(8,128)(2,1)S(1)}, u32[]{:S(2)}, u32[]{:S(2)}) collective-permute-start(bf16[32,2176]{1,0:T(8,128)(2,1)S(1)} %pad_maximum_fusion.refs_0_), channel_id=1, source_target_pairs={{0,12},{4,0},{8,4},{12,8},{1,13},{5,1},{9,5},{13,9},{2,14},{6,2},{... | collective-permute-start | bytes 417800 | tf_op jit(solution)/shard_map/ppermute | solution.py:194
  9.8 0.0 collective-permute-start.7
  9.8 1.0 collective-permute-start
  10.8 0.0 collective-permute-done.3.refs_4_
  10.8 0.0 collective-permute-start.11
  10.8 3.1 %collective-permute-done.2.refs_3_ = bf16[32,2176]{1,0:T(8,128)(2,1)S(1)} collective-permute-done((bf16[32,2176]{1,0:T(8,128)(2,1)S(1)}, bf16[32,2176]{1,0:T(8,128)(2,1)S(1)}, u32[]{:S(2)}, u32[]{:S(2)}) %collective-permute-start.2) | collective-permute-done | bytes 139296 | tf_op jit(solution)/shard_map/ppermute | solution.py:194
  13.9 0.6 collective-permute-start.6
  14.5 7.2 %collective-permute-done.1.refs_2_ = bf16[32,2176]{1,0:T(8,128)(2,1)S(1)} collective-permute-done((bf16[32,2176]{1,0:T(8,128)(2,1)S(1)}, bf16[32,2176]{1,0:T(8,128)(2,1)S(1)}, u32[]{:S(2)}, u32[]{:S(2)}) %collective-permute-start.1) | collective-permute-done | bytes 139296 | tf_op jit(solution)/shard_map/ppermute | solution.py:194
  21.8 0.5 collective-permute-start.5
  22.3 1.5 %collective-permute-start.4 = (bf16[32,2176]{1,0:T(8,128)(2,1)S(1)}, bf16[32,2176]{1,0:T(8,128)(2,1)S(1)}, u32[]{:S(2)}, u32[]{:S(2)}) collective-permute-start(bf16[32,2176]{1,0:T(8,128)(2,1)S(1)} %collective-permute-done.refs_1_), channel_id=1, source_target_pairs={{0,2},{2,0},{1,3},{3,1},{4,6},{6,4},{5,7},{7,5},{8,10},{10,8},{9,1... | collective-permute-start | bytes 417800 | tf_op jit(solution)/shard_map/ppermute | solution.py:194
  23.8 0.0 collective-permute-done.11.refs_12_
  23.8 0.0 collective-permute-start.9
  23.8 0.5 collective-permute-start.8
  24.3 0.1 collective-permute-start.14
  24.4 3.9 %collective-permute-done.5.refs_6_ = bf16[32,2176]{1,0:T(8,128)(2,1)S(1)} collective-permute-done((bf16[32,2176]{1,0:T(8,128)(2,1)S(1)}, bf16[32,2176]{1,0:T(8,128)(2,1)S(1)}, u32[]{:S(2)}, u32[]{:S(2)}) %collective-permute-start.5) | collective-permute-done | bytes 139296 | tf_op jit(solution)/shard_map/ppermute | solution.py:194
  28.3 1.9 %collective-permute-done.4.refs_5_ = bf16[32,2176]{1,0:T(8,128)(2,1)S(1)} collective-permute-done((bf16[32,2176]{1,0:T(8,128)(2,1)S(1)}, bf16[32,2176]{1,0:T(8,128)(2,1)S(1)}, u32[]{:S(2)}, u32[]{:S(2)}) %collective-permute-start.4) | collective-permute-done | bytes 139296 | tf_op jit(solution)/shard_map/ppermute | solution.py:194
  30.2 0.0 collective-permute-start.12
  30.2 0.7 pad_add_fusion.scalars
  30.9 0.0 collective-permute-done.9.refs_10_
  30.9 0.0 collective-permute-done.8.refs_9_
  30.9 0.0 collective-permute-done.14.refs_15_
  30.9 0.0 collective-permute-done.13.refs_14_
  30.9 0.6 collective-permute-done.12.refs_13_
  31.7 0.6 copy-done.18
  32.4 20.1 %routed_forward.1 = (f32[2,128,1152]{2,1,0:T(8,128)}, bf16[2,128,1152]{2,1,0:T(8,128)(2,1)}, bf16[4,2,256,384]{3,2,1,0:T(8,128)(2,1)}, bf16[4,384,256]{2,1,0:T(8...) custom-call(s32[4]{0:T(128)} %pad_add_fusion.scalars, bf16[32,2176]{1,0:T(8,128)(2,1)} %copy-done.3, ...), custom_call_target="tpu_custom_call" | custom-call | flops 8053063680 | bytes 23068672 | tf_op jit(solution)/shard_map/routed_forward/pallas_call | solution.py:91
  52.4 0.6 collective-permute-start.23
  53.0 0.1 collective-permute-start.15
  53.1 0.4 collective-permute-start.24
  53.5 3.6 %collective-permute-done.15.got_ref = bf16[2,128,1152]{2,1,0:T(8,128)(2,1)S(1)} collective-permute-done((bf16[2,128,1152]{2,1,0:T(8,128)(2,1)}, bf16[2,128,1152]{2,1,0:T(8,128)(2,1)S(1)}, u32[]{:S(2)}, u32[]{:S(2)}) %collective-permute-start.15) | collective-permute-done | bytes 589856 | tf_op jit(solution)/shard_map/ppermute | solution.py:194
  57.1 0.8 copy-done.2
  57.9 2.3 %add_and_split.1 = (bf16[32,1152]{1,0:T(8,128)(2,1)}, bf16[32,1152]{1,0:T(8,128)(2,1)}, bf16[32,1152]{1,0:T(8,128)(2,1)}, bf16[32,1152]{1,0:T(8,128)(2,1)}, bf16...) custom-call(f32[2,128,1152]{2,1,0:T(8,128)} %get-tuple-element.27.own_ref,, ...), custom_call_target="tpu_custom_call" | custom-call | tf_op jit(solution)/shard_map/add_and_split/pallas_call | solution.py:341
  60.2 1.1 %collective-permute-start.16 = (bf16[32,1152]{1,0:T(8,128)(2,1)}, bf16[32,1152]{1,0:T(8,128)(2,1)S(1)}, u32[]{:S(2)}, u32[]{:S(2)}) collective-permute-start(bf16[32,1152]{1,0:T(8,128)(2,1)} %get-tuple-element.30), channel_id=1, source_target_pairs={{0,12},{2,14},{4,0},{6,2},{8,4},{10,6},{12,8},{14,10},{1,13},{3,15... | collective-permute-start | bytes 221192 | tf_op jit(solution)/shard_map/ppermute | solution.py:204
  61.3 0.7 copy.21.ids_ref
  61.9 0.0 collective-permute-start.17
  61.9 1.1 %collective-permute-start.18 = (bf16[32,1152]{1,0:T(8,128)(2,1)}, bf16[32,1152]{1,0:T(8,128)(2,1)S(1)}, u32[]{:S(2)}, u32[]{:S(2)}) collective-permute-start(bf16[32,1152]{1,0:T(8,128)(2,1)} %get-tuple-element.32), channel_id=1, source_target_pairs={{0,4},{2,6},{4,8},{6,10},{8,12},{10,14},{12,0},{14,2},{1,5},{3,7},... | collective-permute-start | bytes 221192 | tf_op jit(solution)/shard_map/ppermute | solution.py:204
  63.1 1.9 %collective-permute-done.16.refs_1_ = bf16[32,1152]{1,0:T(8,128)(2,1)S(1)} collective-permute-done((bf16[32,1152]{1,0:T(8,128)(2,1)}, bf16[32,1152]{1,0:T(8,128)(2,1)S(1)}, u32[]{:S(2)}, u32[]{:S(2)}) %collective-permute-start.16) | collective-permute-done | bytes 73760 | tf_op jit(solution)/shard_map/ppermute | solution.py:204
  64.9 0.5 collective-permute-start.19
  65.5 0.7 pad_add_fusion.1.scalars
  66.1 4.3 %collective-permute-done.17.refs_2_ = bf16[32,1152]{1,0:T(8,128)(2,1)S(1)} collective-permute-done((bf16[32,1152]{1,0:T(8,128)(2,1)}, bf16[32,1152]{1,0:T(8,128)(2,1)S(1)}, u32[]{:S(2)}, u32[]{:S(2)}) %collective-permute-start.17) | collective-permute-done | bytes 73760 | tf_op jit(solution)/shard_map/ppermute | solution.py:204
  70.5 0.6 collective-permute-start.20
  71.0 0.0 collective-permute-done.18.refs_3_
  71.0 0.6 collective-permute-start.21
  71.6 1.8 %collective-permute-start.22 = (bf16[32,1152]{1,0:T(8,128)(2,1)}, bf16[32,1152]{1,0:T(8,128)(2,1)S(1)}, u32[]{:S(2)}, u32[]{:S(2)}) collective-permute-start(bf16[32,1152]{1,0:T(8,128)(2,1)} %get-tuple-element.36), channel_id=1, source_target_pairs={{0,6},{2,4},{4,10},{6,8},{8,14},{10,12},{12,2},{14,0},{1,7},{3,5},... | collective-permute-start | bytes 221192 | tf_op jit(solution)/shard_map/ppermute | solution.py:204
  73.5 11.4 %weight_grads.2 = (bf16[8,2048,384]{2,1,0:T(8,128)(2,1)}, bf16[8,2048,384]{2,1,0:T(8,128)(2,1)}, bf16[8,384,2048]{2,1,0:T(8,128)(2,1)}) custom-call(s32[4]{0:T(128)} %pad_add_fusion.scalars, bf16[2048,256]{1,0:T(8,128)(2,1)} %get-tuple-element.39.xt_ref, bf16[256,2048]{1,0:T(8,128)(2,1)} %get-tuple-element.40.og_ref, ...), custom_call_target="tpu_custom_call" | custom-call | flops 4831838208 | bytes 23068672 | tf_op jit(solution)/shard_map/weight_grads/pallas_call | solution.py:143
  84.9 0.0 collective-permute-done.20.refs_5_
  84.9 0.0 collective-permute-done.21.refs_6_
  84.9 0.0 collective-permute-done.22.refs_7_
  84.9 0.5 copy-done.23
  85.5 0.0 copy-done.24
  85.5 0.1 copy-done.25
  85.6 2.3 %sum_of_parts.1 = (bf16[32,1024]{1,0:T(8,128)(2,1)}, f32[32,8]{1,0:T(8,128)}) custom-call(s32[32,8]{1,0:T(8,128)} %copy.21.ids_ref, bf16[32,1152]{1,0:T(8,128)(2,1)} %get-tuple-element.29.refs_0_, bf16[32,1152]{1,0:T(8,128)(2,1)} %copy-done.19, bf16[32,1152]{1,0:T(8,128)(2,1)} %copy-done.20, bf16[32,1152]{1,0:T(8,128)(2,1)} %copy-done.21, ...), custom_call_target="tpu_custom_call" | custom-call | tf_op jit(solution)/shard_map/sum_of_parts/pallas_call | solution.py:353
  87.8 1.4 %copy.22 = f32[32,8]{0,1:T(8,128)} copy(f32[32,8]{1,0:T(8,128)} %get-tuple-element.55) | data formatting | bytes 2048
  89.2 0.0 collective-permute-done.24.weighted_ref
  89.2 0.0 collective-permute-done.23.grads_ref
  89.2 0.9 copy-done.1
  90.1 0.6 copy-done
  90.7 11.4 %weight_grads.3 = (bf16[8,2048,384]{2,1,0:T(8,128)(2,1)}, bf16[8,2048,384]{2,1,0:T(8,128)(2,1)}, bf16[8,384,2048]{2,1,0:T(8,128)(2,1)}) custom-call(s32[2]{0:T(128)} %pad_add_fusion.1.scalars, bf16[2048,256]{1,0:T(8,128)(2,1)} %get-tuple-element.39.xt_ref, ...), custom_call_target="tpu_custom_call", output_to_operand_aliasing={{0}: (5, {}), {1}: (6, {}), {2}: (7, {})} | custom-call | flops 4831838208 | bytes 23068672 | tf_op jit(solution)/shard_map/weight_grads/pallas_call | solution.py:143
  (54 shorter events, 0.1 us)
Async XLA Ops:
  3.2 28.4 %copy-start.3 = (bf16[32,2176]{1,0:T(8,128)(2,1)}, bf16[32,2176]{1,0:T(8,128)(2,1)S(1)}, u32[]{:S(2)}) copy-start(bf16[32,2176]{1,0:T(8,128)(2,1)S(1)} %pad_maximum_fusion.refs_0_) | copy-start | bytes 417796
  3.2 7.6 %collective-permute-start.3 = (bf16[32,2176]{1,0:T(8,128)(2,1)S(1)}, bf16[32,2176]{1,0:T(8,128)(2,1)S(1)}, u32[]{:S(2)}, u32[]{:S(2)}) collective-permute-start(bf16[32,2176]{1,0:T(8,128)(2,1)S(1)} %pad_maximum_fusion.refs_0_), channel_id=1, source_target_pairs={{0,2},{2,0},{1,3},{3,1},{4,6},{6,4},{5,7},{7,5},{8,10},{10,8},{9,1... | collective-permute-start | bytes 417800 | tf_op jit(solution)/shard_map/ppermute | solution.py:194
  6.2 7.8 %collective-permute-start.2 = (bf16[32,2176]{1,0:T(8,128)(2,1)S(1)}, bf16[32,2176]{1,0:T(8,128)(2,1)S(1)}, u32[]{:S(2)}, u32[]{:S(2)}) collective-permute-start(bf16[32,2176]{1,0:T(8,128)(2,1)S(1)} %pad_maximum_fusion.refs_0_), channel_id=1, source_target_pairs={{0,12},{4,0},{8,4},{12,8},{1,13},{5,1},{9,5},{13,9},{2,14},{6,2},{... | collective-permute-start | bytes 417800 | tf_op jit(solution)/shard_map/ppermute | solution.py:194
  9.8 4.2 %collective-permute-start.7 = (bf16[32,2176]{1,0:T(8,128)(2,1)S(1)}, bf16[32,2176]{1,0:T(8,128)(2,1)S(1)}, u32[]{:S(2)}, u32[]{:S(2)}) collective-permute-start(bf16[32,2176]{1,0:T(8,128)(2,1)S(1)} %pad_maximum_fusion.refs_0_), channel_id=1, source_target_pairs={{0,1},{1,0},{2,3},{3,2},{4,5},{5,4},{6,7},{7,6},{8,9},{9,8},{10,11... | collective-permute-start | bytes 417800 | tf_op jit(solution)/shard_map/ppermute | solution.py:194
  9.8 12.0 %collective-permute-start.1 = (bf16[32,2176]{1,0:T(8,128)(2,1)S(1)}, bf16[32,2176]{1,0:T(8,128)(2,1)S(1)}, u32[]{:S(2)}, u32[]{:S(2)}) collective-permute-start(bf16[32,2176]{1,0:T(8,128)(2,1)S(1)} %pad_maximum_fusion.refs_0_), channel_id=1, source_target_pairs={{0,8},{4,12},{8,0},{12,4},{1,9},{5,13},{9,1},{13,5},{2,10},{6,14},... | collective-permute-start | bytes 417800 | tf_op jit(solution)/shard_map/ppermute | solution.py:194
  9.8 12.5 %collective-permute-start = (bf16[32,2176]{1,0:T(8,128)(2,1)S(1)}, bf16[32,2176]{1,0:T(8,128)(2,1)S(1)}, u32[]{:S(2)}, u32[]{:S(2)}) collective-permute-start(bf16[32,2176]{1,0:T(8,128)(2,1)S(1)} %pad_maximum_fusion.refs_0_), channel_id=1, source_target_pairs={{0,4},{4,8},{8,12},{12,0},{1,5},{5,9},{9,13},{13,1},{2,6},{6,10},{... | collective-permute-start | bytes 417800 | tf_op jit(solution)/shard_map/ppermute | solution.py:194
  10.8 20.8 %copy-start.4 = (bf16[32,2176]{1,0:T(8,128)(2,1)}, bf16[32,2176]{1,0:T(8,128)(2,1)S(1)}, u32[]{:S(2)}) copy-start(bf16[32,2176]{1,0:T(8,128)(2,1)S(1)} %collective-permute-done.3.refs_4_) | copy-start | bytes 417796
  10.8 13.0 %collective-permute-start.11 = (bf16[32,2176]{1,0:T(8,128)(2,1)S(1)}, bf16[32,2176]{1,0:T(8,128)(2,1)S(1)}, u32[]{:S(2)}, u32[]{:S(2)}) collective-permute-start(bf16[32,2176]{1,0:T(8,128)(2,1)S(1)} %collective-permute-done.3.refs_4_), channel_id=1, source_target_pairs={{0,1},{1,0},{2,3},{3,2},{4,5},{5,4},{6,7},{7,6},{8,9},{9,8},{10,11... | collective-permute-start | bytes 417800 | tf_op jit(solution)/shard_map/ppermute | solution.py:194
  13.9 17.7 %copy-start.5 = (bf16[32,2176]{1,0:T(8,128)(2,1)}, bf16[32,2176]{1,0:T(8,128)(2,1)S(1)}, u32[]{:S(2)}) copy-start(bf16[32,2176]{1,0:T(8,128)(2,1)S(1)} %collective-permute-done.2.refs_3_) | copy-start | bytes 417796
  13.9 9.9 %collective-permute-start.10 = (bf16[32,2176]{1,0:T(8,128)(2,1)S(1)}, bf16[32,2176]{1,0:T(8,128)(2,1)S(1)}, u32[]{:S(2)}, u32[]{:S(2)}) collective-permute-start(bf16[32,2176]{1,0:T(8,128)(2,1)S(1)} %collective-permute-done.2.refs_3_), channel_id=1, source_target_pairs={{0,1},{1,0},{2,3},{3,2},{4,5},{5,4},{6,7},{7,6},{8,9},{9,8},{10,11... | collective-permute-start | bytes 417800 | tf_op jit(solution)/shard_map/ppermute | solution.py:194
  13.9 17.7 %copy-start.6 = (bf16[32,2176]{1,0:T(8,128)(2,1)}, bf16[32,2176]{1,0:T(8,128)(2,1)S(1)}, u32[]{:S(2)}) copy-start(bf16[32,2176]{1,0:T(8,128)(2,1)S(1)} %collective-permute-done.7.refs_8_) | copy-start | bytes 417796
  13.9 10.4 %collective-permute-start.6 = (bf16[32,2176]{1,0:T(8,128)(2,1)S(1)}, bf16[32,2176]{1,0:T(8,128)(2,1)S(1)}, u32[]{:S(2)}, u32[]{:S(2)}) collective-permute-start(bf16[32,2176]{1,0:T(8,128)(2,1)S(1)} %collective-permute-done.2.refs_3_), channel_id=1, source_target_pairs={{0,2},{2,0},{1,3},{3,1},{4,6},{6,4},{5,7},{7,5},{8,10},{10,8},{9,1... | collective-permute-start | bytes 417800 | tf_op jit(solution)/shard_map/ppermute | solution.py:194
  21.8 9.8 %copy-start.7 = (bf16[32,2176]{1,0:T(8,128)(2,1)}, bf16[32,2176]{1,0:T(8,128)(2,1)S(1)}, u32[]{:S(2)}) copy-start(bf16[32,2176]{1,0:T(8,128)(2,1)S(1)} %collective-permute-done.1.refs_2_) | copy-start | bytes 417796
  21.8 6.6 %collective-permute-start.5 = (bf16[32,2176]{1,0:T(8,128)(2,1)S(1)}, bf16[32,2176]{1,0:T(8,128)(2,1)S(1)}, u32[]{:S(2)}, u32[]{:S(2)}) collective-permute-start(bf16[32,2176]{1,0:T(8,128)(2,1)S(1)} %collective-permute-done.1.refs_2_), channel_id=1, source_target_pairs={{0,2},{2,0},{1,3},{3,1},{4,6},{6,4},{5,7},{7,5},{8,10},{10,8},{9,1... | collective-permute-start | bytes 417800 | tf_op jit(solution)/shard_map/ppermute | solution.py:194
  22.3 9.3 %copy-start.8 = (bf16[32,2176]{1,0:T(8,128)(2,1)}, bf16[32,2176]{1,0:T(8,128)(2,1)S(1)}, u32[]{:S(2)}) copy-start(bf16[32,2176]{1,0:T(8,128)(2,1)S(1)} %collective-permute-done.refs_1_) | copy-start | bytes 417796
  22.3 7.9 %collective-permute-start.4 = (bf16[32,2176]{1,0:T(8,128)(2,1)S(1)}, bf16[32,2176]{1,0:T(8,128)(2,1)S(1)}, u32[]{:S(2)}, u32[]{:S(2)}) collective-permute-start(bf16[32,2176]{1,0:T(8,128)(2,1)S(1)} %collective-permute-done.refs_1_), channel_id=1, source_target_pairs={{0,2},{2,0},{1,3},{3,1},{4,6},{6,4},{5,7},{7,5},{8,10},{10,8},{9,1... | collective-permute-start | bytes 417800 | tf_op jit(solution)/shard_map/ppermute | solution.py:194
  23.8 7.8 %copy-start.9 = (bf16[32,2176]{1,0:T(8,128)(2,1)}, bf16[32,2176]{1,0:T(8,128)(2,1)S(1)}, u32[]{:S(2)}) copy-start(bf16[32,2176]{1,0:T(8,128)(2,1)S(1)} %collective-permute-done.11.refs_12_) | copy-start | bytes 417796
  23.8 7.1 %collective-permute-start.9 = (bf16[32,2176]{1,0:T(8,128)(2,1)S(1)}, bf16[32,2176]{1,0:T(8,128)(2,1)S(1)}, u32[]{:S(2)}, u32[]{:S(2)}) collective-permute-start(bf16[32,2176]{1,0:T(8,128)(2,1)S(1)} %collective-permute-done.1.refs_2_), channel_id=1, source_target_pairs={{0,1},{1,0},{2,3},{3,2},{4,5},{5,4},{6,7},{7,6},{8,9},{9,8},{10,11... | collective-permute-start | bytes 417800 | tf_op jit(solution)/shard_map/ppermute | solution.py:194
  23.8 7.8 %copy-start.10 = (bf16[32,2176]{1,0:T(8,128)(2,1)}, bf16[32,2176]{1,0:T(8,128)(2,1)S(1)}, u32[]{:S(2)}) copy-start(bf16[32,2176]{1,0:T(8,128)(2,1)S(1)} %collective-permute-done.10.refs_11_) | copy-start | bytes 417796
  23.8 7.1 %collective-permute-start.8 = (bf16[32,2176]{1,0:T(8,128)(2,1)S(1)}, bf16[32,2176]{1,0:T(8,128)(2,1)S(1)}, u32[]{:S(2)}, u32[]{:S(2)}) collective-permute-start(bf16[32,2176]{1,0:T(8,128)(2,1)S(1)} %collective-permute-done.refs_1_), channel_id=1, source_target_pairs={{0,1},{1,0},{2,3},{3,2},{4,5},{5,4},{6,7},{7,6},{8,9},{9,8},{10,11... | collective-permute-start | bytes 417800 | tf_op jit(solution)/shard_map/ppermute | solution.py:194
  24.3 7.3 %copy-start.11 = (bf16[32,2176]{1,0:T(8,128)(2,1)}, bf16[32,2176]{1,0:T(8,128)(2,1)S(1)}, u32[]{:S(2)}) copy-start(bf16[32,2176]{1,0:T(8,128)(2,1)S(1)} %collective-permute-done.6.refs_7_) | copy-start | bytes 417796
  24.3 6.6 %collective-permute-start.14 = (bf16[32,2176]{1,0:T(8,128)(2,1)S(1)}, bf16[32,2176]{1,0:T(8,128)(2,1)S(1)}, u32[]{:S(2)}, u32[]{:S(2)}) collective-permute-start(bf16[32,2176]{1,0:T(8,128)(2,1)S(1)} %collective-permute-done.6.refs_7_), channel_id=1, source_target_pairs={{0,1},{1,0},{2,3},{3,2},{4,5},{5,4},{6,7},{7,6},{8,9},{9,8},{10,11... | collective-permute-start | bytes 417800 | tf_op jit(solution)/shard_map/ppermute | solution.py:194
  28.3 3.3 %copy-start.12 = (bf16[32,2176]{1,0:T(8,128)(2,1)}, bf16[32,2176]{1,0:T(8,128)(2,1)S(1)}, u32[]{:S(2)}) copy-start(bf16[32,2176]{1,0:T(8,128)(2,1)S(1)} %collective-permute-done.5.refs_6_) | copy-start | bytes 417796
  28.3 2.6 %collective-permute-start.13 = (bf16[32,2176]{1,0:T(8,128)(2,1)S(1)}, bf16[32,2176]{1,0:T(8,128)(2,1)S(1)}, u32[]{:S(2)}, u32[]{:S(2)}) collective-permute-start(bf16[32,2176]{1,0:T(8,128)(2,1)S(1)} %collective-permute-done.5.refs_6_), channel_id=1, source_target_pairs={{0,1},{1,0},{2,3},{3,2},{4,5},{5,4},{6,7},{7,6},{8,9},{9,8},{10,11... | collective-permute-start | bytes 417800 | tf_op jit(solution)/shard_map/ppermute | solution.py:194
  30.2 1.4 %copy-start.13 = (bf16[32,2176]{1,0:T(8,128)(2,1)}, bf16[32,2176]{1,0:T(8,128)(2,1)S(1)}, u32[]{:S(2)}) copy-start(bf16[32,2176]{1,0:T(8,128)(2,1)S(1)} %collective-permute-done.4.refs_5_) | copy-start | bytes 417796
  30.2 1.4 %collective-permute-start.12 = (bf16[32,2176]{1,0:T(8,128)(2,1)S(1)}, bf16[32,2176]{1,0:T(8,128)(2,1)S(1)}, u32[]{:S(2)}, u32[]{:S(2)}) collective-permute-start(bf16[32,2176]{1,0:T(8,128)(2,1)S(1)} %collective-permute-done.4.refs_5_), channel_id=1, source_target_pairs={{0,1},{1,0},{2,3},{3,2},{4,5},{5,4},{6,7},{7,6},{8,9},{9,8},{10,11... | collective-permute-start | bytes 417800 | tf_op jit(solution)/shard_map/ppermute | solution.py:194
  30.9 30.4 %copy-start.26 = (s32[32,8]{0,1:T(8,128)S(1)}, s32[32,8]{0,1:T(8,128)}, u32[]{:S(2)}) copy-start(s32[32,8]{0,1:T(8,128)} %param.9) | copy-start | bytes 3076
  30.9 0.8 copy-start.14
  30.9 0.8 copy-start.15
  30.9 0.8 copy-start.16
  30.9 0.8 copy-start.17
  31.7 0.7 copy-start.18
  52.4 36.8 %collective-permute-start.23 = (bf16[4,2,256,384]{3,2,1,0:T(8,128)(2,1)}, bf16[4,2,256,384]{3,2,1,0:T(8,128)(2,1)S(1)}, u32[]{:S(2)}, u32[]{:S(2)}) collective-permute-start(bf16[4,2,256,384]{3,2,1,0:T(8,128)(2,1)} %get-tuple-element.41.grads_ref), channel_id=1, source_target_pairs={{0,1},{1,0},{2,3},{3,2},{4,5},{5,4},{6,7},{7,6},{8,9},{9,8},{10,11... | collective-permute-start | bytes 4718600 | tf_op jit(solution)/shard_map/ppermute | solution.py:194
  53.0 4.1 %collective-permute-start.15 = (bf16[2,128,1152]{2,1,0:T(8,128)(2,1)}, bf16[2,128,1152]{2,1,0:T(8,128)(2,1)S(1)}, u32[]{:S(2)}, u32[]{:S(2)}) collective-permute-start(bf16[2,128,1152]{2,1,0:T(8,128)(2,1)} %get-tuple-element.28), channel_id=1, source_target_pairs={{0,1},{1,0},{2,3},{3,2},{4,5},{5,4},{6,7},{7,6},{8,9},{9,8},{10,11... | collective-permute-start | bytes 1769480 | tf_op jit(solution)/shard_map/ppermute | solution.py:194
  53.1 36.2 %collective-permute-start.24 = (bf16[4,384,256]{2,1,0:T(8,128)(2,1)}, bf16[4,384,256]{2,1,0:T(8,128)(2,1)S(1)}, u32[]{:S(2)}, u32[]{:S(2)}) collective-permute-start(bf16[4,384,256]{2,1,0:T(8,128)(2,1)} %get-tuple-element.42.weighted_ref), channel_id=1, source_target_pairs={{0,1},{1,0},{2,3},{3,2},{4,5},{5,4},{6,7},{7,6},{8,9},{9,8},{10,11... | collective-permute-start | bytes 2359304 | tf_op jit(solution)/shard_map/ppermute | solution.py:194
  57.1 0.8 copy-start.2
  60.2 4.8 %collective-permute-start.16 = (bf16[32,1152]{1,0:T(8,128)(2,1)}, bf16[32,1152]{1,0:T(8,128)(2,1)S(1)}, u32[]{:S(2)}, u32[]{:S(2)}) collective-permute-start(bf16[32,1152]{1,0:T(8,128)(2,1)} %get-tuple-element.30), channel_id=1, source_target_pairs={{0,12},{2,14},{4,0},{6,2},{8,4},{10,6},{12,8},{14,10},{1,13},{3,15... | collective-permute-start | bytes 221192 | tf_op jit(solution)/shard_map/ppermute | solution.py:204
  61.9 8.5 %collective-permute-start.17 = (bf16[32,1152]{1,0:T(8,128)(2,1)}, bf16[32,1152]{1,0:T(8,128)(2,1)S(1)}, u32[]{:S(2)}, u32[]{:S(2)}) collective-permute-start(bf16[32,1152]{1,0:T(8,128)(2,1)} %get-tuple-element.31), channel_id=1, source_target_pairs={{0,8},{2,10},{4,12},{6,14},{8,0},{10,2},{12,4},{14,6},{1,9},{3,11}... | collective-permute-start | bytes 221192 | tf_op jit(solution)/shard_map/ppermute | solution.py:204
  61.9 9.1 %collective-permute-start.18 = (bf16[32,1152]{1,0:T(8,128)(2,1)}, bf16[32,1152]{1,0:T(8,128)(2,1)S(1)}, u32[]{:S(2)}, u32[]{:S(2)}) collective-permute-start(bf16[32,1152]{1,0:T(8,128)(2,1)} %get-tuple-element.32), channel_id=1, source_target_pairs={{0,4},{2,6},{4,8},{6,10},{8,12},{10,14},{12,0},{14,2},{1,5},{3,7},... | collective-permute-start | bytes 221192 | tf_op jit(solution)/shard_map/ppermute | solution.py:204
  64.9 20.0 %copy-start.19 = (bf16[32,1152]{1,0:T(8,128)(2,1)}, bf16[32,1152]{1,0:T(8,128)(2,1)S(1)}, u32[]{:S(2)}) copy-start(bf16[32,1152]{1,0:T(8,128)(2,1)S(1)} %collective-permute-done.16.refs_1_) | copy-start | bytes 221188
  64.9 6.7 %collective-permute-start.19 = (bf16[32,1152]{1,0:T(8,128)(2,1)}, bf16[32,1152]{1,0:T(8,128)(2,1)S(1)}, u32[]{:S(2)}, u32[]{:S(2)}) collective-permute-start(bf16[32,1152]{1,0:T(8,128)(2,1)} %get-tuple-element.33), channel_id=1, source_target_pairs={{0,2},{2,0},{4,6},{6,4},{8,10},{10,8},{12,14},{14,12},{1,3},{3,1},... | collective-permute-start | bytes 221192 | tf_op jit(solution)/shard_map/ppermute | solution.py:204
  70.5 14.5 %copy-start.20 = (bf16[32,1152]{1,0:T(8,128)(2,1)}, bf16[32,1152]{1,0:T(8,128)(2,1)S(1)}, u32[]{:S(2)}) copy-start(bf16[32,1152]{1,0:T(8,128)(2,1)S(1)} %collective-permute-done.17.refs_2_) | copy-start | bytes 221188
  70.5 14.4 %collective-permute-start.20 = (bf16[32,1152]{1,0:T(8,128)(2,1)}, bf16[32,1152]{1,0:T(8,128)(2,1)S(1)}, u32[]{:S(2)}, u32[]{:S(2)}) collective-permute-start(bf16[32,1152]{1,0:T(8,128)(2,1)} %get-tuple-element.34), channel_id=1, source_target_pairs={{0,14},{2,12},{4,2},{6,0},{8,6},{10,4},{12,10},{14,8},{1,15},{3,13... | collective-permute-start | bytes 221192 | tf_op jit(solution)/shard_map/ppermute | solution.py:204
  71.0 13.9 %copy-start.21 = (bf16[32,1152]{1,0:T(8,128)(2,1)}, bf16[32,1152]{1,0:T(8,128)(2,1)S(1)}, u32[]{:S(2)}) copy-start(bf16[32,1152]{1,0:T(8,128)(2,1)S(1)} %collective-permute-done.18.refs_3_) | copy-start | bytes 221188
  71.0 13.8 %collective-permute-start.21 = (bf16[32,1152]{1,0:T(8,128)(2,1)}, bf16[32,1152]{1,0:T(8,128)(2,1)S(1)}, u32[]{:S(2)}, u32[]{:S(2)}) collective-permute-start(bf16[32,1152]{1,0:T(8,128)(2,1)} %get-tuple-element.35), channel_id=1, source_target_pairs={{0,10},{2,8},{4,14},{6,12},{8,2},{10,0},{12,6},{14,4},{1,11},{3,9}... | collective-permute-start | bytes 221192 | tf_op jit(solution)/shard_map/ppermute | solution.py:204
  71.6 13.3 %copy-start.22 = (bf16[32,1152]{1,0:T(8,128)(2,1)}, bf16[32,1152]{1,0:T(8,128)(2,1)S(1)}, u32[]{:S(2)}) copy-start(bf16[32,1152]{1,0:T(8,128)(2,1)S(1)} %collective-permute-done.19.refs_4_) | copy-start | bytes 221188
  71.6 13.3 %collective-permute-start.22 = (bf16[32,1152]{1,0:T(8,128)(2,1)}, bf16[32,1152]{1,0:T(8,128)(2,1)S(1)}, u32[]{:S(2)}, u32[]{:S(2)}) collective-permute-start(bf16[32,1152]{1,0:T(8,128)(2,1)} %get-tuple-element.36), channel_id=1, source_target_pairs={{0,6},{2,4},{4,10},{6,8},{8,14},{10,12},{12,2},{14,0},{1,7},{3,5},... | collective-permute-start | bytes 221192 | tf_op jit(solution)/shard_map/ppermute | solution.py:204
  84.9 0.6 copy-start.23
  84.9 0.6 copy-start.24
  84.9 0.7 copy-start.25
  89.2 0.9 copy-start.1
  89.2 1.5 %copy-start = (bf16[4,2,256,384]{3,2,1,0:T(8,128)(2,1)}, bf16[4,2,256,384]{3,2,1,0:T(8,128)(2,1)S(1)}, u32[]{:S(2)}) copy-start(bf16[4,2,256,384]{3,2,1,0:T(8,128)(2,1)S(1)} %collective-permute-done.23.grads_ref) | copy-start | bytes 4718596

commit v2 on v0

--- a/solution.py
+++ b/solution.py
@@ -1,14 +1,203 @@
+import functools
+
 import jax
 import jax.numpy as jnp
 from jax import lax
+from jax.experimental import pallas as pl
+from jax.experimental.pallas import tpu as pltpu
 from jax.sharding import PartitionSpec as P
 
-D = 2048
-TOP = 8
 CAP = 16
-
-
-def body(activations, out_grad, expert_ids, gate_probs, w_gate, w_up, w_down):
+META = 128
+MIB = 1024 * 1024
+NT = (((1,), (1,)), ((), ()))
+TN = (((0,), (0,)), ((), ()))
+ANY = pl.BlockSpec(memory_space=pl.ANY)
+SMEM = pl.BlockSpec(memory_space=pltpu.SMEM)
+VMEM = pl.BlockSpec(memory_space=pltpu.VMEM)
+
+
+def near(*arrays):
+    return [pltpu.with_memory_space_constraint(x, pltpu.VMEM) for x in arrays]
+
+
+def far(*arrays):
+    return [pltpu.with_memory_space_constraint(x, pltpu.HBM) for x in arrays]
+
+
+def load_kernel(own, first_ref, wg_ref, wu_ref, wd_ref, in_ref, out_ref, sem):
+    ff = wd_ref.shape[1]
+    copies = []
+    for i in range(own):
+        for j, source in enumerate((wg_ref, wu_ref)):
+            target = in_ref.at[:, pl.ds((2 * i + j) * ff, ff)]
+            copies.append(pltpu.make_async_copy(source.at[first_ref[0] + i], target, sem))
+        copies.append(pltpu.make_async_copy(wd_ref.at[first_ref[0] + i], out_ref.at[pl.ds(i * ff, ff), :], sem))
+    for copy in copies:
+        copy.start()
+    for copy in copies:
+        copy.wait()
+
+
+def load_weights(scalars, w_gate, w_up, w_down, own):
+    _, d, ff = w_gate.shape
+    return pl.pallas_call(
+        functools.partial(load_kernel, own),
+        in_specs=[SMEM, ANY, ANY, ANY],
+        out_specs=[VMEM, VMEM],
+        out_shape=[pltpu.VMEM((d, own * 2 * ff), jnp.bfloat16), pltpu.VMEM((own * ff, d), jnp.bfloat16)],
+        scratch_shapes=[pltpu.SemaphoreType.DMA],
+        compiler_params=pltpu.CompilerParams(vmem_limit_bytes=4 * MIB),
+        cost_estimate=pl.CostEstimate(flops=0, bytes_accessed=6 * own * d * ff, transcendentals=0),
+        name="load_weights",
+    )(scalars, *far(w_gate, w_up, w_down))
+
+
+def forward_kernel(places, n_tensor, top, own, scalars, *refs):
+    count = len(places)
+    shards, (w_in, w_out) = refs[:count], refs[count : count + 2]
+    x_ref, og_ref, grads_ref, kept_ref, sent_ref, meta_ref = refs[count + 2 :]
+    tensor = scalars[1]
+    tokens, d = x_ref.shape
+    wide, share = d // n_tensor, tokens // 2
+    ff = w_out.shape[0] // own
+    for shard, (row, side) in zip(shards, places):
+        rows = shard.shape[0]
+        columns = pl.ds(pl.multiple_of(lax.rem(tensor + side, n_tensor) * wide, wide), wide)
+        x_ref[pl.ds(row, rows), columns] = shard[:, :wide]
+        og_ref[pl.ds(row, rows), columns] = shard[:, wide : 2 * wide]
+        if side == 0:
+            meta_ref[pl.ds(row, rows), :] = shard[:, 2 * wide :].astype(jnp.float32)
+    pre = jnp.dot(x_ref[...], w_in[...], preferred_element_type=jnp.float32)
+    hidden_grads = lax.dot_general(og_ref[...], w_out[...], NT, preferred_element_type=jnp.float32)
+    meta = meta_ref[...]
+    lane = lax.broadcasted_iota(jnp.int32, meta.shape, 1)
+    inners = jnp.zeros(meta.shape, jnp.float32)
+    both = []
+    for i in range(own):
+        gate_pre, up_pre = pre[:, 2 * i * ff : (2 * i + 1) * ff], pre[:, (2 * i + 1) * ff : (2 * i + 2) * ff]
+        hidden_grad = hidden_grads[:, i * ff : (i + 1) * ff]
+        expert = scalars[2] + i
+        hit = meta[:, :top] == expert.astype(jnp.float32)
+        prob = jnp.sum(jnp.where(hit, meta[:, top : 2 * top], 0.0), axis=1, keepdims=True)
+        sigma = jax.nn.sigmoid(gate_pre)
+        activated = gate_pre * sigma
+        hidden = activated * up_pre
+        inner = jnp.sum(hidden * hidden_grad, axis=1, keepdims=True)
+        inners = jnp.where(lane == expert, inner, inners)
+        scaled = prob * hidden_grad
+        gate_grad = (scaled * up_pre * sigma * (1.0 + gate_pre * (1.0 - sigma))).astype(jnp.bfloat16)
+        up_grad = (scaled * activated).astype(jnp.bfloat16)
+        grads_ref[i, :, :ff] = gate_grad
+        grads_ref[i, :, ff : 2 * ff] = up_grad
+        grads_ref[i, :, 2 * ff :] = (prob * hidden).astype(jnp.bfloat16)
+        both += [gate_grad, up_grad]
+    both = jnp.concatenate(both, axis=1)
+    for side in range(n_tensor):
+        at = pl.ds(pl.multiple_of(lax.rem(tensor + side, n_tensor) * wide, wide), wide)
+        total = lax.dot_general(both, w_in[at, :], NT, preferred_element_type=jnp.float32)
+        kept_ref[side, :, :wide] = total[:share]
+        kept_ref[side, :, wide:] = inners[:share]
+        sent_ref[side, :, :wide] = total[share:].astype(jnp.bfloat16)
+        sent_ref[side, :, wide:] = inners[share:].astype(jnp.bfloat16)
+
+
+def forward(shards, places, scalars, w_in, w_out, own, tokens, n_tensor, top):
+    d, ff = w_out.shape[1], w_out.shape[0] // own
+    sums = (n_tensor, tokens // 2, d // n_tensor + META)
+    return pl.pallas_call(
+        functools.partial(forward_kernel, places, n_tensor, top, own),
+        in_specs=[SMEM] + [VMEM] * (len(shards) + 2),
+        out_specs=[VMEM] * 5,
+        out_shape=[
+            pltpu.VMEM((tokens, d), jnp.bfloat16),
+            pltpu.VMEM((tokens, d), jnp.bfloat16),
+            pltpu.VMEM((own, tokens, 3 * ff), jnp.bfloat16),
+            pltpu.VMEM(sums, jnp.float32),
+            pltpu.VMEM(sums, jnp.bfloat16),
+        ],
+        scratch_shapes=[pltpu.VMEM((tokens, META), jnp.float32)],
+        compiler_params=pltpu.CompilerParams(vmem_limit_bytes=20 * MIB),
+        cost_estimate=pl.CostEstimate(
+            flops=10 * own * tokens * d * ff, bytes_accessed=16 * tokens * d, transcendentals=0
+        ),
+        name="routed_forward",
+    )(scalars, *near(*shards), w_in, w_out)
+
+
+def weight_kernel(swap, scalars, x_ref, og_ref, grads_ref, *refs):
+    gate_ref, up_ref, down_ref = refs[-3:]
+    ff = gate_ref.shape[2]
+    grads = grads_ref[0]
+    if swap:
+        half = grads.shape[0] // 2
+        grads = jnp.concatenate([grads[half:], grads[:half]], axis=0)
+    both = lax.dot_general(x_ref[...], grads[:, : 2 * ff], TN, preferred_element_type=jnp.float32)
+    gate_ref[0] = both[:, :ff].astype(jnp.bfloat16)
+    up_ref[0] = both[:, ff:].astype(jnp.bfloat16)
+    down = lax.dot_general(grads[:, 2 * ff :], og_ref[...], TN, preferred_element_type=jnp.float32)
+    down_ref[0] = down.astype(jnp.bfloat16)
+
+
+def weight_grads(scalars, x, og, grads, local_count, into=None):
+    own, tokens, ff = grads.shape[0], grads.shape[1], grads.shape[2] // 3
+    d = x.shape[1]
+    whole = pl.BlockSpec((tokens, d), lambda i, s: (0, 0))
+    out = lambda shape: pl.BlockSpec((1, *shape), lambda i, s: (s[0] + i, 0, 0))
+    kept = [] if into is None else list(into)
+    shapes = [(d, ff), (d, ff), (ff, d)]
+    return pl.pallas_call(
+        functools.partial(weight_kernel, into is not None),
+        grid_spec=pltpu.PrefetchScalarGridSpec(
+            num_scalar_prefetch=1,
+            grid=(own,),
+            in_specs=[whole, whole, pl.BlockSpec((1, tokens, 3 * ff), lambda i, s: (i, 0, 0))] + [ANY] * len(kept),
+            out_specs=[out(s) for s in shapes],
+        ),
+        out_shape=[jax.ShapeDtypeStruct((local_count, *s), jnp.bfloat16) for s in shapes],
+        input_output_aliases={4 + i: i for i in range(len(kept))},
+        compiler_params=pltpu.CompilerParams(vmem_limit_bytes=32 * MIB),
+        cost_estimate=pl.CostEstimate(
+            flops=6 * own * tokens * d * ff, bytes_accessed=6 * own * d * ff + 8 * tokens * d, transcendentals=0
+        ),
+        name="weight_grads",
+    )(scalars, x, og, grads, *kept)
+
+
+def dp_sum_kernel(kept_ref, got_ref, here_ref, there_ref):
+    here_ref[...] = kept_ref[0] + got_ref[0].astype(jnp.float32)
+    there_ref[...] = (kept_ref[1] + got_ref[1].astype(jnp.float32)).astype(jnp.bfloat16)
+
+
+def tensor_sum_kernel(here_ref, got_ref, own_ref, *out_refs):
+    rows = own_ref.shape[0]
+    for block, target in enumerate((own_ref, *out_refs)):
+        at = pl.ds(block * rows, rows)
+        target[...] = (here_ref[at, :] + got_ref[at, :].astype(jnp.float32)).astype(target.dtype)
+
+
+def finish_kernel(top, ids_ref, own_ref, *refs):
+    parts, (grad_ref, probs_ref) = refs[:-2], refs[-2:]
+    total = own_ref[...]
+    for part in parts:
+        total = total + part[...].astype(jnp.float32)
+    wide = grad_ref.shape[1]
+    grad_ref[...] = total[:, :wide].astype(jnp.bfloat16)
+    inner = total[:, wide:]
+    ids = ids_ref[...]
+    lane = lax.broadcasted_iota(jnp.int32, inner.shape, 1)
+    for k in range(top):
+        picked = jnp.where(lane == ids[:, k : k + 1], inner, 0.0)
+        probs_ref[:, k : k + 1] = jnp.sum(picked, axis=1, keepdims=True)
+
+
+def shift(x, axis, by):
+    count = lax.axis_size(axis)
+    return lax.ppermute(x, axis, [(i, (i + by) % count) for i in range(count)])
+
+
+def general_body(activations, out_grad, expert_ids, gate_probs, w_gate, w_up, w_down):
+    d = activations.shape[1] * lax.axis_size("tensor")
     expert_count = lax.axis_size("expert")
     local_count = w_gate.shape[0]
     experts = expert_count * local_count
@@ -17,7 +206,7 @@
     onehot = (flat_ids[:, None] == jnp.arange(experts, dtype=jnp.int32)[None, :]).astype(jnp.int32)
     before = jnp.cumsum(onehot, axis=0) - onehot
     slot_index = jnp.sum(before * onehot, axis=1)
-    position = (flat_ids * CAP + slot_index).reshape(token_rows, TOP)
+    position = (flat_ids * CAP + slot_index).reshape(token_rows, expert_ids.shape[1])
     lane_index = jnp.arange(experts * CAP, dtype=jnp.int32)
     matches = position[None, :, :] == lane_index[:, None, None]
     placing = jnp.sum(matches.astype(jnp.int32), axis=2).astype(jnp.bfloat16)
@@ -30,20 +219,20 @@
     send_rows = (
         jnp.dot(placing, full_rows, preferred_element_type=jnp.float32)
         .astype(jnp.bfloat16)
-        .reshape(experts, CAP, D)
+        .reshape(experts, CAP, d)
     )
     send_grads = (
         jnp.dot(placing, full_grads, preferred_element_type=jnp.float32)
         .astype(jnp.bfloat16)
-        .reshape(experts, CAP, D)
+        .reshape(experts, CAP, d)
     )
     got_rows, got_grads, got_probs = (
         lax.all_to_all(send_rows, "expert", split_axis=0, concat_axis=0, tiled=True),
         lax.all_to_all(send_grads, "expert", split_axis=0, concat_axis=0, tiled=True),
         lax.all_to_all(send_probs, "expert", split_axis=0, concat_axis=0, tiled=True),
     )
-    rows_in = got_rows.reshape(expert_count, local_count, CAP, D)
-    grads_in = got_grads.reshape(expert_count, local_count, CAP, D)
+    rows_in = got_rows.reshape(expert_count, local_count, CAP, d)
+    grads_in = got_grads.reshape(expert_count, local_count, CAP, d)
     row_probs = got_probs.reshape(expert_count, local_count, CAP, 1).astype(jnp.float32)
     gate_pre = jnp.einsum("slcd,ldf->slcf", rows_in, w_gate, preferred_element_type=jnp.float32)
     up_pre = jnp.einsum("slcd,ldf->slcf", rows_in, w_up, preferred_element_type=jnp.float32)
@@ -114,6 +303,67 @@
     )
 
 
+def body(activations, out_grad, expert_ids, gate_probs, w_gate, w_up, w_down):
+    n_expert, n_tensor, n_dp = (lax.axis_size(a) for a in ("expert", "tensor", "dp"))
+    local_count, d, ff = w_gate.shape
+    rows, top = expert_ids.shape
+    tokens = rows * n_expert * n_dp
+    wide = d // n_tensor
+    own = local_count // n_dp
+    e, t, p = (lax.axis_index(a) for a in ("expert", "tensor", "dp"))
+    first = p * own
+    scalars = jnp.stack([first, t, e * local_count + first, own - first]).astype(jnp.int32)
+    meta = jnp.concatenate([expert_ids.astype(jnp.bfloat16), gate_probs], axis=1)
+    meta = jnp.pad(meta, ((0, 0), (0, META - 2 * top)))
+    packed = jnp.concatenate([activations, out_grad, meta], axis=1)
+    w_in, w_out = load_weights(scalars, w_gate, w_up, w_down, own)
+    along = [packed] + [shift(packed, "expert", k) for k in range(1, n_expert)]
+    along[1], w_in, w_out = lax.optimization_barrier((along[1], w_in, w_out))
+    shards, places = [], []
+    for side in range(n_tensor):
+        for k in range(n_expert):
+            shards.append(along[k] if side == 0 else shift(along[k], "tensor", 1))
+            places.append((k * rows, side))
+    for i in range(n_expert * n_tensor):
+        shards.append(shift(shards[i], "dp", 1))
+        places.append((tokens // 2 + places[i][0], places[i][1]))
+    x, og, grads, kept, sent = forward(
+        shards, tuple(places), scalars, w_in, w_out, own, tokens, n_tensor, top
+    )
+    got = shift(sent, "dp", 1)
+    got_grads = shift(grads, "dp", 1)
+    half = (tokens // 2, wide + META)
+    here, there = pl.pallas_call(
+        dp_sum_kernel,
+        in_specs=[VMEM] * 2,
+        out_specs=[VMEM] * 2,
+        out_shape=[pltpu.VMEM(half, jnp.float32), pltpu.VMEM(half, jnp.bfloat16)],
+        name="sum_over_cores",
+    )(kept, *near(got))
+    crossed = shift(there, "tensor", 1)
+    outputs = weight_grads(scalars, x, og, grads, local_count)
+    crossed, outputs = lax.optimization_barrier((crossed, outputs))
+    piece = (rows, wide + META)
+    pieces = pl.pallas_call(
+        tensor_sum_kernel,
+        in_specs=[VMEM] * 2,
+        out_specs=[VMEM] * n_expert,
+        out_shape=[pltpu.VMEM(piece, jnp.float32)] + [pltpu.VMEM(piece, jnp.bfloat16)] * (n_expert - 1),
+        name="sum_over_tensor",
+    )(here, *near(crossed))
+    received = [shift(pieces[k], "expert", -k) for k in range(1, n_expert)]
+    outputs = weight_grads(scalars[3:], x, og, got_grads, local_count, outputs)
+    received, outputs = lax.optimization_barrier((received, outputs))
+    grad, probs = pl.pallas_call(
+        functools.partial(finish_kernel, top),
+        in_specs=[VMEM] * (n_expert + 1),
+        out_specs=[VMEM] * 2,
+        out_shape=[jax.ShapeDtypeStruct((rows, wide), jnp.bfloat16), jax.ShapeDtypeStruct((rows, top), jnp.float32)],
+        name="sum_over_experts",
+    )(expert_ids, pieces[0], *near(*received))
+    return (grad, probs, *outputs)
+
+
 def solution(mesh):
     in_specs = (
         P(("groups", "expert", "dp"), "tensor"),
@@ -131,4 +381,6 @@
         P(("groups", "expert"), None, "tensor"),
         P(("groups", "expert"), "tensor", None),
     )
-    return jax.shard_map(body, mesh=mesh, in_specs=in_specs, out_specs=out_specs, check_vma=False)
+    sizes = dict(mesh.shape)
+    compact = sizes["expert"] <= 4 and sizes["tensor"] == 2 and sizes["dp"] == 2
+    return jax.shard_map(body if compact else general_body, mesh=mesh, in_specs=in_specs, out_specs=out_specs, check_vma=False)

time: 343 us -> 83.2 us (0.24)
  waiting for transfers between devices: 179 us -> 14.2 us
  matrix products: 71.7 us -> 0 us
  Pallas kernels: 0 us -> 42 us
  blocking collectives: 24 us -> 0 us
  local copies, waits for them, and re-layouts: 31.3 us -> 7.38 us
  between operations: 15.6 us -> 0.76 us
    all_to_all x4 -> x0, waiting for transfers between devices: 104 us -> none  [the longest x1 40.1 us: body(): lax.all_to_all(send_rows, 'expert', split_axis=0, concat_axis=0, tiled=True)]
    dot_general x11 -> x0, matrix products: 71.7 us -> none  [the longest x1 10.2 us: body(): jnp.einsum('slcd,lfd->slcf', grads_in, w_down, preferred_element_type=jnp...]
    psum x1 -> x0, waiting for transfers between devices: 68.5 us -> none  [body(): lax.psum(gate_total.astype(jnp.bfloat16), 'dp').astype(jnp.float32)]
    pallas_call x0 -> x7, Pallas kernels: none -> 42 us  [the longest x2 19.6 us: weight_grads(): pl.pallas_call(functools.partial(weight_kernel, into is not None), grid_s...]
    unnamed x21 -> x17, local copies, waits for them, and re-layouts: 27.4 us -> 7.29 us
    all_to_all x4 -> x0, starting transfers between devices: 17.6 us -> none  [the longest x1 5.36 us: body(): lax.all_to_all(send_rows, 'expert', split_axis=0, concat_axis=0, tiled=True)]
    ppermute x0 -> x21, starting transfers between devices: none -> 16.6 us  [shift(): return lax.ppermute(x, axis, [(i, (i + by) % count) for i in range(count)])]
    ppermute x0 -> x21, waiting for transfers between devices: none -> 14.2 us  [shift(): return lax.ppermute(x, axis, [(i, (i + by) % count) for i in range(count)])]
  transfers between devices with their start and end apart: 6 -> 21, of which waited for: 6 -> 6; matrix products, arithmetic and copies ran while one was open for 13% -> 1% of each run, Pallas kernels for 0% -> 35%
where the time goes in v2:
time: 83.2 us; the launch traced here: 82.7 us
  Pallas kernels  42 us (50%)
  starting transfers between devices  16.6 us (20%)
  waiting for transfers between devices  14.2 us (17%)
  local copies, waits for them, and re-layouts  7.38 us (9%)
  other arithmetic  1.74 us (2%)
    pallas_call x2, Pallas kernels, weight_grads(): pl.pallas_call(functools.partial(weight_kernel, into is not None), grid_s...  19.6 us
    ppermute x21, starting transfers between devices, shift(): return lax.ppermute(x, axis, [(i, (i + by) % count) for i in range(count)])  16.6 us
    ppermute x21, waiting for transfers between devices, shift(): return lax.ppermute(x, axis, [(i, (i + by) % count) for i in range(count)])  14.2 us
    pallas_call x1, Pallas kernels, forward(): pl.pallas_call(functools.partial(forward_kernel, places, n_tensor, top, o...  10.9 us
    unnamed x17, local copies, waits for them, and re-layouts  7.29 us
    pallas_call x1, Pallas kernels, load_weights(): pl.pallas_call(functools.partial(load_kernel, own), in_specs=[SMEM, ANY,...  6.97 us
    pallas_call x1, Pallas kernels, body(): pl.pallas_call(functools.partial(finish_kernel, top), in_specs=[VMEM] * (...  2.02 us
  transfers between devices with their start and end apart: 21, of which 6 were waited for; matrix products, arithmetic and copies ran while one was open for 1% of the time, Pallas kernels for 35%

profile of v2, /device:TPU:0, one launch (start us, length us, event | category | flops | bytes accessed | tf_op | source)
XLA Modules:
  0.0 82.7 jit_solution(18169478716472638611)
XLA Ops:
  0.6 0.7 convert_element_type.5
  1.3 0.1 copy.19
  1.4 0.8 copy.20
  2.2 0.1 fusion.2
  2.3 0.9 %pad_maximum_fusion.refs_0_ = bf16[32,2176]{1,0:T(8,128)(2,1)S(1)} fusion(bf16[32,128]{1,0:T(8,128)(2,1)S(1)} %fusion.2, bf16[32,1024]{1,0:T(8,128)(2,1)} %param.8, bf16[32,1024]{1,0:T(8,128)(2,1)} %param.7), kind=kLoop, calls=%fused_computation | loop fusion | flops 417792 | bytes 278528 | tf_op jit(solution)/shard_map/concatenate | solution.py:318
  3.2 3.1 %collective-permute-start = (bf16[32,2176]{1,0:T(8,128)(2,1)S(1)}, bf16[32,2176]{1,0:T(8,128)(2,1)S(1)}, u32[]{:S(2)}, u32[]{:S(2)}) collective-permute-start(bf16[32,2176]{1,0:T(8,128)(2,1)S(1)} %pad_maximum_fusion.refs_0_), channel_id=1, source_target_pairs={{0,4},{4,8},{8,12},{12,0},{1,5},{5,9},{9,13},{13,1},{2,6},{6,10},{... | collective-permute-start | bytes 417800 | tf_op jit(solution)/shard_map/ppermute | solution.py:196
  6.2 1.5 %collective-permute-start.3 = (bf16[32,2176]{1,0:T(8,128)(2,1)S(1)}, bf16[32,2176]{1,0:T(8,128)(2,1)S(1)}, u32[]{:S(2)}, u32[]{:S(2)}) collective-permute-start(bf16[32,2176]{1,0:T(8,128)(2,1)S(1)} %pad_maximum_fusion.refs_0_), channel_id=1, source_target_pairs={{0,2},{2,0},{1,3},{3,1},{4,6},{6,4},{5,7},{7,5},{8,10},{10,8},{9,1... | collective-permute-start | bytes 417800 | tf_op jit(solution)/shard_map/ppermute | solution.py:196
  7.7 2.2 %collective-permute-start.2 = (bf16[32,2176]{1,0:T(8,128)(2,1)S(1)}, bf16[32,2176]{1,0:T(8,128)(2,1)S(1)}, u32[]{:S(2)}, u32[]{:S(2)}) collective-permute-start(bf16[32,2176]{1,0:T(8,128)(2,1)S(1)} %pad_maximum_fusion.refs_0_), channel_id=1, source_target_pairs={{0,12},{4,0},{8,4},{12,8},{1,13},{5,1},{9,5},{13,9},{2,14},{6,2},{... | collective-permute-start | bytes 417800 | tf_op jit(solution)/shard_map/ppermute | solution.py:196
  10.0 0.8 collective-permute-start.1
  10.8 0.0 collective-permute-start.7
  10.8 0.1 pad_add_fusion.first_ref.scalars
  10.8 7.0 %load_weights.1 = (bf16[2048,3072]{1,0:T(8,128)(2,1)S(1)}, bf16[1536,2048]{1,0:T(8,128)(2,1)S(1)}) custom-call(s32[4]{0:T(128)S(1)} %pad_add_fusion.first_ref.scalars, bf16[8,2048,384]{2,1,0:T(8,128)(2,1)} %wg_ref.1, bf16[8,2048,384]{2,1,0:T(8,128)(2,1)} %wu_ref.1, bf16[8,384,2048]{2,1,0:T(8,128)(2,1)} %wd_ref.1), custom_call_target="tpu_custom_call" | custom-call | bytes 18874368 | tf_op jit(solution)/shard_map/load_weights/pallas_call | solution.py:44
  17.8 0.0 collective-permute-done.refs_1_
  17.8 0.0 copy-start.6
  17.8 0.0 collective-permute-done.3.refs_4_
  17.9 0.6 collective-permute-start.11
  18.5 0.0 collective-permute-done.2.refs_3_
  18.5 0.1 collective-permute-start.10
  18.6 0.5 collective-permute-start.6
  19.1 1.8 %collective-permute-done.1.refs_2_ = bf16[32,2176]{1,0:T(8,128)(2,1)S(1)} collective-permute-done((bf16[32,2176]{1,0:T(8,128)(2,1)S(1)}, bf16[32,2176]{1,0:T(8,128)(2,1)S(1)}, u32[]{:S(2)}, u32[]{:S(2)}) %collective-permute-start.1) | collective-permute-done | bytes 139296 | tf_op jit(solution)/shard_map/ppermute | solution.py:196
  20.9 1.5 %collective-permute-start.5 = (bf16[32,2176]{1,0:T(8,128)(2,1)S(1)}, bf16[32,2176]{1,0:T(8,128)(2,1)S(1)}, u32[]{:S(2)}, u32[]{:S(2)}) collective-permute-start(bf16[32,2176]{1,0:T(8,128)(2,1)S(1)} %collective-permute-done.1.refs_2_), channel_id=1, source_target_pairs={{0,2},{2,0},{1,3},{3,1},{4,6},{6,4},{5,7},{7,5},{8,10},{10,8},{9,1... | collective-permute-start | bytes 417800 | tf_op jit(solution)/shard_map/ppermute | solution.py:196
  22.4 0.0 collective-permute-done.7.refs_8_
  22.4 0.5 collective-permute-start.4
  22.9 0.0 collective-permute-done.11.refs_12_
  22.9 0.0 collective-permute-start.8
  22.9 0.0 collective-permute-done.10.refs_11_
  22.9 0.5 collective-permute-start.9
  23.4 1.6 %collective-permute-done.6.refs_7_ = bf16[32,2176]{1,0:T(8,128)(2,1)S(1)} collective-permute-done((bf16[32,2176]{1,0:T(8,128)(2,1)S(1)}, bf16[32,2176]{1,0:T(8,128)(2,1)S(1)}, u32[]{:S(2)}, u32[]{:S(2)}) %collective-permute-start.6) | collective-permute-done | bytes 139296 | tf_op jit(solution)/shard_map/ppermute | solution.py:196
  25.0 0.0 collective-permute-start.14
  25.0 3.0 %collective-permute-done.5.refs_6_ = bf16[32,2176]{1,0:T(8,128)(2,1)S(1)} collective-permute-done((bf16[32,2176]{1,0:T(8,128)(2,1)S(1)}, bf16[32,2176]{1,0:T(8,128)(2,1)S(1)}, u32[]{:S(2)}, u32[]{:S(2)}) %collective-permute-start.5) | collective-permute-done | bytes 139296 | tf_op jit(solution)/shard_map/ppermute | solution.py:196
  28.0 0.0 collective-permute-start.13
  28.0 2.5 %collective-permute-done.4.refs_5_ = bf16[32,2176]{1,0:T(8,128)(2,1)S(1)} collective-permute-done((bf16[32,2176]{1,0:T(8,128)(2,1)S(1)}, bf16[32,2176]{1,0:T(8,128)(2,1)S(1)}, u32[]{:S(2)}, u32[]{:S(2)}) %collective-permute-start.4) | collective-permute-done | bytes 139296 | tf_op jit(solution)/shard_map/ppermute | solution.py:196
  30.5 0.0 collective-permute-start.12
  30.5 0.0 collective-permute-done.9.refs_10_
  30.5 0.0 collective-permute-done.8.refs_9_
  30.6 0.0 collective-permute-done.14.refs_15_
  30.6 0.0 collective-permute-done.13.refs_14_
  30.6 1.3 %collective-permute-done.12.refs_13_ = bf16[32,2176]{1,0:T(8,128)(2,1)S(1)} collective-permute-done((bf16[32,2176]{1,0:T(8,128)(2,1)S(1)}, bf16[32,2176]{1,0:T(8,128)(2,1)S(1)}, u32[]{:S(2)}, u32[]{:S(2)}) %collective-permute-start.12) | collective-permute-done | bytes 139296 | tf_op jit(solution)/shard_map/ppermute | solution.py:196
  31.9 10.9 %routed_forward.1 = (bf16[256,2048]{1,0:T(8,128)(2,1)S(1)}, bf16[256,2048]{1,0:T(8,128)(2,1)S(1)}, bf16[4,256,1152]{2,1,0:T(8,128)(2,1)}, f32[2,128,1152]{2,1,0:T(8,128)S(1)}, bf16[2,128,1152]{2,1,0:T(8,128)(2,1)S(1)}) custom-call(s32[4]{0:T(128)S(1)} %pad_add_fusion.first_ref.scalars, bf16[32,2176]{1,0:T(8,128)(2,1)S(1)} %pad_maximum_fusion.refs_0_, ...), custom_call_target="tpu_custom_call" | custom-call | flops 8053063680 | bytes 8388608 | tf_op jit(solution)/shard_map/routed_forward/pallas_call | solution.py:108
  42.8 1.0 %copy-done = f32[2,128,1152]{2,1,0:T(8,128)} copy-done((f32[2,128,1152]{2,1,0:T(8,128)}, f32[2,128,1152]{2,1,0:T(8,128)S(1)}, u32[]{:S(2)}) %copy-start) | copy-done | bytes 1179672
  43.8 1.0 %copy-done.1 = bf16[256,2048]{1,0:T(8,128)(2,1)} copy-done((bf16[256,2048]{1,0:T(8,128)(2,1)}, bf16[256,2048]{1,0:T(8,128)(2,1)S(1)}, u32[]{:S(2)}) %copy-start.1) | copy-done | bytes 1048600
  44.8 0.2 collective-permute-start.20
  45.0 0.4 collective-permute-start.15
  45.4 0.0 copy-done.6
  45.4 0.7 copy.21.ids_ref
  46.0 4.0 %collective-permute-done.15.got_ref = bf16[2,128,1152]{2,1,0:T(8,128)(2,1)S(1)} collective-permute-done((bf16[2,128,1152]{2,1,0:T(8,128)(2,1)S(1)}, bf16[2,128,1152]{2,1,0:T(8,128)(2,1)S(1)}, u32[]{:S(2)}, u32[]{:S(2)}) %collective-permute-start.15) | collective-permute-done | bytes 589856 | tf_op jit(solution)/shard_map/ppermute | solution.py:196
  50.0 1.4 %sum_over_cores.1 = (f32[128,1152]{1,0:T(8,128)S(1)}, bf16[128,1152]{1,0:T(8,128)(2,1)S(1)}) custom-call(f32[2,128,1152]{2,1,0:T(8,128)} %copy-done, bf16[2,128,1152]{2,1,0:T(8,128)(2,1)S(1)} %collective-permute-done.15.got_ref), custom_call_target="tpu_custom_call" | custom-call | tf_op jit(solution)/shard_map/sum_over_cores/pallas_call | solution.py:336
  51.4 0.6 collective-permute-start.16
  52.0 1.2 %copy-done.2 = bf16[256,2048]{1,0:T(8,128)(2,1)S(1)} copy-done((bf16[256,2048]{1,0:T(8,128)(2,1)S(1)}, bf16[256,2048]{1,0:T(8,128)(2,1)}, u32[]{:S(2)}) %copy-start.2) | copy-done | bytes 1048600
  53.2 10.1 %weight_grads.2 = (bf16[8,2048,384]{2,1,0:T(8,128)(2,1)}, bf16[8,2048,384]{2,1,0:T(8,128)(2,1)}, bf16[8,384,2048]{2,1,0:T(8,128)(2,1)}) custom-call(s32[4]{0:T(128)S(1)} %pad_add_fusion.first_ref.scalars, bf16[256,2048]{1,0:T(8,128)(2,1)S(1)} %get-tuple-element.48.x_ref, bf16[256,2048]{1,0:T(8,128)(2,1)S(1)} %copy-done.2, ...), custom_call_target="tpu_custom_call" | custom-call | flops 4831838208 | bytes 23068672 | tf_op jit(solution)/shard_map/weight_grads/pallas_call | solution.py:149
  63.3 0.0 collective-permute-done.16.got_ref
  63.3 1.1 %sum_over_tensor.1 = (f32[32,1152]{1,0:T(8,128)S(1)}, bf16[32,1152]{1,0:T(8,128)(2,1)S(1)}, bf16[32,1152]{1,0:T(8,128)(2,1)S(1)}, bf16[32,1152]{1,0:T(8,128)(2,1)S(1)}) custom-call(f32[128,1152]{1,0:T(8,128)} %copy-done.4, bf16[128,1152]{1,0:T(8,128)(2,1)S(1)} %collective-permute-done.16.got_ref), custom_call_target="tpu_custom_call" | custom-call | tf_op jit(solution)/shard_map/sum_over_tensor/pallas_call | solution.py:347
  64.5 1.4 %collective-permute-start.17 = (bf16[32,1152]{1,0:T(8,128)(2,1)S(1)}, bf16[32,1152]{1,0:T(8,128)(2,1)S(1)}, u32[]{:S(2)}, u32[]{:S(2)}) collective-permute-start(bf16[32,1152]{1,0:T(8,128)(2,1)S(1)} %get-tuple-element.56), channel_id=1, source_target_pairs={{0,12},{4,0},{8,4},{12,8},{1,13},{5,1},{9,5},{13,9},{2,14},{6,2},{... | collective-permute-start | bytes 221192 | tf_op jit(solution)/shard_map/ppermute | solution.py:196
  65.9 1.7 %collective-permute-start.18 = (bf16[32,1152]{1,0:T(8,128)(2,1)S(1)}, bf16[32,1152]{1,0:T(8,128)(2,1)S(1)}, u32[]{:S(2)}, u32[]{:S(2)}) collective-permute-start(bf16[32,1152]{1,0:T(8,128)(2,1)S(1)} %get-tuple-element.57), channel_id=1, source_target_pairs={{0,8},{4,12},{8,0},{12,4},{1,9},{5,13},{9,1},{13,5},{2,10},{6,14},... | collective-permute-start | bytes 221192 | tf_op jit(solution)/shard_map/ppermute | solution.py:196
  67.6 1.0 %collective-permute-start.19 = (bf16[32,1152]{1,0:T(8,128)(2,1)S(1)}, bf16[32,1152]{1,0:T(8,128)(2,1)S(1)}, u32[]{:S(2)}, u32[]{:S(2)}) collective-permute-start(bf16[32,1152]{1,0:T(8,128)(2,1)S(1)} %get-tuple-element.58), channel_id=1, source_target_pairs={{0,4},{4,8},{8,12},{12,0},{1,5},{5,9},{9,13},{13,1},{2,6},{6,10},{... | collective-permute-start | bytes 221192 | tf_op jit(solution)/shard_map/ppermute | solution.py:196
  68.5 0.0 collective-permute-done.20.grads_ref
  68.5 1.2 %copy-done.3 = bf16[256,2048]{1,0:T(8,128)(2,1)S(1)} copy-done((bf16[256,2048]{1,0:T(8,128)(2,1)S(1)}, bf16[256,2048]{1,0:T(8,128)(2,1)}, u32[]{:S(2)}) %copy-start.3) | copy-done | bytes 1048600
  69.8 9.5 %weight_grads.3 = (bf16[8,2048,384]{2,1,0:T(8,128)(2,1)}, bf16[8,2048,384]{2,1,0:T(8,128)(2,1)}, bf16[8,384,2048]{2,1,0:T(8,128)(2,1)}) custom-call(s32[1]{0:T(128)} %bitcast.3.scalars, bf16[256,2048]{1,0:T(8,128)(2,1)S(1)} %get-tuple-element.48.x_ref, bf16[256,2048]{1,0:T(8,128)(2,1)S(1)} %copy-done.3, ...), custom_call_target="tpu_custom_call", output_to_operand_aliasing={{0}: (4, {}), {1}: (5, {}), {2}: (6, {})} | custom-call | flops 4831838208 | bytes 23068672 | tf_op jit(solution)/shard_map/weight_grads/pallas_call | solution.py:149
  79.3 0.0 copy-done.5
  79.3 0.0 collective-permute-done.17.refs_0_
  79.3 0.0 collective-permute-done.18.refs_1_
  79.3 0.0 collective-permute-done.19.refs_2_
  79.3 2.0 %sum_over_experts.1 = (bf16[32,1024]{1,0:T(8,128)(2,1)}, f32[32,8]{1,0:T(8,128)}) custom-call(s32[32,8]{1,0:T(8,128)} %copy.21.ids_ref, f32[32,1152]{1,0:T(8,128)} %copy-done.5, bf16[32,1152]{1,0:T(8,128)(2,1)S(1)} %collective-permute-done.17.refs_0_, bf16[32,1152]{1,0:T(8,128)(2,1)S(1)} %collective-permute-done.18.refs_1_, ...), custom_call_target="tpu_custom_call" | custom-call | tf_op jit(solution)/shard_map/sum_over_experts/pallas_call | solution.py:357
  81.3 1.4 %copy.22 = f32[32,8]{0,1:T(8,128)} copy(f32[32,8]{1,0:T(8,128)} %get-tuple-element.79) | data formatting | bytes 2048
  (7 shorter events, 0.0 us)
Async XLA Ops:
  3.2 14.7 %collective-permute-start = (bf16[32,2176]{1,0:T(8,128)(2,1)S(1)}, bf16[32,2176]{1,0:T(8,128)(2,1)S(1)}, u32[]{:S(2)}, u32[]{:S(2)}) collective-permute-start(bf16[32,2176]{1,0:T(8,128)(2,1)S(1)} %pad_maximum_fusion.refs_0_), channel_id=1, source_target_pairs={{0,4},{4,8},{8,12},{12,0},{1,5},{5,9},{9,13},{13,1},{2,6},{6,10},{... | collective-permute-start | bytes 417800 | tf_op jit(solution)/shard_map/ppermute | solution.py:196
  6.2 11.6 %collective-permute-start.3 = (bf16[32,2176]{1,0:T(8,128)(2,1)S(1)}, bf16[32,2176]{1,0:T(8,128)(2,1)S(1)}, u32[]{:S(2)}, u32[]{:S(2)}) collective-permute-start(bf16[32,2176]{1,0:T(8,128)(2,1)S(1)} %pad_maximum_fusion.refs_0_), channel_id=1, source_target_pairs={{0,2},{2,0},{1,3},{3,1},{4,6},{6,4},{5,7},{7,5},{8,10},{10,8},{9,1... | collective-permute-start | bytes 417800 | tf_op jit(solution)/shard_map/ppermute | solution.py:196
  7.7 10.7 %collective-permute-start.2 = (bf16[32,2176]{1,0:T(8,128)(2,1)S(1)}, bf16[32,2176]{1,0:T(8,128)(2,1)S(1)}, u32[]{:S(2)}, u32[]{:S(2)}) collective-permute-start(bf16[32,2176]{1,0:T(8,128)(2,1)S(1)} %pad_maximum_fusion.refs_0_), channel_id=1, source_target_pairs={{0,12},{4,0},{8,4},{12,8},{1,13},{5,1},{9,5},{13,9},{2,14},{6,2},{... | collective-permute-start | bytes 417800 | tf_op jit(solution)/shard_map/ppermute | solution.py:196
  10.0 10.9 %collective-permute-start.1 = (bf16[32,2176]{1,0:T(8,128)(2,1)S(1)}, bf16[32,2176]{1,0:T(8,128)(2,1)S(1)}, u32[]{:S(2)}, u32[]{:S(2)}) collective-permute-start(bf16[32,2176]{1,0:T(8,128)(2,1)S(1)} %pad_maximum_fusion.refs_0_), channel_id=1, source_target_pairs={{0,8},{4,12},{8,0},{12,4},{1,9},{5,13},{9,1},{13,5},{2,10},{6,14},... | collective-permute-start | bytes 417800 | tf_op jit(solution)/shard_map/ppermute | solution.py:196
  10.8 11.6 %collective-permute-start.7 = (bf16[32,2176]{1,0:T(8,128)(2,1)S(1)}, bf16[32,2176]{1,0:T(8,128)(2,1)S(1)}, u32[]{:S(2)}, u32[]{:S(2)}) collective-permute-start(bf16[32,2176]{1,0:T(8,128)(2,1)S(1)} %pad_maximum_fusion.refs_0_), channel_id=1, source_target_pairs={{0,1},{1,0},{2,3},{3,2},{4,5},{5,4},{6,7},{7,6},{8,9},{9,8},{10,11... | collective-permute-start | bytes 417800 | tf_op jit(solution)/shard_map/ppermute | solution.py:196
  17.8 27.5 %copy-start.6 = (s32[32,8]{0,1:T(8,128)S(1)}, s32[32,8]{0,1:T(8,128)}, u32[]{:S(2)}) copy-start(s32[32,8]{0,1:T(8,128)} %param.9) | copy-start | bytes 3076
  17.9 5.1 %collective-permute-start.11 = (bf16[32,2176]{1,0:T(8,128)(2,1)S(1)}, bf16[32,2176]{1,0:T(8,128)(2,1)S(1)}, u32[]{:S(2)}, u32[]{:S(2)}) collective-permute-start(bf16[32,2176]{1,0:T(8,128)(2,1)S(1)} %collective-permute-done.3.refs_4_), channel_id=1, source_target_pairs={{0,1},{1,0},{2,3},{3,2},{4,5},{5,4},{6,7},{7,6},{8,9},{9,8},{10,11... | collective-permute-start | bytes 417800 | tf_op jit(solution)/shard_map/ppermute | solution.py:196
  18.5 4.5 %collective-permute-start.10 = (bf16[32,2176]{1,0:T(8,128)(2,1)S(1)}, bf16[32,2176]{1,0:T(8,128)(2,1)S(1)}, u32[]{:S(2)}, u32[]{:S(2)}) collective-permute-start(bf16[32,2176]{1,0:T(8,128)(2,1)S(1)} %collective-permute-done.2.refs_3_), channel_id=1, source_target_pairs={{0,1},{1,0},{2,3},{3,2},{4,5},{5,4},{6,7},{7,6},{8,9},{9,8},{10,11... | collective-permute-start | bytes 417800 | tf_op jit(solution)/shard_map/ppermute | solution.py:196
  18.6 6.5 %collective-permute-start.6 = (bf16[32,2176]{1,0:T(8,128)(2,1)S(1)}, bf16[32,2176]{1,0:T(8,128)(2,1)S(1)}, u32[]{:S(2)}, u32[]{:S(2)}) collective-permute-start(bf16[32,2176]{1,0:T(8,128)(2,1)S(1)} %collective-permute-done.2.refs_3_), channel_id=1, source_target_pairs={{0,2},{2,0},{1,3},{3,1},{4,6},{6,4},{5,7},{7,5},{8,10},{10,8},{9,1... | collective-permute-start | bytes 417800 | tf_op jit(solution)/shard_map/ppermute | solution.py:196
  20.9 7.1 %collective-permute-start.5 = (bf16[32,2176]{1,0:T(8,128)(2,1)S(1)}, bf16[32,2176]{1,0:T(8,128)(2,1)S(1)}, u32[]{:S(2)}, u32[]{:S(2)}) collective-permute-start(bf16[32,2176]{1,0:T(8,128)(2,1)S(1)} %collective-permute-done.1.refs_2_), channel_id=1, source_target_pairs={{0,2},{2,0},{1,3},{3,1},{4,6},{6,4},{5,7},{7,5},{8,10},{10,8},{9,1... | collective-permute-start | bytes 417800 | tf_op jit(solution)/shard_map/ppermute | solution.py:196
  22.4 8.2 %collective-permute-start.4 = (bf16[32,2176]{1,0:T(8,128)(2,1)S(1)}, bf16[32,2176]{1,0:T(8,128)(2,1)S(1)}, u32[]{:S(2)}, u32[]{:S(2)}) collective-permute-start(bf16[32,2176]{1,0:T(8,128)(2,1)S(1)} %collective-permute-done.refs_1_), channel_id=1, source_target_pairs={{0,2},{2,0},{1,3},{3,1},{4,6},{6,4},{5,7},{7,5},{8,10},{10,8},{9,1... | collective-permute-start | bytes 417800 | tf_op jit(solution)/shard_map/ppermute | solution.py:196
  22.9 7.6 %collective-permute-start.8 = (bf16[32,2176]{1,0:T(8,128)(2,1)S(1)}, bf16[32,2176]{1,0:T(8,128)(2,1)S(1)}, u32[]{:S(2)}, u32[]{:S(2)}) collective-permute-start(bf16[32,2176]{1,0:T(8,128)(2,1)S(1)} %collective-permute-done.refs_1_), channel_id=1, source_target_pairs={{0,1},{1,0},{2,3},{3,2},{4,5},{5,4},{6,7},{7,6},{8,9},{9,8},{10,11... | collective-permute-start | bytes 417800 | tf_op jit(solution)/shard_map/ppermute | solution.py:196
  22.9 7.6 %collective-permute-start.9 = (bf16[32,2176]{1,0:T(8,128)(2,1)S(1)}, bf16[32,2176]{1,0:T(8,128)(2,1)S(1)}, u32[]{:S(2)}, u32[]{:S(2)}) collective-permute-start(bf16[32,2176]{1,0:T(8,128)(2,1)S(1)} %collective-permute-done.1.refs_2_), channel_id=1, source_target_pairs={{0,1},{1,0},{2,3},{3,2},{4,5},{5,4},{6,7},{7,6},{8,9},{9,8},{10,11... | collective-permute-start | bytes 417800 | tf_op jit(solution)/shard_map/ppermute | solution.py:196
  25.0 5.5 %collective-permute-start.14 = (bf16[32,2176]{1,0:T(8,128)(2,1)S(1)}, bf16[32,2176]{1,0:T(8,128)(2,1)S(1)}, u32[]{:S(2)}, u32[]{:S(2)}) collective-permute-start(bf16[32,2176]{1,0:T(8,128)(2,1)S(1)} %collective-permute-done.6.refs_7_), channel_id=1, source_target_pairs={{0,1},{1,0},{2,3},{3,2},{4,5},{5,4},{6,7},{7,6},{8,9},{9,8},{10,11... | collective-permute-start | bytes 417800 | tf_op jit(solution)/shard_map/ppermute | solution.py:196
  28.0 2.5 %collective-permute-start.13 = (bf16[32,2176]{1,0:T(8,128)(2,1)S(1)}, bf16[32,2176]{1,0:T(8,128)(2,1)S(1)}, u32[]{:S(2)}, u32[]{:S(2)}) collective-permute-start(bf16[32,2176]{1,0:T(8,128)(2,1)S(1)} %collective-permute-done.5.refs_6_), channel_id=1, source_target_pairs={{0,1},{1,0},{2,3},{3,2},{4,5},{5,4},{6,7},{7,6},{8,9},{9,8},{10,11... | collective-permute-start | bytes 417800 | tf_op jit(solution)/shard_map/ppermute | solution.py:196
  30.5 1.4 %collective-permute-start.12 = (bf16[32,2176]{1,0:T(8,128)(2,1)S(1)}, bf16[32,2176]{1,0:T(8,128)(2,1)S(1)}, u32[]{:S(2)}, u32[]{:S(2)}) collective-permute-start(bf16[32,2176]{1,0:T(8,128)(2,1)S(1)} %collective-permute-done.4.refs_5_), channel_id=1, source_target_pairs={{0,1},{1,0},{2,3},{3,2},{4,5},{5,4},{6,7},{7,6},{8,9},{9,8},{10,11... | collective-permute-start | bytes 417800 | tf_op jit(solution)/shard_map/ppermute | solution.py:196
  42.8 1.0 %copy-start = (f32[2,128,1152]{2,1,0:T(8,128)}, f32[2,128,1152]{2,1,0:T(8,128)S(1)}, u32[]{:S(2)}) copy-start(f32[2,128,1152]{2,1,0:T(8,128)S(1)} %get-tuple-element.44.kept_ref) | copy-start | bytes 3538948
  43.8 1.0 %copy-start.1 = (bf16[256,2048]{1,0:T(8,128)(2,1)}, bf16[256,2048]{1,0:T(8,128)(2,1)S(1)}, u32[]{:S(2)}) copy-start(bf16[256,2048]{1,0:T(8,128)(2,1)S(1)} %get-tuple-element.49.og_ref) | copy-start | bytes 3145732
  44.8 23.7 %collective-permute-start.20 = (bf16[4,256,1152]{2,1,0:T(8,128)(2,1)}, bf16[4,256,1152]{2,1,0:T(8,128)(2,1)}, u32[]{:S(2)}, u32[]{:S(2)}) collective-permute-start(bf16[4,256,1152]{2,1,0:T(8,128)(2,1)} %get-tuple-element.50.grads_ref), channel_id=1, source_target_pairs={{0,1},{1,0},{2,3},{3,2},{4,5},{5,4},{6,7},{7,6},{8,9},{9,8},{10,11... | collective-permute-start | bytes 7077896 | tf_op jit(solution)/shard_map/ppermute | solution.py:196
  45.0 5.0 %collective-permute-start.15 = (bf16[2,128,1152]{2,1,0:T(8,128)(2,1)S(1)}, bf16[2,128,1152]{2,1,0:T(8,128)(2,1)S(1)}, u32[]{:S(2)}, u32[]{:S(2)}) collective-permute-start(bf16[2,128,1152]{2,1,0:T(8,128)(2,1)S(1)} %get-tuple-element.45), channel_id=1, source_target_pairs={{0,1},{1,0},{2,3},{3,2},{4,5},{5,4},{6,7},{7,6},{8,9},{9,8},{10,11... | collective-permute-start | bytes 1769480 | tf_op jit(solution)/shard_map/ppermute | solution.py:196
  51.4 11.9 %copy-start.4 = (f32[128,1152]{1,0:T(8,128)}, f32[128,1152]{1,0:T(8,128)S(1)}, u32[]{:S(2)}) copy-start(f32[128,1152]{1,0:T(8,128)S(1)} %get-tuple-element.46.here_ref) | copy-start | bytes 1769476
  51.4 11.9 %collective-permute-start.16 = (bf16[128,1152]{1,0:T(8,128)(2,1)S(1)}, bf16[128,1152]{1,0:T(8,128)(2,1)S(1)}, u32[]{:S(2)}, u32[]{:S(2)}) collective-permute-start(bf16[128,1152]{1,0:T(8,128)(2,1)S(1)} %get-tuple-element.47), channel_id=1, source_target_pairs={{0,2},{2,0},{1,3},{3,1},{4,6},{6,4},{5,7},{7,5},{8,10},{10,8},{9,1... | collective-permute-start | bytes 884744 | tf_op jit(solution)/shard_map/ppermute | solution.py:196
  52.0 1.2 %copy-start.2 = (bf16[256,2048]{1,0:T(8,128)(2,1)S(1)}, bf16[256,2048]{1,0:T(8,128)(2,1)}, u32[]{:S(2)}) copy-start(bf16[256,2048]{1,0:T(8,128)(2,1)} %copy-done.1) | copy-start | bytes 3145732
  64.4 14.8 %copy-start.5 = (f32[32,1152]{1,0:T(8,128)}, f32[32,1152]{1,0:T(8,128)S(1)}, u32[]{:S(2)}) copy-start(f32[32,1152]{1,0:T(8,128)S(1)} %get-tuple-element.55.own_ref) | copy-start | bytes 442372
  64.5 14.8 %collective-permute-start.17 = (bf16[32,1152]{1,0:T(8,128)(2,1)S(1)}, bf16[32,1152]{1,0:T(8,128)(2,1)S(1)}, u32[]{:S(2)}, u32[]{:S(2)}) collective-permute-start(bf16[32,1152]{1,0:T(8,128)(2,1)S(1)} %get-tuple-element.56), channel_id=1, source_target_pairs={{0,12},{4,0},{8,4},{12,8},{1,13},{5,1},{9,5},{13,9},{2,14},{6,2},{... | collective-permute-start | bytes 221192 | tf_op jit(solution)/shard_map/ppermute | solution.py:196
  65.9 13.4 %collective-permute-start.18 = (bf16[32,1152]{1,0:T(8,128)(2,1)S(1)}, bf16[32,1152]{1,0:T(8,128)(2,1)S(1)}, u32[]{:S(2)}, u32[]{:S(2)}) collective-permute-start(bf16[32,1152]{1,0:T(8,128)(2,1)S(1)} %get-tuple-element.57), channel_id=1, source_target_pairs={{0,8},{4,12},{8,0},{12,4},{1,9},{5,13},{9,1},{13,5},{2,10},{6,14},... | collective-permute-start | bytes 221192 | tf_op jit(solution)/shard_map/ppermute | solution.py:196
  67.6 11.7 %collective-permute-start.19 = (bf16[32,1152]{1,0:T(8,128)(2,1)S(1)}, bf16[32,1152]{1,0:T(8,128)(2,1)S(1)}, u32[]{:S(2)}, u32[]{:S(2)}) collective-permute-start(bf16[32,1152]{1,0:T(8,128)(2,1)S(1)} %get-tuple-element.58), channel_id=1, source_target_pairs={{0,4},{4,8},{8,12},{12,0},{1,5},{5,9},{9,13},{13,1},{2,6},{6,10},{... | collective-permute-start | bytes 221192 | tf_op jit(solution)/shard_map/ppermute | solution.py:196
  68.5 1.2 %copy-start.3 = (bf16[256,2048]{1,0:T(8,128)(2,1)S(1)}, bf16[256,2048]{1,0:T(8,128)(2,1)}, u32[]{:S(2)}) copy-start(bf16[256,2048]{1,0:T(8,128)(2,1)} %copy-done.1) | copy-start | bytes 3145732

commit v3 on v2

--- a/solution.py
+++ b/solution.py
@@ -9,6 +9,7 @@
 
 CAP = 16
 META = 128
+PARTS = 2
 MIB = 1024 * 1024
 NT = (((1,), (1,)), ((), ()))
 TN = (((0,), (0,)), ((), ()))
@@ -25,32 +26,71 @@
     return [pltpu.with_memory_space_constraint(x, pltpu.HBM) for x in arrays]
 
 
-def load_kernel(own, first_ref, wg_ref, wu_ref, wd_ref, in_ref, out_ref, sem):
-    ff = wd_ref.shape[1]
+def pack_kernel(top, act_hbm, og_hbm, ids_hbm, probs_hbm, out_ref, ids_ref, probs_ref, sems):
+    rows, wide = act_hbm.shape
+    copies = [
+        pltpu.make_async_copy(act_hbm, out_ref.at[:, :wide], sems.at[0]),
+        pltpu.make_async_copy(og_hbm, out_ref.at[:, wide : 2 * wide], sems.at[1]),
+        pltpu.make_async_copy(ids_hbm, ids_ref, sems.at[2]),
+        pltpu.make_async_copy(probs_hbm, probs_ref, sems.at[3]),
+    ]
+    for copy in copies:
+        copy.start()
+    for copy in copies[2:]:
+        copy.wait()
+    meta = jnp.concatenate([ids_ref[...].astype(jnp.float32), probs_ref[...].astype(jnp.float32)], axis=0)
+    meta = jnp.concatenate([meta, jnp.zeros((META - 2 * top, rows), jnp.float32)], axis=0)
+    out_ref[:, 2 * wide :] = meta.T.astype(jnp.bfloat16)
+    for copy in copies[:2]:
+        copy.wait()
+
+
+def pack(activations, out_grad, ids, probs):
+    rows, wide = activations.shape
+    return pl.pallas_call(
+        functools.partial(pack_kernel, ids.shape[0]),
+        in_specs=[ANY] * 4,
+        out_specs=VMEM,
+        out_shape=pltpu.VMEM((rows, 2 * wide + META), jnp.bfloat16),
+        scratch_shapes=[
+            pltpu.VMEM(ids.shape, ids.dtype),
+            pltpu.VMEM(probs.shape, probs.dtype),
+            pltpu.SemaphoreType.DMA((4,)),
+        ],
+        compiler_params=pltpu.CompilerParams(vmem_limit_bytes=4 * MIB),
+        name="pack_tokens",
+    )(*far(activations, out_grad, ids, probs))
+
+
+def load_kernel(by_row, first_ref, *refs):
+    *sources, target_ref, sem = refs
     copies = []
-    for i in range(own):
-        for j, source in enumerate((wg_ref, wu_ref)):
-            target = in_ref.at[:, pl.ds((2 * i + j) * ff, ff)]
+    count, step = len(sources), sources[0].shape[1 if by_row else 2]
+    for i in range(target_ref.shape[0 if by_row else 1] // (count * step)):
+        for j, source in enumerate(sources):
+            at = pl.ds((count * i + j) * step, step)
+            target = target_ref.at[at, :] if by_row else target_ref.at[:, at]
             copies.append(pltpu.make_async_copy(source.at[first_ref[0] + i], target, sem))
-        copies.append(pltpu.make_async_copy(wd_ref.at[first_ref[0] + i], out_ref.at[pl.ds(i * ff, ff), :], sem))
     for copy in copies:
         copy.start()
     for copy in copies:
         copy.wait()
 
 
-def load_weights(scalars, w_gate, w_up, w_down, own):
-    _, d, ff = w_gate.shape
+def load_weights(first, sources, count, by_row):
+    _, rows, columns = sources[0].shape
+    many = count * len(sources)
+    shape = (many * rows, columns) if by_row else (rows, many * columns)
     return pl.pallas_call(
-        functools.partial(load_kernel, own),
-        in_specs=[SMEM, ANY, ANY, ANY],
-        out_specs=[VMEM, VMEM],
-        out_shape=[pltpu.VMEM((d, own * 2 * ff), jnp.bfloat16), pltpu.VMEM((own * ff, d), jnp.bfloat16)],
+        functools.partial(load_kernel, by_row),
+        in_specs=[SMEM] + [ANY] * len(sources),
+        out_specs=VMEM,
+        out_shape=pltpu.VMEM(shape, jnp.bfloat16),
         scratch_shapes=[pltpu.SemaphoreType.DMA],
         compiler_params=pltpu.CompilerParams(vmem_limit_bytes=4 * MIB),
-        cost_estimate=pl.CostEstimate(flops=0, bytes_accessed=6 * own * d * ff, transcendentals=0),
+        cost_estimate=pl.CostEstimate(flops=0, bytes_accessed=2 * many * rows * columns, transcendentals=0),
         name="load_weights",
-    )(scalars, *far(w_gate, w_up, w_down))
+    )(first, *far(*sources))
 
 
 def forward_kernel(places, n_tensor, top, own, scalars, *refs):
@@ -102,8 +142,8 @@
         sent_ref[side, :, wide:] = inners[share:].astype(jnp.bfloat16)
 
 
-def forward(shards, places, scalars, w_in, w_out, own, tokens, n_tensor, top):
-    d, ff = w_out.shape[1], w_out.shape[0] // own
+def forward(shards, places, scalars, weights, own, tokens, n_tensor, top):
+    d, ff = weights[1].shape[1], weights[1].shape[0] // own
     sums = (n_tensor, tokens // 2, d // n_tensor + META)
     return pl.pallas_call(
         functools.partial(forward_kernel, places, n_tensor, top, own),
@@ -117,51 +157,62 @@
             pltpu.VMEM(sums, jnp.bfloat16),
         ],
         scratch_shapes=[pltpu.VMEM((tokens, META), jnp.float32)],
-        compiler_params=pltpu.CompilerParams(vmem_limit_bytes=20 * MIB),
+        compiler_params=pltpu.CompilerParams(vmem_limit_bytes=16 * MIB),
         cost_estimate=pl.CostEstimate(
             flops=10 * own * tokens * d * ff, bytes_accessed=16 * tokens * d, transcendentals=0
         ),
         name="routed_forward",
-    )(scalars, *near(*shards), w_in, w_out)
-
-
-def weight_kernel(swap, scalars, x_ref, og_ref, grads_ref, *refs):
-    gate_ref, up_ref, down_ref = refs[-3:]
-    ff = gate_ref.shape[2]
-    grads = grads_ref[0]
-    if swap:
-        half = grads.shape[0] // 2
-        grads = jnp.concatenate([grads[half:], grads[:half]], axis=0)
-    both = lax.dot_general(x_ref[...], grads[:, : 2 * ff], TN, preferred_element_type=jnp.float32)
-    gate_ref[0] = both[:, :ff].astype(jnp.bfloat16)
-    up_ref[0] = both[:, ff:].astype(jnp.bfloat16)
-    down = lax.dot_general(grads[:, 2 * ff :], og_ref[...], TN, preferred_element_type=jnp.float32)
-    down_ref[0] = down.astype(jnp.bfloat16)
-
-
-def weight_grads(scalars, x, og, grads, local_count, into=None):
+    )(scalars, *near(*shards, *weights))
+
+
+def weight_kernel(swap, first_ref, x_ref, og_ref, grads_ref, *refs):
+    *targets, gate_ref, up_ref, down_ref, sem = refs[-7:]
+    own, d, ff = gate_ref.shape
+    half, step = grads_ref.shape[1] // 2, d // PARTS
+    copies = []
+
+    def send(ref, target, i, at):
+        copies.append(pltpu.make_async_copy(ref.at[(i, *at)], target.at[(first_ref[0] + i, *at)], sem))
+        copies[-1].start()
+
+    for i in range(own):
+        grads = grads_ref[i]
+        if swap:
+            grads = jnp.concatenate([grads[half:], grads[:half]], axis=0)
+        for part in range(PARTS):
+            at, every = pl.ds(part * step, step), pl.ds(0, ff)
+            total = lax.dot_general(x_ref[:, at], grads[:, : 2 * ff], TN, preferred_element_type=jnp.float32)
+            gate_ref[i, at, :] = total[:, :ff].astype(jnp.bfloat16)
+            up_ref[i, at, :] = total[:, ff:].astype(jnp.bfloat16)
+            send(gate_ref, targets[0], i, (at, every))
+            send(up_ref, targets[1], i, (at, every))
+        for part in range(PARTS):
+            at, every = pl.ds(part * step, step), pl.ds(0, ff)
+            total = lax.dot_general(grads[:, 2 * ff :], og_ref[:, at], TN, preferred_element_type=jnp.float32)
+            down_ref[i, :, at] = total.astype(jnp.bfloat16)
+            send(down_ref, targets[2], i, (every, at))
+    for copy in copies:
+        copy.wait()
+
+
+def weight_grads(first, x, og, grads, local_count, into=None):
     own, tokens, ff = grads.shape[0], grads.shape[1], grads.shape[2] // 3
     d = x.shape[1]
-    whole = pl.BlockSpec((tokens, d), lambda i, s: (0, 0))
-    out = lambda shape: pl.BlockSpec((1, *shape), lambda i, s: (s[0] + i, 0, 0))
     kept = [] if into is None else list(into)
     shapes = [(d, ff), (d, ff), (ff, d)]
     return pl.pallas_call(
         functools.partial(weight_kernel, into is not None),
-        grid_spec=pltpu.PrefetchScalarGridSpec(
-            num_scalar_prefetch=1,
-            grid=(own,),
-            in_specs=[whole, whole, pl.BlockSpec((1, tokens, 3 * ff), lambda i, s: (i, 0, 0))] + [ANY] * len(kept),
-            out_specs=[out(s) for s in shapes],
-        ),
-        out_shape=[jax.ShapeDtypeStruct((local_count, *s), jnp.bfloat16) for s in shapes],
+        in_specs=[SMEM] + [VMEM] * 3 + [ANY] * len(kept),
+        out_specs=[ANY] * 3,
+        out_shape=[pltpu.HBM((local_count, *s), jnp.bfloat16) for s in shapes],
+        scratch_shapes=[pltpu.VMEM((own, *s), jnp.bfloat16) for s in shapes] + [pltpu.SemaphoreType.DMA],
         input_output_aliases={4 + i: i for i in range(len(kept))},
-        compiler_params=pltpu.CompilerParams(vmem_limit_bytes=32 * MIB),
+        compiler_params=pltpu.CompilerParams(vmem_limit_bytes=26 * MIB),
         cost_estimate=pl.CostEstimate(
-            flops=6 * own * tokens * d * ff, bytes_accessed=6 * own * d * ff + 8 * tokens * d, transcendentals=0
+            flops=6 * own * tokens * d * ff, bytes_accessed=6 * own * d * ff, transcendentals=0
         ),
         name="weight_grads",
-    )(scalars, x, og, grads, *kept)
+    )(first, *near(x, og, grads), *kept)
 
 
 def dp_sum_kernel(kept_ref, got_ref, here_ref, there_ref):
@@ -183,12 +234,12 @@
         total = total + part[...].astype(jnp.float32)
     wide = grad_ref.shape[1]
     grad_ref[...] = total[:, :wide].astype(jnp.bfloat16)
-    inner = total[:, wide:]
+    inner = total[:, wide:].T
     ids = ids_ref[...]
-    lane = lax.broadcasted_iota(jnp.int32, inner.shape, 1)
+    expert = lax.broadcasted_iota(jnp.int32, inner.shape, 0)
     for k in range(top):
-        picked = jnp.where(lane == ids[:, k : k + 1], inner, 0.0)
-        probs_ref[:, k : k + 1] = jnp.sum(picked, axis=1, keepdims=True)
+        picked = jnp.where(expert == ids[k : k + 1, :], inner, 0.0)
+        probs_ref[k : k + 1, :] = jnp.sum(picked, axis=0, keepdims=True)
 
 
 def shift(x, axis, by):
@@ -313,24 +364,25 @@
     e, t, p = (lax.axis_index(a) for a in ("expert", "tensor", "dp"))
     first = p * own
     scalars = jnp.stack([first, t, e * local_count + first, own - first]).astype(jnp.int32)
-    meta = jnp.concatenate([expert_ids.astype(jnp.bfloat16), gate_probs], axis=1)
-    meta = jnp.pad(meta, ((0, 0), (0, META - 2 * top)))
-    packed = jnp.concatenate([activations, out_grad, meta], axis=1)
-    w_in, w_out = load_weights(scalars, w_gate, w_up, w_down, own)
+    ids = expert_ids.T
+    packed = pack(activations, out_grad, ids, gate_probs.T)
     along = [packed] + [shift(packed, "expert", k) for k in range(1, n_expert)]
-    along[1], w_in, w_out = lax.optimization_barrier((along[1], w_in, w_out))
-    shards, places = [], []
-    for side in range(n_tensor):
-        for k in range(n_expert):
-            shards.append(along[k] if side == 0 else shift(along[k], "tensor", 1))
-            places.append((k * rows, side))
+    w_in = load_weights(scalars, (w_gate, w_up), own, False)
+    along[3], w_in, then = lax.optimization_barrier((along[3], w_in, scalars))
+    across = [shift(along[0], "tensor", 1), None, None, shift(along[3], "tensor", 1)]
+    w_out = load_weights(then, (w_down,), own, True)
+    along[1], along[2], w_out = lax.optimization_barrier((along[1], along[2], w_out))
+    across[1], across[2] = (shift(x, "tensor", 1) for x in along[1:3])
+    shards = along + across
+    places = [(k * rows, side) for side in range(n_tensor) for k in range(n_expert)]
     for i in range(n_expert * n_tensor):
         shards.append(shift(shards[i], "dp", 1))
         places.append((tokens // 2 + places[i][0], places[i][1]))
     x, og, grads, kept, sent = forward(
-        shards, tuple(places), scalars, w_in, w_out, own, tokens, n_tensor, top
+        shards, tuple(places), scalars, (w_in, w_out), own, tokens, n_tensor, top
     )
     got = shift(sent, "dp", 1)
+    got, grads = lax.optimization_barrier((got, grads))
     got_grads = shift(grads, "dp", 1)
     half = (tokens // 2, wide + META)
     here, there = pl.pallas_call(
@@ -338,6 +390,7 @@
         in_specs=[VMEM] * 2,
         out_specs=[VMEM] * 2,
         out_shape=[pltpu.VMEM(half, jnp.float32), pltpu.VMEM(half, jnp.bfloat16)],
+        compiler_params=pltpu.CompilerParams(vmem_limit_bytes=4 * MIB),
         name="sum_over_cores",
     )(kept, *near(got))
     crossed = shift(there, "tensor", 1)
@@ -349,6 +402,7 @@
         in_specs=[VMEM] * 2,
         out_specs=[VMEM] * n_expert,
         out_shape=[pltpu.VMEM(piece, jnp.float32)] + [pltpu.VMEM(piece, jnp.bfloat16)] * (n_expert - 1),
+        compiler_params=pltpu.CompilerParams(vmem_limit_bytes=4 * MIB),
         name="sum_over_tensor",
     )(here, *near(crossed))
     received = [shift(pieces[k], "expert", -k) for k in range(1, n_expert)]
@@ -358,10 +412,11 @@
         functools.partial(finish_kernel, top),
         in_specs=[VMEM] * (n_expert + 1),
         out_specs=[VMEM] * 2,
-        out_shape=[jax.ShapeDtypeStruct((rows, wide), jnp.bfloat16), jax.ShapeDtypeStruct((rows, top), jnp.float32)],
+        out_shape=[jax.ShapeDtypeStruct((rows, wide), jnp.bfloat16), jax.ShapeDtypeStruct((top, rows), jnp.float32)],
+        compiler_params=pltpu.CompilerParams(vmem_limit_bytes=4 * MIB),
         name="sum_over_experts",
-    )(expert_ids, pieces[0], *near(*received))
-    return (grad, probs, *outputs)
+    )(ids, pieces[0], *near(*received))
+    return (grad, probs.T, *outputs)
 
 
 def solution(mesh):
@@ -382,5 +437,5 @@
         P(("groups", "expert"), "tensor", None),
     )
     sizes = dict(mesh.shape)
-    compact = sizes["expert"] <= 4 and sizes["tensor"] == 2 and sizes["dp"] == 2
+    compact = sizes["expert"] == 4 and sizes["tensor"] == 2 and sizes["dp"] == 2
     return jax.shard_map(body if compact else general_body, mesh=mesh, in_specs=in_specs, out_specs=out_specs, check_vma=False)

time: 83.2 us -> 65 us (0.78)
  local copies, waits for them, and re-layouts: 7.38 us -> 0.01 us
  Pallas kernels: 42 us -> 34.8 us
  other arithmetic: 1.74 us -> 0.08 us
  waiting for transfers between devices: 14.2 us -> 12.9 us
    unnamed x17 -> x2, local copies, waits for them, and re-layouts: 7.29 us -> 0.01 us
    pallas_call x3 -> x5, Pallas kernels: 26.5 us -> 23.9 us  [the longest x2 14.5 us: weight_grads(): pl.pallas_call(functools.partial(weight_kernel, into is not None), in_spe...]
    ppermute x21, waiting for transfers between devices: 14.2 us -> 12.9 us  [shift(): return lax.ppermute(x, axis, [(i, (i + by) % count) for i in range(count)])]
    pallas_call x1, Pallas kernels: 1.37 us -> 0.14 us  [body(): pl.pallas_call(dp_sum_kernel, in_specs=[VMEM] * 2, out_specs=[VMEM] * 2,...]
    pallas_call x1, Pallas kernels: 2.02 us -> 0.84 us  [body(): pl.pallas_call(functools.partial(finish_kernel, top), in_specs=[VMEM] * (...]
    pallas_call x1, Pallas kernels: 10.9 us -> 9.81 us  [forward(): pl.pallas_call(functools.partial(forward_kernel, places, n_tensor, top, o...]
    pallas_call x1, Pallas kernels: 1.14 us -> 0.05 us  [body(): pl.pallas_call(tensor_sum_kernel, in_specs=[VMEM] * 2, out_specs=[VMEM] *...]
    concatenate x2 -> x0, other arithmetic: 0.97 us -> none  [the longest x1 0.89 us: body(): packed = jnp.concatenate([activations, out_grad, meta], axis=1)]
  transfers between devices with their start and end apart: 21 -> 21, of which waited for: 6 -> 6; matrix products, arithmetic and copies ran while one was open for 1% -> 0% of each run, Pallas kernels for 35% -> 36%
where the time goes in v3:
time: 65 us; the launch traced here: 64.9 us
  Pallas kernels  34.8 us (54%)
  starting transfers between devices  16.4 us (25%)
  waiting for transfers between devices  12.9 us (20%)
  between operations  0.78 us (1%)
    ppermute x21, starting transfers between devices, shift(): return lax.ppermute(x, axis, [(i, (i + by) % count) for i in range(count)])  16.4 us
    pallas_call x2, Pallas kernels, weight_grads(): pl.pallas_call(functools.partial(weight_kernel, into is not None), in_spe...  14.5 us
    ppermute x21, waiting for transfers between devices, shift(): return lax.ppermute(x, axis, [(i, (i + by) % count) for i in range(count)])  12.9 us
    pallas_call x1, Pallas kernels, forward(): pl.pallas_call(functools.partial(forward_kernel, places, n_tensor, top, o...  9.81 us
    pallas_call x2, Pallas kernels, load_weights(): pl.pallas_call(functools.partial(load_kernel, by_row), in_specs=[SMEM] +...  8.57 us
  transfers between devices with their start and end apart: 21, of which 6 were waited for; matrix products, arithmetic and copies ran while one was open for 0% of the time, Pallas kernels for 36%

profile of v3, /device:TPU:0, one launch (start us, length us, event | category | flops | bytes accessed | tf_op | source)
XLA Modules:
  0.0 64.9 jit_solution(6971181574926702396)
XLA Ops:
  0.6 0.9 %pack_tokens.1.refs_0_ = bf16[32,2176]{1,0:T(8,128)(2,1)S(1)} custom-call(bf16[32,1024]{1,0:T(8,128)(2,1)} %act_hbm.1, bf16[32,1024]{1,0:T(8,128)(2,1)} %og_hbm.1, s32[8,32]{1,0:T(8,128)} %bitcast.7, bf16[8,32]{1,0:T(8,128)(2,1)} %bitcast.9), custom_call_target="tpu_custom_call" | custom-call | tf_op jit(solution)/shard_map/pack_tokens/pallas_call | solution.py:50
  1.5 5.1 %collective-permute-start.2 = (bf16[32,2176]{1,0:T(8,128)(2,1)S(1)}, bf16[32,2176]{1,0:T(8,128)(2,1)S(1)}, u32[]{:S(2)}, u32[]{:S(2)}) collective-permute-start(bf16[32,2176]{1,0:T(8,128)(2,1)S(1)} %pack_tokens.1.refs_0_), channel_id=1, source_target_pairs={{0,12},{4,0},{8,4},{12,8},{1,13},{5,1},{9,5},{13,9},{2,14},{6,2},{... | collective-permute-start | bytes 417800 | tf_op jit(solution)/shard_map/ppermute | solution.py:247
  6.6 1.5 %collective-permute-start.3 = (bf16[32,2176]{1,0:T(8,128)(2,1)S(1)}, bf16[32,2176]{1,0:T(8,128)(2,1)S(1)}, u32[]{:S(2)}, u32[]{:S(2)}) collective-permute-start(bf16[32,2176]{1,0:T(8,128)(2,1)S(1)} %pack_tokens.1.refs_0_), channel_id=1, source_target_pairs={{0,2},{2,0},{1,3},{3,1},{4,6},{6,4},{5,7},{7,5},{8,10},{10,8},{9,1... | collective-permute-start | bytes 417800 | tf_op jit(solution)/shard_map/ppermute | solution.py:247
  8.1 0.0 collective-permute-start.1
  8.1 1.0 %collective-permute-start = (bf16[32,2176]{1,0:T(8,128)(2,1)S(1)}, bf16[32,2176]{1,0:T(8,128)(2,1)S(1)}, u32[]{:S(2)}, u32[]{:S(2)}) collective-permute-start(bf16[32,2176]{1,0:T(8,128)(2,1)S(1)} %pack_tokens.1.refs_0_), channel_id=1, source_target_pairs={{0,4},{4,8},{8,12},{12,0},{1,5},{5,9},{9,13},{13,1},{2,6},{6,10},{... | collective-permute-start | bytes 417800 | tf_op jit(solution)/shard_map/ppermute | solution.py:247
  9.2 0.0 collective-permute-start.7
  9.2 0.1 pad_add_fusion.first_ref.scalars
  9.2 5.2 %load_weights.2.refs_16_ = bf16[2048,3072]{1,0:T(8,128)(2,1)S(1)} custom-call(s32[4]{0:T(128)S(1)} %pad_add_fusion.first_ref.scalars, bf16[8,2048,384]{2,1,0:T(8,128)(2,1)} %refs_0_.2, bf16[8,2048,384]{2,1,0:T(8,128)(2,1)} %refs_1_.1), custom_call_target="tpu_custom_call" | custom-call | bytes 12582912 | tf_op jit(solution)/shard_map/load_weights/pallas_call | solution.py:84
  14.4 0.0 collective-permute-done.2.refs_3_
  14.4 0.6 collective-permute-start.10
  15.0 3.4 %load_weights.3.refs_17_ = bf16[1536,2048]{1,0:T(8,128)(2,1)S(1)} custom-call(s32[4]{0:T(128)S(1)} %pad_add_fusion.first_ref.scalars, bf16[8,384,2048]{2,1,0:T(8,128)(2,1)} %refs_0_.3), custom_call_target="tpu_custom_call" | custom-call | bytes 6291456 | tf_op jit(solution)/shard_map/load_weights/pallas_call | solution.py:84
  18.4 0.0 collective-permute-done.3.refs_4_
  18.4 0.6 collective-permute-start.6
  19.0 0.0 collective-permute-done.1.refs_2_
  19.1 0.0 collective-permute-start.11
  19.1 0.0 collective-permute-done.refs_1_
  19.1 1.5 %collective-permute-start.4 = (bf16[32,2176]{1,0:T(8,128)(2,1)S(1)}, bf16[32,2176]{1,0:T(8,128)(2,1)S(1)}, u32[]{:S(2)}, u32[]{:S(2)}) collective-permute-start(bf16[32,2176]{1,0:T(8,128)(2,1)S(1)} %collective-permute-done.refs_1_), channel_id=1, source_target_pairs={{0,2},{2,0},{1,3},{3,1},{4,6},{6,4},{5,7},{7,5},{8,10},{10,8},{9,1... | collective-permute-start | bytes 417800 | tf_op jit(solution)/shard_map/ppermute | solution.py:247
  20.6 0.0 collective-permute-done.7.refs_8_
  20.6 0.5 collective-permute-start.5
  21.2 0.0 collective-permute-done.11.refs_12_
  21.2 0.0 collective-permute-start.8
  21.2 0.0 collective-permute-done.10.refs_11_
  21.2 0.5 collective-permute-start.9
  21.7 3.4 %collective-permute-done.6.refs_7_ = bf16[32,2176]{1,0:T(8,128)(2,1)S(1)} collective-permute-done((bf16[32,2176]{1,0:T(8,128)(2,1)S(1)}, bf16[32,2176]{1,0:T(8,128)(2,1)S(1)}, u32[]{:S(2)}, u32[]{:S(2)}) %collective-permute-start.6) | collective-permute-done | bytes 139296 | tf_op jit(solution)/shard_map/ppermute | solution.py:247
  25.0 0.0 collective-permute-start.14
  25.0 3.0 %collective-permute-done.4.refs_5_ = bf16[32,2176]{1,0:T(8,128)(2,1)S(1)} collective-permute-done((bf16[32,2176]{1,0:T(8,128)(2,1)S(1)}, bf16[32,2176]{1,0:T(8,128)(2,1)S(1)}, u32[]{:S(2)}, u32[]{:S(2)}) %collective-permute-start.4) | collective-permute-done | bytes 139296 | tf_op jit(solution)/shard_map/ppermute | solution.py:247
  28.0 0.0 collective-permute-start.12
  28.0 2.0 %collective-permute-done.5.refs_6_ = bf16[32,2176]{1,0:T(8,128)(2,1)S(1)} collective-permute-done((bf16[32,2176]{1,0:T(8,128)(2,1)S(1)}, bf16[32,2176]{1,0:T(8,128)(2,1)S(1)}, u32[]{:S(2)}, u32[]{:S(2)}) %collective-permute-start.5) | collective-permute-done | bytes 139296 | tf_op jit(solution)/shard_map/ppermute | solution.py:247
  30.1 0.0 collective-permute-start.13
  30.1 0.0 collective-permute-done.8.refs_9_
  30.1 0.0 collective-permute-done.9.refs_10_
  30.1 0.0 collective-permute-done.14.refs_15_
  30.1 0.0 collective-permute-done.12.refs_13_
  30.1 1.3 %collective-permute-done.13.refs_14_ = bf16[32,2176]{1,0:T(8,128)(2,1)S(1)} collective-permute-done((bf16[32,2176]{1,0:T(8,128)(2,1)S(1)}, bf16[32,2176]{1,0:T(8,128)(2,1)S(1)}, u32[]{:S(2)}, u32[]{:S(2)}) %collective-permute-start.13) | collective-permute-done | bytes 139296 | tf_op jit(solution)/shard_map/ppermute | solution.py:247
  31.4 9.8 %routed_forward.1 = (bf16[256,2048]{1,0:T(8,128)(2,1)S(1)}, bf16[256,2048]{1,0:T(8,128)(2,1)S(1)}, bf16[4,256,1152]{2,1,0:T(8,128)(2,1)S(1)}, f32[2,128,1152]{2,1,0:T(8,128)S(1)}, bf16[2,128,1152]{2,1,0:T(8,128)(2,1)S(1)}) custom-call(s32[4]{0:T(128)S(1)} %pad_add_fusion.first_ref.scalars, bf16[32,2176]{1,0:T(8,128)(2,1)S(1)} %pack_tokens.1.refs_0_, ...), custom_call_target="tpu_custom_call" | custom-call | flops 8053063680 | bytes 8388608 | tf_op jit(solution)/shard_map/routed_forward/pallas_call | solution.py:148
  41.2 0.2 collective-permute-start.15
  41.5 1.9 %collective-permute-done.15.got_ref = bf16[2,128,1152]{2,1,0:T(8,128)(2,1)S(1)} collective-permute-done((bf16[2,128,1152]{2,1,0:T(8,128)(2,1)S(1)}, bf16[2,128,1152]{2,1,0:T(8,128)(2,1)S(1)}, u32[]{:S(2)}, u32[]{:S(2)}) %collective-permute-start.15) | collective-permute-done | bytes 589856 | tf_op jit(solution)/shard_map/ppermute | solution.py:247
  43.3 0.2 collective-permute-start.20
  43.5 0.1 sum_over_cores.1
  43.6 0.6 collective-permute-start.16
  44.2 7.5 %weight_grads.2 = (bf16[8,2048,384]{2,1,0:T(8,128)(2,1)}, bf16[8,2048,384]{2,1,0:T(8,128)(2,1)}, bf16[8,384,2048]{2,1,0:T(8,128)(2,1)}) custom-call(s32[4]{0:T(128)S(1)} %pad_add_fusion.first_ref.scalars, bf16[256,2048]{1,0:T(8,128)(2,1)S(1)} %get-tuple-element.54.x_ref, bf16[256,2048]{1,0:T(8,128)(2,1)S(1)} %get-tuple-element.55.og_ref, ...), custom_call_target="tpu_custom_call" | custom-call | flops 4831838208 | bytes 18874368 | tf_op jit(solution)/shard_map/weight_grads/pallas_call | solution.py:203
  51.7 1.2 %collective-permute-done.16.got_ref = bf16[128,1152]{1,0:T(8,128)(2,1)S(1)} collective-permute-done((bf16[128,1152]{1,0:T(8,128)(2,1)S(1)}, bf16[128,1152]{1,0:T(8,128)(2,1)S(1)}, u32[]{:S(2)}, u32[]{:S(2)}) %collective-permute-start.16) | collective-permute-done | bytes 294944 | tf_op jit(solution)/shard_map/ppermute | solution.py:247
  52.9 0.1 sum_over_tensor.1
  53.0 2.9 %collective-permute-start.17 = (bf16[32,1152]{1,0:T(8,128)(2,1)S(1)}, bf16[32,1152]{1,0:T(8,128)(2,1)S(1)}, u32[]{:S(2)}, u32[]{:S(2)}) collective-permute-start(bf16[32,1152]{1,0:T(8,128)(2,1)S(1)} %get-tuple-element.62), channel_id=1, source_target_pairs={{0,12},{4,0},{8,4},{12,8},{1,13},{5,1},{9,5},{13,9},{2,14},{6,2},{... | collective-permute-start | bytes 221192 | tf_op jit(solution)/shard_map/ppermute | solution.py:247
  55.9 1.1 %collective-permute-start.18 = (bf16[32,1152]{1,0:T(8,128)(2,1)S(1)}, bf16[32,1152]{1,0:T(8,128)(2,1)S(1)}, u32[]{:S(2)}, u32[]{:S(2)}) collective-permute-start(bf16[32,1152]{1,0:T(8,128)(2,1)S(1)} %get-tuple-element.63), channel_id=1, source_target_pairs={{0,8},{4,12},{8,0},{12,4},{1,9},{5,13},{9,1},{13,5},{2,10},{6,14},... | collective-permute-start | bytes 221192 | tf_op jit(solution)/shard_map/ppermute | solution.py:247
  57.0 0.0 copy-start
  57.0 0.0 collective-permute-start.19
  57.0 0.0 collective-permute-done.20.grads_ref
  57.0 7.0 %weight_grads.3 = (bf16[8,2048,384]{2,1,0:T(8,128)(2,1)}, bf16[8,2048,384]{2,1,0:T(8,128)(2,1)}, bf16[8,384,2048]{2,1,0:T(8,128)(2,1)}) custom-call(s32[1]{0:T(128)} %bitcast.4.first_ref, bf16[256,2048]{1,0:T(8,128)(2,1)S(1)} %get-tuple-element.54.x_ref, ...), custom_call_target="tpu_custom_call", output_to_operand_aliasing={{0}: (4, {}), {1}: (5, {}), {2}: (6, {})} | custom-call | flops 4831838208 | bytes 18874368 | tf_op jit(solution)/shard_map/weight_grads/pallas_call | solution.py:203
  64.0 0.0 collective-permute-done.17.refs_0_
  64.0 0.0 collective-permute-done.18.refs_1_
  64.0 0.0 collective-permute-done.19.refs_2_
  64.0 0.0 copy-done
  64.0 0.8 %sum_over_experts.1 = (bf16[32,1024]{1,0:T(8,128)(2,1)}, f32[8,32]{1,0:T(8,128)}) custom-call(s32[8,32]{1,0:T(8,128)S(1)} %bitcast.8, f32[32,1152]{1,0:T(8,128)S(1)} %get-tuple-element.61.own_ref, bf16[32,1152]{1,0:T(8,128)(2,1)S(1)} %collective-permute-done.17.refs_0_, bf16[32,1152]{1,0:T(8,128)(2,1)S(1)} %collective-permute-done.18.refs_1_, ...), custom_call_target="tpu_custom_call" | custom-call | tf_op jit(solution)/shard_map/sum_over_experts/pallas_call | solution.py:411
Async XLA Ops:
  1.5 12.9 %collective-permute-start.2 = (bf16[32,2176]{1,0:T(8,128)(2,1)S(1)}, bf16[32,2176]{1,0:T(8,128)(2,1)S(1)}, u32[]{:S(2)}, u32[]{:S(2)}) collective-permute-start(bf16[32,2176]{1,0:T(8,128)(2,1)S(1)} %pack_tokens.1.refs_0_), channel_id=1, source_target_pairs={{0,12},{4,0},{8,4},{12,8},{1,13},{5,1},{9,5},{13,9},{2,14},{6,2},{... | collective-permute-start | bytes 417800 | tf_op jit(solution)/shard_map/ppermute | solution.py:247
  6.6 11.8 %collective-permute-start.3 = (bf16[32,2176]{1,0:T(8,128)(2,1)S(1)}, bf16[32,2176]{1,0:T(8,128)(2,1)S(1)}, u32[]{:S(2)}, u32[]{:S(2)}) collective-permute-start(bf16[32,2176]{1,0:T(8,128)(2,1)S(1)} %pack_tokens.1.refs_0_), channel_id=1, source_target_pairs={{0,2},{2,0},{1,3},{3,1},{4,6},{6,4},{5,7},{7,5},{8,10},{10,8},{9,1... | collective-permute-start | bytes 417800 | tf_op jit(solution)/shard_map/ppermute | solution.py:247
  8.1 10.9 %collective-permute-start.1 = (bf16[32,2176]{1,0:T(8,128)(2,1)S(1)}, bf16[32,2176]{1,0:T(8,128)(2,1)S(1)}, u32[]{:S(2)}, u32[]{:S(2)}) collective-permute-start(bf16[32,2176]{1,0:T(8,128)(2,1)S(1)} %pack_tokens.1.refs_0_), channel_id=1, source_target_pairs={{0,8},{4,12},{8,0},{12,4},{1,9},{5,13},{9,1},{13,5},{2,10},{6,14},... | collective-permute-start | bytes 417800 | tf_op jit(solution)/shard_map/ppermute | solution.py:247
  8.1 10.9 %collective-permute-start = (bf16[32,2176]{1,0:T(8,128)(2,1)S(1)}, bf16[32,2176]{1,0:T(8,128)(2,1)S(1)}, u32[]{:S(2)}, u32[]{:S(2)}) collective-permute-start(bf16[32,2176]{1,0:T(8,128)(2,1)S(1)} %pack_tokens.1.refs_0_), channel_id=1, source_target_pairs={{0,4},{4,8},{8,12},{12,0},{1,5},{5,9},{9,13},{13,1},{2,6},{6,10},{... | collective-permute-start | bytes 417800 | tf_op jit(solution)/shard_map/ppermute | solution.py:247
  9.2 11.5 %collective-permute-start.7 = (bf16[32,2176]{1,0:T(8,128)(2,1)S(1)}, bf16[32,2176]{1,0:T(8,128)(2,1)S(1)}, u32[]{:S(2)}, u32[]{:S(2)}) collective-permute-start(bf16[32,2176]{1,0:T(8,128)(2,1)S(1)} %pack_tokens.1.refs_0_), channel_id=1, source_target_pairs={{0,1},{1,0},{2,3},{3,2},{4,5},{5,4},{6,7},{7,6},{8,9},{9,8},{10,11... | collective-permute-start | bytes 417800 | tf_op jit(solution)/shard_map/ppermute | solution.py:247
  14.4 6.7 %collective-permute-start.10 = (bf16[32,2176]{1,0:T(8,128)(2,1)S(1)}, bf16[32,2176]{1,0:T(8,128)(2,1)S(1)}, u32[]{:S(2)}, u32[]{:S(2)}) collective-permute-start(bf16[32,2176]{1,0:T(8,128)(2,1)S(1)} %collective-permute-done.2.refs_3_), channel_id=1, source_target_pairs={{0,1},{1,0},{2,3},{3,2},{4,5},{5,4},{6,7},{7,6},{8,9},{9,8},{10,11... | collective-permute-start | bytes 417800 | tf_op jit(solution)/shard_map/ppermute | solution.py:247
  18.4 6.6 %collective-permute-start.6 = (bf16[32,2176]{1,0:T(8,128)(2,1)S(1)}, bf16[32,2176]{1,0:T(8,128)(2,1)S(1)}, u32[]{:S(2)}, u32[]{:S(2)}) collective-permute-start(bf16[32,2176]{1,0:T(8,128)(2,1)S(1)} %collective-permute-done.2.refs_3_), channel_id=1, source_target_pairs={{0,2},{2,0},{1,3},{3,1},{4,6},{6,4},{5,7},{7,5},{8,10},{10,8},{9,1... | collective-permute-start | bytes 417800 | tf_op jit(solution)/shard_map/ppermute | solution.py:247
  19.1 2.1 %collective-permute-start.11 = (bf16[32,2176]{1,0:T(8,128)(2,1)S(1)}, bf16[32,2176]{1,0:T(8,128)(2,1)S(1)}, u32[]{:S(2)}, u32[]{:S(2)}) collective-permute-start(bf16[32,2176]{1,0:T(8,128)(2,1)S(1)} %collective-permute-done.3.refs_4_), channel_id=1, source_target_pairs={{0,1},{1,0},{2,3},{3,2},{4,5},{5,4},{6,7},{7,6},{8,9},{9,8},{10,11... | collective-permute-start | bytes 417800 | tf_op jit(solution)/shard_map/ppermute | solution.py:247
  19.1 8.9 %collective-permute-start.4 = (bf16[32,2176]{1,0:T(8,128)(2,1)S(1)}, bf16[32,2176]{1,0:T(8,128)(2,1)S(1)}, u32[]{:S(2)}, u32[]{:S(2)}) collective-permute-start(bf16[32,2176]{1,0:T(8,128)(2,1)S(1)} %collective-permute-done.refs_1_), channel_id=1, source_target_pairs={{0,2},{2,0},{1,3},{3,1},{4,6},{6,4},{5,7},{7,5},{8,10},{10,8},{9,1... | collective-permute-start | bytes 417800 | tf_op jit(solution)/shard_map/ppermute | solution.py:247
  20.6 9.5 %collective-permute-start.5 = (bf16[32,2176]{1,0:T(8,128)(2,1)S(1)}, bf16[32,2176]{1,0:T(8,128)(2,1)S(1)}, u32[]{:S(2)}, u32[]{:S(2)}) collective-permute-start(bf16[32,2176]{1,0:T(8,128)(2,1)S(1)} %collective-permute-done.1.refs_2_), channel_id=1, source_target_pairs={{0,2},{2,0},{1,3},{3,1},{4,6},{6,4},{5,7},{7,5},{8,10},{10,8},{9,1... | collective-permute-start | bytes 417800 | tf_op jit(solution)/shard_map/ppermute | solution.py:247
  21.2 8.9 %collective-permute-start.8 = (bf16[32,2176]{1,0:T(8,128)(2,1)S(1)}, bf16[32,2176]{1,0:T(8,128)(2,1)S(1)}, u32[]{:S(2)}, u32[]{:S(2)}) collective-permute-start(bf16[32,2176]{1,0:T(8,128)(2,1)S(1)} %collective-permute-done.refs_1_), channel_id=1, source_target_pairs={{0,1},{1,0},{2,3},{3,2},{4,5},{5,4},{6,7},{7,6},{8,9},{9,8},{10,11... | collective-permute-start | bytes 417800 | tf_op jit(solution)/shard_map/ppermute | solution.py:247
  21.2 8.9 %collective-permute-start.9 = (bf16[32,2176]{1,0:T(8,128)(2,1)S(1)}, bf16[32,2176]{1,0:T(8,128)(2,1)S(1)}, u32[]{:S(2)}, u32[]{:S(2)}) collective-permute-start(bf16[32,2176]{1,0:T(8,128)(2,1)S(1)} %collective-permute-done.1.refs_2_), channel_id=1, source_target_pairs={{0,1},{1,0},{2,3},{3,2},{4,5},{5,4},{6,7},{7,6},{8,9},{9,8},{10,11... | collective-permute-start | bytes 417800 | tf_op jit(solution)/shard_map/ppermute | solution.py:247
  25.0 5.0 %collective-permute-start.14 = (bf16[32,2176]{1,0:T(8,128)(2,1)S(1)}, bf16[32,2176]{1,0:T(8,128)(2,1)S(1)}, u32[]{:S(2)}, u32[]{:S(2)}) collective-permute-start(bf16[32,2176]{1,0:T(8,128)(2,1)S(1)} %collective-permute-done.6.refs_7_), channel_id=1, source_target_pairs={{0,1},{1,0},{2,3},{3,2},{4,5},{5,4},{6,7},{7,6},{8,9},{9,8},{10,11... | collective-permute-start | bytes 417800 | tf_op jit(solution)/shard_map/ppermute | solution.py:247
  28.0 2.1 %collective-permute-start.12 = (bf16[32,2176]{1,0:T(8,128)(2,1)S(1)}, bf16[32,2176]{1,0:T(8,128)(2,1)S(1)}, u32[]{:S(2)}, u32[]{:S(2)}) collective-permute-start(bf16[32,2176]{1,0:T(8,128)(2,1)S(1)} %collective-permute-done.4.refs_5_), channel_id=1, source_target_pairs={{0,1},{1,0},{2,3},{3,2},{4,5},{5,4},{6,7},{7,6},{8,9},{9,8},{10,11... | collective-permute-start | bytes 417800 | tf_op jit(solution)/shard_map/ppermute | solution.py:247
  30.1 1.4 %collective-permute-start.13 = (bf16[32,2176]{1,0:T(8,128)(2,1)S(1)}, bf16[32,2176]{1,0:T(8,128)(2,1)S(1)}, u32[]{:S(2)}, u32[]{:S(2)}) collective-permute-start(bf16[32,2176]{1,0:T(8,128)(2,1)S(1)} %collective-permute-done.5.refs_6_), channel_id=1, source_target_pairs={{0,1},{1,0},{2,3},{3,2},{4,5},{5,4},{6,7},{7,6},{8,9},{9,8},{10,11... | collective-permute-start | bytes 417800 | tf_op jit(solution)/shard_map/ppermute | solution.py:247
  41.2 2.1 %collective-permute-start.15 = (bf16[2,128,1152]{2,1,0:T(8,128)(2,1)S(1)}, bf16[2,128,1152]{2,1,0:T(8,128)(2,1)S(1)}, u32[]{:S(2)}, u32[]{:S(2)}) collective-permute-start(bf16[2,128,1152]{2,1,0:T(8,128)(2,1)S(1)} %get-tuple-element.49), channel_id=1, source_target_pairs={{0,1},{1,0},{2,3},{3,2},{4,5},{5,4},{6,7},{7,6},{8,9},{9,8},{10,11... | collective-permute-start | bytes 1769480 | tf_op jit(solution)/shard_map/ppermute | solution.py:247
  43.3 13.7 %collective-permute-start.20 = (bf16[4,256,1152]{2,1,0:T(8,128)(2,1)S(1)}, bf16[4,256,1152]{2,1,0:T(8,128)(2,1)S(1)}, u32[]{:S(2)}, u32[]{:S(2)}) collective-permute-start(bf16[4,256,1152]{2,1,0:T(8,128)(2,1)S(1)} %get-tuple-element.56.grads_ref), channel_id=1, source_target_pairs={{0,1},{1,0},{2,3},{3,2},{4,5},{5,4},{6,7},{7,6},{8,9},{9,8},{10,11... | collective-permute-start | bytes 7077896 | tf_op jit(solution)/shard_map/ppermute | solution.py:247
  43.6 9.3 %collective-permute-start.16 = (bf16[128,1152]{1,0:T(8,128)(2,1)S(1)}, bf16[128,1152]{1,0:T(8,128)(2,1)S(1)}, u32[]{:S(2)}, u32[]{:S(2)}) collective-permute-start(bf16[128,1152]{1,0:T(8,128)(2,1)S(1)} %get-tuple-element.53), channel_id=1, source_target_pairs={{0,2},{2,0},{1,3},{3,1},{4,6},{6,4},{5,7},{7,5},{8,10},{10,8},{9,1... | collective-permute-start | bytes 884744 | tf_op jit(solution)/shard_map/ppermute | solution.py:247
  53.0 11.0 %collective-permute-start.17 = (bf16[32,1152]{1,0:T(8,128)(2,1)S(1)}, bf16[32,1152]{1,0:T(8,128)(2,1)S(1)}, u32[]{:S(2)}, u32[]{:S(2)}) collective-permute-start(bf16[32,1152]{1,0:T(8,128)(2,1)S(1)} %get-tuple-element.62), channel_id=1, source_target_pairs={{0,12},{4,0},{8,4},{12,8},{1,13},{5,1},{9,5},{13,9},{2,14},{6,2},{... | collective-permute-start | bytes 221192 | tf_op jit(solution)/shard_map/ppermute | solution.py:247
  55.9 8.1 %collective-permute-start.18 = (bf16[32,1152]{1,0:T(8,128)(2,1)S(1)}, bf16[32,1152]{1,0:T(8,128)(2,1)S(1)}, u32[]{:S(2)}, u32[]{:S(2)}) collective-permute-start(bf16[32,1152]{1,0:T(8,128)(2,1)S(1)} %get-tuple-element.63), channel_id=1, source_target_pairs={{0,8},{4,12},{8,0},{12,4},{1,9},{5,13},{9,1},{13,5},{2,10},{6,14},... | collective-permute-start | bytes 221192 | tf_op jit(solution)/shard_map/ppermute | solution.py:247
  57.0 7.0 %copy-start = (s32[32,8]{0,1:T(8,128)S(1)}, s32[32,8]{0,1:T(8,128)}, u32[]{:S(2)}) copy-start(s32[32,8]{0,1:T(8,128)} %param.9) | copy-start | bytes 3076
  57.0 7.0 %collective-permute-start.19 = (bf16[32,1152]{1,0:T(8,128)(2,1)S(1)}, bf16[32,1152]{1,0:T(8,128)(2,1)S(1)}, u32[]{:S(2)}, u32[]{:S(2)}) collective-permute-start(bf16[32,1152]{1,0:T(8,128)(2,1)S(1)} %get-tuple-element.64), channel_id=1, source_target_pairs={{0,4},{4,8},{8,12},{12,0},{1,5},{5,9},{9,13},{13,1},{2,6},{6,10},{... | collective-permute-start | bytes 221192 | tf_op jit(solution)/shard_map/ppermute | solution.py:247

commit v4 on v3

--- a/solution.py
+++ b/solution.py
@@ -16,6 +16,7 @@
 ANY = pl.BlockSpec(memory_space=pl.ANY)
 SMEM = pl.BlockSpec(memory_space=pltpu.SMEM)
 VMEM = pl.BlockSpec(memory_space=pltpu.VMEM)
+LIGHT = pl.CostEstimate(flops=0, bytes_accessed=1024, transcendentals=0)
 
 
 def near(*arrays):
@@ -62,14 +63,33 @@
     )(*far(activations, out_grad, ids, probs))
 
 
-def load_kernel(by_row, first_ref, *refs):
-    *sources, target_ref, sem = refs
+def collect_kernel(*refs):
+    *shards, out_ref = refs
+    rows = shards[0].shape[0]
+    for i, shard in enumerate(shards):
+        out_ref[pl.ds(i * rows, rows), :] = shard[...]
+
+
+def collect(shards):
+    rows, columns = shards[0].shape
+    return pl.pallas_call(
+        collect_kernel,
+        in_specs=[VMEM] * len(shards),
+        out_specs=VMEM,
+        out_shape=pltpu.VMEM((len(shards) * rows, columns), shards[0].dtype),
+        compiler_params=pltpu.CompilerParams(vmem_limit_bytes=4 * MIB),
+        cost_estimate=LIGHT,
+        name="collect",
+    )(*near(*shards))
+
+
+def load_kernel(count, start, first_ref, wg_ref, wu_ref, *refs):
+    target_ref, sem = refs[-2:]
+    ff = wg_ref.shape[2]
     copies = []
-    count, step = len(sources), sources[0].shape[1 if by_row else 2]
-    for i in range(target_ref.shape[0 if by_row else 1] // (count * step)):
-        for j, source in enumerate(sources):
-            at = pl.ds((count * i + j) * step, step)
-            target = target_ref.at[at, :] if by_row else target_ref.at[:, at]
+    for i in range(start, start + count):
+        for j, source in enumerate((wg_ref, wu_ref)):
+            target = target_ref.at[:, pl.ds((2 * i + j) * ff, ff)]
             copies.append(pltpu.make_async_copy(source.at[first_ref[0] + i], target, sem))
     for copy in copies:
         copy.start()
@@ -77,38 +97,47 @@
         copy.wait()
 
 
-def load_weights(first, sources, count, by_row):
-    _, rows, columns = sources[0].shape
-    many = count * len(sources)
-    shape = (many * rows, columns) if by_row else (rows, many * columns)
+def load_weights(first, w_gate, w_up, own, count, into=None):
+    _, d, ff = w_gate.shape
+    kept = [] if into is None else near(into)
     return pl.pallas_call(
-        functools.partial(load_kernel, by_row),
-        in_specs=[SMEM] + [ANY] * len(sources),
+        functools.partial(load_kernel, own - count if kept else count, count if kept else 0),
+        in_specs=[SMEM, ANY, ANY] + [VMEM] * len(kept),
         out_specs=VMEM,
-        out_shape=pltpu.VMEM(shape, jnp.bfloat16),
+        out_shape=pltpu.VMEM((d, own * 2 * ff), jnp.bfloat16),
         scratch_shapes=[pltpu.SemaphoreType.DMA],
-        compiler_params=pltpu.CompilerParams(vmem_limit_bytes=4 * MIB),
-        cost_estimate=pl.CostEstimate(flops=0, bytes_accessed=2 * many * rows * columns, transcendentals=0),
+        input_output_aliases={3: 0} if kept else {},
+        compiler_params=pltpu.CompilerParams(vmem_limit_bytes=4 * MIB),
+        cost_estimate=LIGHT,
         name="load_weights",
-    )(first, *far(*sources))
+    )(first, *far(w_gate, w_up), *kept)
 
 
 def forward_kernel(places, n_tensor, top, own, scalars, *refs):
     count = len(places)
-    shards, (w_in, w_out) = refs[:count], refs[count : count + 2]
-    x_ref, og_ref, grads_ref, kept_ref, sent_ref, meta_ref = refs[count + 2 :]
+    shards, (w_in, wd_ref) = refs[:count], refs[count : count + 2]
+    x_ref, og_ref, grads_ref, kept_ref, sent_ref, meta_ref, w_out, sem = refs[count + 2 :]
     tensor = scalars[1]
     tokens, d = x_ref.shape
     wide, share = d // n_tensor, tokens // 2
-    ff = w_out.shape[0] // own
-    for shard, (row, side) in zip(shards, places):
-        rows = shard.shape[0]
-        columns = pl.ds(pl.multiple_of(lax.rem(tensor + side, n_tensor) * wide, wide), wide)
-        x_ref[pl.ds(row, rows), columns] = shard[:, :wide]
-        og_ref[pl.ds(row, rows), columns] = shard[:, wide : 2 * wide]
-        if side == 0:
-            meta_ref[pl.ds(row, rows), :] = shard[:, 2 * wide :].astype(jnp.float32)
+    ff = wd_ref.shape[1]
+    copies = [
+        pltpu.make_async_copy(wd_ref.at[scalars[0] + i], w_out.at[pl.ds(i * ff, ff), :], sem) for i in range(own)
+    ]
+    for copy in copies:
+        copy.start()
+    for shard, held in zip(shards, places):
+        rows = shard.shape[0] // len(held)
+        for i, (row, side) in enumerate(held):
+            at = pl.ds(i * rows, rows)
+            columns = pl.ds(pl.multiple_of(lax.rem(tensor + side, n_tensor) * wide, wide), wide)
+            x_ref[pl.ds(row, rows), columns] = shard[at, :wide]
+            og_ref[pl.ds(row, rows), columns] = shard[at, wide : 2 * wide]
+            if side == 0:
+                meta_ref[pl.ds(row, rows), :] = shard[at, 2 * wide :].astype(jnp.float32)
     pre = jnp.dot(x_ref[...], w_in[...], preferred_element_type=jnp.float32)
+    for copy in copies:
+        copy.wait()
     hidden_grads = lax.dot_general(og_ref[...], w_out[...], NT, preferred_element_type=jnp.float32)
     meta = meta_ref[...]
     lane = lax.broadcasted_iota(jnp.int32, meta.shape, 1)
@@ -142,12 +171,12 @@
         sent_ref[side, :, wide:] = inners[share:].astype(jnp.bfloat16)
 
 
-def forward(shards, places, scalars, weights, own, tokens, n_tensor, top):
-    d, ff = weights[1].shape[1], weights[1].shape[0] // own
+def forward(shards, places, scalars, w_in, w_down, own, tokens, n_tensor, top):
+    _, ff, d = w_down.shape
     sums = (n_tensor, tokens // 2, d // n_tensor + META)
     return pl.pallas_call(
         functools.partial(forward_kernel, places, n_tensor, top, own),
-        in_specs=[SMEM] + [VMEM] * (len(shards) + 2),
+        in_specs=[SMEM] + [VMEM] * (len(shards) + 1) + [ANY],
         out_specs=[VMEM] * 5,
         out_shape=[
             pltpu.VMEM((tokens, d), jnp.bfloat16),
@@ -156,13 +185,17 @@
             pltpu.VMEM(sums, jnp.float32),
             pltpu.VMEM(sums, jnp.bfloat16),
         ],
-        scratch_shapes=[pltpu.VMEM((tokens, META), jnp.float32)],
-        compiler_params=pltpu.CompilerParams(vmem_limit_bytes=16 * MIB),
+        scratch_shapes=[
+            pltpu.VMEM((tokens, META), jnp.float32),
+            pltpu.VMEM((own * ff, d), jnp.bfloat16),
+            pltpu.SemaphoreType.DMA,
+        ],
+        compiler_params=pltpu.CompilerParams(vmem_limit_bytes=22 * MIB),
         cost_estimate=pl.CostEstimate(
             flops=10 * own * tokens * d * ff, bytes_accessed=16 * tokens * d, transcendentals=0
         ),
         name="routed_forward",
-    )(scalars, *near(*shards, *weights))
+    )(scalars, *near(*shards, w_in), *far(w_down))
 
 
 def weight_kernel(swap, first_ref, x_ref, og_ref, grads_ref, *refs):
@@ -367,19 +400,18 @@
     ids = expert_ids.T
     packed = pack(activations, out_grad, ids, gate_probs.T)
     along = [packed] + [shift(packed, "expert", k) for k in range(1, n_expert)]
-    w_in = load_weights(scalars, (w_gate, w_up), own, False)
-    along[3], w_in, then = lax.optimization_barrier((along[3], w_in, scalars))
-    across = [shift(along[0], "tensor", 1), None, None, shift(along[3], "tensor", 1)]
-    w_out = load_weights(then, (w_down,), own, True)
-    along[1], along[2], w_out = lax.optimization_barrier((along[1], along[2], w_out))
-    across[1], across[2] = (shift(x, "tensor", 1) for x in along[1:3])
-    shards = along + across
+    across = {k: shift(along[k], "tensor", 1) for k in (0, 3, 1)}
+    along[2], across, then = lax.optimization_barrier((along[2], across, scalars))
+    across[2] = shift(along[2], "tensor", 1)
+    w_in = load_weights(then, w_gate, w_up, own, own // 2)
+    across[2], w_in, then = lax.optimization_barrier((across[2], w_in, scalars))
+    w_in = load_weights(then, w_gate, w_up, own, own // 2, w_in)
+    held = collect(along + [across[k] for k in range(n_expert)])
     places = [(k * rows, side) for side in range(n_tensor) for k in range(n_expert)]
-    for i in range(n_expert * n_tensor):
-        shards.append(shift(shards[i], "dp", 1))
-        places.append((tokens // 2 + places[i][0], places[i][1]))
+    places = [places, [(tokens // 2 + row, side) for row, side in places]]
+    shards = [held, shift(held, "dp", 1)]
     x, og, grads, kept, sent = forward(
-        shards, tuple(places), scalars, (w_in, w_out), own, tokens, n_tensor, top
+        shards, places, scalars, w_in, w_down, own, tokens, n_tensor, top
     )
     got = shift(sent, "dp", 1)
     got, grads = lax.optimization_barrier((got, grads))

time: 65 us -> 61.8 us (0.951)
  waiting for transfers between devices: 12.9 us -> 9.99 us
  Pallas kernels: 34.8 us -> 33.2 us
  starting transfers between devices: 16.4 us -> 17.7 us
    ppermute x21 -> x14, waiting for transfers between devices: 12.9 us -> 9.99 us  [shift(): return lax.ppermute(x, axis, [(i, (i + by) % count) for i in range(count)])]
    pallas_call x2 -> x3, Pallas kernels: 8.57 us -> 6.85 us  [the longest x2 6.77 us: load_weights(): pl.pallas_call(functools.partial(load_kernel, own - count if kept else co...]
    ppermute x21 -> x14, starting transfers between devices: 16.4 us -> 17.7 us  [shift(): return lax.ppermute(x, axis, [(i, (i + by) % count) for i in range(count)])]
  transfers between devices with their start and end apart: 21 -> 14, of which waited for: 6 -> 7; matrix products, arithmetic and copies ran while one was open for 0% -> 0% of each run, Pallas kernels for 36% -> 35%
where the time goes in v4:
time: 61.8 us; the launch traced here: 61.7 us
  Pallas kernels  33.2 us (54%)
  starting transfers between devices  17.7 us (29%)
  waiting for transfers between devices  9.99 us (16%)
  between operations  0.75 us (1%)
    ppermute x14, starting transfers between devices, shift(): return lax.ppermute(x, axis, [(i, (i + by) % count) for i in range(count)])  17.7 us
    pallas_call x2, Pallas kernels, weight_grads(): pl.pallas_call(functools.partial(weight_kernel, into is not None), in_spe...  14.5 us
    ppermute x14, waiting for transfers between devices, shift(): return lax.ppermute(x, axis, [(i, (i + by) % count) for i in range(count)])  9.99 us
    pallas_call x1, Pallas kernels, forward(): pl.pallas_call(functools.partial(forward_kernel, places, n_tensor, top, o...  9.91 us
    pallas_call x2, Pallas kernels, load_weights(): pl.pallas_call(functools.partial(load_kernel, own - count if kept else co...  6.77 us
  transfers between devices with their start and end apart: 14, of which 7 were waited for; matrix products, arithmetic and copies ran while one was open for 0% of the time, Pallas kernels for 35%

profile of v4, /device:TPU:0, one launch (start us, length us, event | category | flops | bytes accessed | tf_op | source)
XLA Modules:
  0.0 61.7 jit_solution(15628498139248724544)
XLA Ops:
  0.6 0.9 %pack_tokens.1.refs_0_ = bf16[32,2176]{1,0:T(8,128)(2,1)S(1)} custom-call(bf16[32,1024]{1,0:T(8,128)(2,1)} %act_hbm.1, bf16[32,1024]{1,0:T(8,128)(2,1)} %og_hbm.1, s32[8,32]{1,0:T(8,128)} %bitcast.7, bf16[8,32]{1,0:T(8,128)(2,1)} %bitcast.9), custom_call_target="tpu_custom_call" | custom-call | tf_op jit(solution)/shard_map/pack_tokens/pallas_call | solution.py:51
  1.5 5.1 %collective-permute-start.4 = (bf16[32,2176]{1,0:T(8,128)(2,1)S(1)}, bf16[32,2176]{1,0:T(8,128)(2,1)S(1)}, u32[]{:S(2)}, u32[]{:S(2)}) collective-permute-start(bf16[32,2176]{1,0:T(8,128)(2,1)S(1)} %pack_tokens.1.refs_0_), channel_id=1, source_target_pairs={{0,12},{4,0},{8,4},{12,8},{1,13},{5,1},{9,5},{13,9},{2,14},{6,2},{... | collective-permute-start | bytes 417800 | tf_op jit(solution)/shard_map/ppermute | solution.py:280
  6.6 0.0 collective-permute-start
  6.7 1.5 %collective-permute-start.2 = (bf16[32,2176]{1,0:T(8,128)(2,1)S(1)}, bf16[32,2176]{1,0:T(8,128)(2,1)S(1)}, u32[]{:S(2)}, u32[]{:S(2)}) collective-permute-start(bf16[32,2176]{1,0:T(8,128)(2,1)S(1)} %pack_tokens.1.refs_0_), channel_id=1, source_target_pairs={{0,2},{2,0},{1,3},{3,1},{4,6},{6,4},{5,7},{7,5},{8,10},{10,8},{9,1... | collective-permute-start | bytes 417800 | tf_op jit(solution)/shard_map/ppermute | solution.py:280
  8.1 1.0 %collective-permute-start.1 = (bf16[32,2176]{1,0:T(8,128)(2,1)S(1)}, bf16[32,2176]{1,0:T(8,128)(2,1)S(1)}, u32[]{:S(2)}, u32[]{:S(2)}) collective-permute-start(bf16[32,2176]{1,0:T(8,128)(2,1)S(1)} %pack_tokens.1.refs_0_), channel_id=1, source_target_pairs={{0,8},{4,12},{8,0},{12,4},{1,9},{5,13},{9,1},{13,5},{2,10},{6,14},... | collective-permute-start | bytes 417800 | tf_op jit(solution)/shard_map/ppermute | solution.py:280
  9.2 1.6 %collective-permute-done.4.refs_3_ = bf16[32,2176]{1,0:T(8,128)(2,1)S(1)} collective-permute-done((bf16[32,2176]{1,0:T(8,128)(2,1)S(1)}, bf16[32,2176]{1,0:T(8,128)(2,1)S(1)}, u32[]{:S(2)}, u32[]{:S(2)}) %collective-permute-start.4) | collective-permute-done | bytes 139296 | tf_op jit(solution)/shard_map/ppermute | solution.py:280
  10.7 1.5 %collective-permute-start.5 = (bf16[32,2176]{1,0:T(8,128)(2,1)S(1)}, bf16[32,2176]{1,0:T(8,128)(2,1)S(1)}, u32[]{:S(2)}, u32[]{:S(2)}) collective-permute-start(bf16[32,2176]{1,0:T(8,128)(2,1)S(1)} %collective-permute-done.4.refs_3_), channel_id=1, source_target_pairs={{0,2},{2,0},{1,3},{3,1},{4,6},{6,4},{5,7},{7,5},{8,10},{10,8},{9,1... | collective-permute-start | bytes 417800 | tf_op jit(solution)/shard_map/ppermute | solution.py:280
  12.2 2.9 %collective-permute-done.refs_1_ = bf16[32,2176]{1,0:T(8,128)(2,1)S(1)} collective-permute-done((bf16[32,2176]{1,0:T(8,128)(2,1)S(1)}, bf16[32,2176]{1,0:T(8,128)(2,1)S(1)}, u32[]{:S(2)}, u32[]{:S(2)}) %collective-permute-start) | collective-permute-done | bytes 139296 | tf_op jit(solution)/shard_map/ppermute | solution.py:280
  15.1 1.4 %collective-permute-start.3 = (bf16[32,2176]{1,0:T(8,128)(2,1)S(1)}, bf16[32,2176]{1,0:T(8,128)(2,1)S(1)}, u32[]{:S(2)}, u32[]{:S(2)}) collective-permute-start(bf16[32,2176]{1,0:T(8,128)(2,1)S(1)} %collective-permute-done.refs_1_), channel_id=1, source_target_pairs={{0,2},{2,0},{1,3},{3,1},{4,6},{6,4},{5,7},{7,5},{8,10},{10,8},{9,1... | collective-permute-start | bytes 417800 | tf_op jit(solution)/shard_map/ppermute | solution.py:280
  16.6 0.1 pad_add_fusion.first_ref.scalars
  16.7 0.0 collective-permute-done.2.refs_4_
  16.7 2.9 %collective-permute-done.1.refs_2_ = bf16[32,2176]{1,0:T(8,128)(2,1)S(1)} collective-permute-done((bf16[32,2176]{1,0:T(8,128)(2,1)S(1)}, bf16[32,2176]{1,0:T(8,128)(2,1)S(1)}, u32[]{:S(2)}, u32[]{:S(2)}) %collective-permute-start.1) | collective-permute-done | bytes 139296 | tf_op jit(solution)/shard_map/ppermute | solution.py:280
  19.5 0.0 collective-permute-done.5.refs_7_
  19.6 0.6 %collective-permute-done.3.refs_5_ = bf16[32,2176]{1,0:T(8,128)(2,1)S(1)} collective-permute-done((bf16[32,2176]{1,0:T(8,128)(2,1)S(1)}, bf16[32,2176]{1,0:T(8,128)(2,1)S(1)}, u32[]{:S(2)}, u32[]{:S(2)}) %collective-permute-start.3) | collective-permute-done | bytes 139296 | tf_op jit(solution)/shard_map/ppermute | solution.py:280
  20.2 1.4 %collective-permute-start.6 = (bf16[32,2176]{1,0:T(8,128)(2,1)S(1)}, bf16[32,2176]{1,0:T(8,128)(2,1)S(1)}, u32[]{:S(2)}, u32[]{:S(2)}) collective-permute-start(bf16[32,2176]{1,0:T(8,128)(2,1)S(1)} %collective-permute-done.1.refs_2_), channel_id=1, source_target_pairs={{0,2},{2,0},{1,3},{3,1},{4,6},{6,4},{5,7},{7,5},{8,10},{10,8},{9,1... | collective-permute-start | bytes 417800 | tf_op jit(solution)/shard_map/ppermute | solution.py:280
  21.6 3.4 %load_weights.2.refs_0_ = bf16[2048,3072]{1,0:T(8,128)(2,1)S(1)} custom-call(s32[4]{0:T(128)S(1)} %pad_add_fusion.first_ref.scalars, bf16[8,2048,384]{2,1,0:T(8,128)(2,1)} %wg_ref.3, bf16[8,2048,384]{2,1,0:T(8,128)(2,1)} %wu_ref.3), custom_call_target="tpu_custom_call" | custom-call | bytes 1024 | tf_op jit(solution)/shard_map/load_weights/pallas_call | solution.py:103
  25.0 0.2 collective-permute-done.6.refs_6_
  25.3 0.1 collect.1.refs_0_
  25.3 0.1 collective-permute-start.7
  25.4 3.4 %load_weights.3.refs_2_ = bf16[2048,3072]{1,0:T(8,128)(2,1)S(1)} custom-call(s32[4]{0:T(128)S(1)} %pad_add_fusion.first_ref.scalars, bf16[8,2048,384]{2,1,0:T(8,128)(2,1)} %wg_ref.3, bf16[8,2048,384]{2,1,0:T(8,128)(2,1)} %wu_ref.3, bf16[2048,3072]{1,0:T(8,128)(2,1)S(1)} %load_weights.2.refs_0_), custom_call_target="tpu_custom_call", output_to_operand_aliasing={{}: (3, {})} | custom-call | bytes 1024 | tf_op jit(solution)/shard_map/load_weights/pallas_call | solution.py:103
  28.8 0.0 collective-permute-done.7.refs_1_
  28.8 9.9 %routed_forward.1 = (bf16[256,2048]{1,0:T(8,128)(2,1)S(1)}, bf16[256,2048]{1,0:T(8,128)(2,1)S(1)}, bf16[4,256,1152]{2,1,0:T(8,128)(2,1)S(1)}, f32[2,128,1152]{2,1,0:T(8,128)S(1)}, bf16[2,128,1152]{2,1,0:T(8,128)(2,1)S(1)}) custom-call(s32[4]{0:T(128)S(1)} %pad_add_fusion.first_ref.scalars, bf16[256,2176]{1,0:T(8,128)(2,1)S(1)} %collect.1.refs_0_, ...), custom_call_target="tpu_custom_call" | custom-call | flops 8053063680 | bytes 8388608 | tf_op jit(solution)/shard_map/routed_forward/pallas_call | solution.py:177
  38.7 0.6 collective-permute-start.8
  39.3 1.6 %collective-permute-done.8.got_ref = bf16[2,128,1152]{2,1,0:T(8,128)(2,1)S(1)} collective-permute-done((bf16[2,128,1152]{2,1,0:T(8,128)(2,1)S(1)}, bf16[2,128,1152]{2,1,0:T(8,128)(2,1)S(1)}, u32[]{:S(2)}, u32[]{:S(2)}) %collective-permute-start.8) | collective-permute-done | bytes 589856 | tf_op jit(solution)/shard_map/ppermute | solution.py:280
  40.9 0.4 collective-permute-start.13
  41.3 0.1 sum_over_cores.1
  41.4 1.5 %collective-permute-start.9 = (bf16[128,1152]{1,0:T(8,128)(2,1)S(1)}, bf16[128,1152]{1,0:T(8,128)(2,1)S(1)}, u32[]{:S(2)}, u32[]{:S(2)}) collective-permute-start(bf16[128,1152]{1,0:T(8,128)(2,1)S(1)} %get-tuple-element.57), channel_id=1, source_target_pairs={{0,2},{2,0},{1,3},{3,1},{4,6},{6,4},{5,7},{7,5},{8,10},{10,8},{9,1... | collective-permute-start | bytes 884744 | tf_op jit(solution)/shard_map/ppermute | solution.py:280
  42.9 7.5 %weight_grads.2 = (bf16[8,2048,384]{2,1,0:T(8,128)(2,1)}, bf16[8,2048,384]{2,1,0:T(8,128)(2,1)}, bf16[8,384,2048]{2,1,0:T(8,128)(2,1)}) custom-call(s32[4]{0:T(128)S(1)} %pad_add_fusion.first_ref.scalars, bf16[256,2048]{1,0:T(8,128)(2,1)S(1)} %get-tuple-element.58.x_ref, bf16[256,2048]{1,0:T(8,128)(2,1)S(1)} %get-tuple-element.59.og_ref, ...), custom_call_target="tpu_custom_call" | custom-call | flops 4831838208 | bytes 18874368 | tf_op jit(solution)/shard_map/weight_grads/pallas_call | solution.py:236
  50.5 0.1 collective-permute-done.9.got_ref
  50.6 0.1 sum_over_tensor.1
  50.6 1.4 %collective-permute-start.10 = (bf16[32,1152]{1,0:T(8,128)(2,1)S(1)}, bf16[32,1152]{1,0:T(8,128)(2,1)S(1)}, u32[]{:S(2)}, u32[]{:S(2)}) collective-permute-start(bf16[32,1152]{1,0:T(8,128)(2,1)S(1)} %get-tuple-element.66), channel_id=1, source_target_pairs={{0,12},{4,0},{8,4},{12,8},{1,13},{5,1},{9,5},{13,9},{2,14},{6,2},{... | collective-permute-start | bytes 221192 | tf_op jit(solution)/shard_map/ppermute | solution.py:280
  52.0 1.8 %collective-permute-start.11 = (bf16[32,1152]{1,0:T(8,128)(2,1)S(1)}, bf16[32,1152]{1,0:T(8,128)(2,1)S(1)}, u32[]{:S(2)}, u32[]{:S(2)}) collective-permute-start(bf16[32,1152]{1,0:T(8,128)(2,1)S(1)} %get-tuple-element.67), channel_id=1, source_target_pairs={{0,8},{4,12},{8,0},{12,4},{1,9},{5,13},{9,1},{13,5},{2,10},{6,14},... | collective-permute-start | bytes 221192 | tf_op jit(solution)/shard_map/ppermute | solution.py:280
  53.8 0.0 copy-start
  53.8 0.0 collective-permute-start.12
  53.8 0.0 collective-permute-done.13.grads_ref
  53.8 7.0 %weight_grads.3 = (bf16[8,2048,384]{2,1,0:T(8,128)(2,1)}, bf16[8,2048,384]{2,1,0:T(8,128)(2,1)}, bf16[8,384,2048]{2,1,0:T(8,128)(2,1)}) custom-call(s32[1]{0:T(128)} %bitcast.4.first_ref, bf16[256,2048]{1,0:T(8,128)(2,1)S(1)} %get-tuple-element.58.x_ref, ...), custom_call_target="tpu_custom_call", output_to_operand_aliasing={{0}: (4, {}), {1}: (5, {}), {2}: (6, {})} | custom-call | flops 4831838208 | bytes 18874368 | tf_op jit(solution)/shard_map/weight_grads/pallas_call | solution.py:236
  60.8 0.0 collective-permute-done.10.refs_0_
  60.8 0.0 collective-permute-done.11.refs_1_
  60.8 0.0 collective-permute-done.12.refs_2_
  60.8 0.0 copy-done
  60.8 0.8 %sum_over_experts.1 = (bf16[32,1024]{1,0:T(8,128)(2,1)}, f32[8,32]{1,0:T(8,128)}) custom-call(s32[8,32]{1,0:T(8,128)S(1)} %bitcast.8, f32[32,1152]{1,0:T(8,128)S(1)} %get-tuple-element.65.own_ref, bf16[32,1152]{1,0:T(8,128)(2,1)S(1)} %collective-permute-done.10.refs_0_, bf16[32,1152]{1,0:T(8,128)(2,1)S(1)} %collective-permute-done.11.refs_1_, ...), custom_call_target="tpu_custom_call" | custom-call | tf_op jit(solution)/shard_map/sum_over_experts/pallas_call | solution.py:443
Async XLA Ops:
  1.5 9.2 %collective-permute-start.4 = (bf16[32,2176]{1,0:T(8,128)(2,1)S(1)}, bf16[32,2176]{1,0:T(8,128)(2,1)S(1)}, u32[]{:S(2)}, u32[]{:S(2)}) collective-permute-start(bf16[32,2176]{1,0:T(8,128)(2,1)S(1)} %pack_tokens.1.refs_0_), channel_id=1, source_target_pairs={{0,12},{4,0},{8,4},{12,8},{1,13},{5,1},{9,5},{13,9},{2,14},{6,2},{... | collective-permute-start | bytes 417800 | tf_op jit(solution)/shard_map/ppermute | solution.py:280
  6.6 8.5 %collective-permute-start = (bf16[32,2176]{1,0:T(8,128)(2,1)S(1)}, bf16[32,2176]{1,0:T(8,128)(2,1)S(1)}, u32[]{:S(2)}, u32[]{:S(2)}) collective-permute-start(bf16[32,2176]{1,0:T(8,128)(2,1)S(1)} %pack_tokens.1.refs_0_), channel_id=1, source_target_pairs={{0,4},{4,8},{8,12},{12,0},{1,5},{5,9},{9,13},{13,1},{2,6},{6,10},{... | collective-permute-start | bytes 417800 | tf_op jit(solution)/shard_map/ppermute | solution.py:280
  6.7 10.0 %collective-permute-start.2 = (bf16[32,2176]{1,0:T(8,128)(2,1)S(1)}, bf16[32,2176]{1,0:T(8,128)(2,1)S(1)}, u32[]{:S(2)}, u32[]{:S(2)}) collective-permute-start(bf16[32,2176]{1,0:T(8,128)(2,1)S(1)} %pack_tokens.1.refs_0_), channel_id=1, source_target_pairs={{0,2},{2,0},{1,3},{3,1},{4,6},{6,4},{5,7},{7,5},{8,10},{10,8},{9,1... | collective-permute-start | bytes 417800 | tf_op jit(solution)/shard_map/ppermute | solution.py:280
  8.1 11.4 %collective-permute-start.1 = (bf16[32,2176]{1,0:T(8,128)(2,1)S(1)}, bf16[32,2176]{1,0:T(8,128)(2,1)S(1)}, u32[]{:S(2)}, u32[]{:S(2)}) collective-permute-start(bf16[32,2176]{1,0:T(8,128)(2,1)S(1)} %pack_tokens.1.refs_0_), channel_id=1, source_target_pairs={{0,8},{4,12},{8,0},{12,4},{1,9},{5,13},{9,1},{13,5},{2,10},{6,14},... | collective-permute-start | bytes 417800 | tf_op jit(solution)/shard_map/ppermute | solution.py:280
  10.7 8.8 %collective-permute-start.5 = (bf16[32,2176]{1,0:T(8,128)(2,1)S(1)}, bf16[32,2176]{1,0:T(8,128)(2,1)S(1)}, u32[]{:S(2)}, u32[]{:S(2)}) collective-permute-start(bf16[32,2176]{1,0:T(8,128)(2,1)S(1)} %collective-permute-done.4.refs_3_), channel_id=1, source_target_pairs={{0,2},{2,0},{1,3},{3,1},{4,6},{6,4},{5,7},{7,5},{8,10},{10,8},{9,1... | collective-permute-start | bytes 417800 | tf_op jit(solution)/shard_map/ppermute | solution.py:280
  15.1 5.1 %collective-permute-start.3 = (bf16[32,2176]{1,0:T(8,128)(2,1)S(1)}, bf16[32,2176]{1,0:T(8,128)(2,1)S(1)}, u32[]{:S(2)}, u32[]{:S(2)}) collective-permute-start(bf16[32,2176]{1,0:T(8,128)(2,1)S(1)} %collective-permute-done.refs_1_), channel_id=1, source_target_pairs={{0,2},{2,0},{1,3},{3,1},{4,6},{6,4},{5,7},{7,5},{8,10},{10,8},{9,1... | collective-permute-start | bytes 417800 | tf_op jit(solution)/shard_map/ppermute | solution.py:280
  20.2 5.1 %collective-permute-start.6 = (bf16[32,2176]{1,0:T(8,128)(2,1)S(1)}, bf16[32,2176]{1,0:T(8,128)(2,1)S(1)}, u32[]{:S(2)}, u32[]{:S(2)}) collective-permute-start(bf16[32,2176]{1,0:T(8,128)(2,1)S(1)} %collective-permute-done.1.refs_2_), channel_id=1, source_target_pairs={{0,2},{2,0},{1,3},{3,1},{4,6},{6,4},{5,7},{7,5},{8,10},{10,8},{9,1... | collective-permute-start | bytes 417800 | tf_op jit(solution)/shard_map/ppermute | solution.py:280
  25.3 3.5 %collective-permute-start.7 = (bf16[256,2176]{1,0:T(8,128)(2,1)S(1)}, bf16[256,2176]{1,0:T(8,128)(2,1)S(1)}, u32[]{:S(2)}, u32[]{:S(2)}) collective-permute-start(bf16[256,2176]{1,0:T(8,128)(2,1)S(1)} %collect.1.refs_0_), channel_id=1, source_target_pairs={{0,1},{1,0},{2,3},{3,2},{4,5},{5,4},{6,7},{7,6},{8,9},{9,8},{10,11... | collective-permute-start | bytes 3342344 | tf_op jit(solution)/shard_map/ppermute | solution.py:280
  38.7 2.2 %collective-permute-start.8 = (bf16[2,128,1152]{2,1,0:T(8,128)(2,1)S(1)}, bf16[2,128,1152]{2,1,0:T(8,128)(2,1)S(1)}, u32[]{:S(2)}, u32[]{:S(2)}) collective-permute-start(bf16[2,128,1152]{2,1,0:T(8,128)(2,1)S(1)} %get-tuple-element.53), channel_id=1, source_target_pairs={{0,1},{1,0},{2,3},{3,2},{4,5},{5,4},{6,7},{7,6},{8,9},{9,8},{10,11... | collective-permute-start | bytes 1769480 | tf_op jit(solution)/shard_map/ppermute | solution.py:280
  40.9 12.9 %collective-permute-start.13 = (bf16[4,256,1152]{2,1,0:T(8,128)(2,1)S(1)}, bf16[4,256,1152]{2,1,0:T(8,128)(2,1)S(1)}, u32[]{:S(2)}, u32[]{:S(2)}) collective-permute-start(bf16[4,256,1152]{2,1,0:T(8,128)(2,1)S(1)} %get-tuple-element.60.grads_ref), channel_id=1, source_target_pairs={{0,1},{1,0},{2,3},{3,2},{4,5},{5,4},{6,7},{7,6},{8,9},{9,8},{10,11... | collective-permute-start | bytes 7077896 | tf_op jit(solution)/shard_map/ppermute | solution.py:280
  41.4 9.1 %collective-permute-start.9 = (bf16[128,1152]{1,0:T(8,128)(2,1)S(1)}, bf16[128,1152]{1,0:T(8,128)(2,1)S(1)}, u32[]{:S(2)}, u32[]{:S(2)}) collective-permute-start(bf16[128,1152]{1,0:T(8,128)(2,1)S(1)} %get-tuple-element.57), channel_id=1, source_target_pairs={{0,2},{2,0},{1,3},{3,1},{4,6},{6,4},{5,7},{7,5},{8,10},{10,8},{9,1... | collective-permute-start | bytes 884744 | tf_op jit(solution)/shard_map/ppermute | solution.py:280
  50.6 10.2 %collective-permute-start.10 = (bf16[32,1152]{1,0:T(8,128)(2,1)S(1)}, bf16[32,1152]{1,0:T(8,128)(2,1)S(1)}, u32[]{:S(2)}, u32[]{:S(2)}) collective-permute-start(bf16[32,1152]{1,0:T(8,128)(2,1)S(1)} %get-tuple-element.66), channel_id=1, source_target_pairs={{0,12},{4,0},{8,4},{12,8},{1,13},{5,1},{9,5},{13,9},{2,14},{6,2},{... | collective-permute-start | bytes 221192 | tf_op jit(solution)/shard_map/ppermute | solution.py:280
  52.0 8.8 %collective-permute-start.11 = (bf16[32,1152]{1,0:T(8,128)(2,1)S(1)}, bf16[32,1152]{1,0:T(8,128)(2,1)S(1)}, u32[]{:S(2)}, u32[]{:S(2)}) collective-permute-start(bf16[32,1152]{1,0:T(8,128)(2,1)S(1)} %get-tuple-element.67), channel_id=1, source_target_pairs={{0,8},{4,12},{8,0},{12,4},{1,9},{5,13},{9,1},{13,5},{2,10},{6,14},... | collective-permute-start | bytes 221192 | tf_op jit(solution)/shard_map/ppermute | solution.py:280
  53.8 7.0 %copy-start = (s32[32,8]{0,1:T(8,128)S(1)}, s32[32,8]{0,1:T(8,128)}, u32[]{:S(2)}) copy-start(s32[32,8]{0,1:T(8,128)} %param.9) | copy-start | bytes 3076
  53.8 7.0 %collective-permute-start.12 = (bf16[32,1152]{1,0:T(8,128)(2,1)S(1)}, bf16[32,1152]{1,0:T(8,128)(2,1)S(1)}, u32[]{:S(2)}, u32[]{:S(2)}) collective-permute-start(bf16[32,1152]{1,0:T(8,128)(2,1)S(1)} %get-tuple-element.68), channel_id=1, source_target_pairs={{0,4},{4,8},{8,12},{12,0},{1,5},{5,9},{9,13},{13,1},{2,6},{6,10},{... | collective-permute-start | bytes 221192 | tf_op jit(solution)/shard_map/ppermute | solution.py:280

commit v5 on v4

--- a/solution.py
+++ b/solution.py
@@ -83,13 +83,15 @@
     )(*near(*shards))
 
 
-def load_kernel(count, start, first_ref, wg_ref, wu_ref, *refs):
-    target_ref, sem = refs[-2:]
-    ff = wg_ref.shape[2]
+def load_kernel(by_row, start, count, first_ref, *refs):
+    *sources, target_ref, sem = refs
+    step = sources[0].shape[1 if by_row else 2]
+    many = len(sources)
     copies = []
     for i in range(start, start + count):
-        for j, source in enumerate((wg_ref, wu_ref)):
-            target = target_ref.at[:, pl.ds((2 * i + j) * ff, ff)]
+        for j, source in enumerate(sources):
+            at = pl.ds((many * i + j) * step, step)
+            target = target_ref.at[at, :] if by_row else target_ref.at[:, at]
             copies.append(pltpu.make_async_copy(source.at[first_ref[0] + i], target, sem))
     for copy in copies:
         copy.start()
@@ -97,26 +99,31 @@
         copy.wait()
 
 
-def load_weights(first, w_gate, w_up, own, count, into=None):
-    _, d, ff = w_gate.shape
+def load_kernel_into(by_row, start, count, first_ref, *refs):
+    *refs, _, target_ref, sem = refs
+    load_kernel(by_row, start, count, first_ref, *refs, target_ref, sem)
+
+
+def load_weights(first, sources, by_row, own, start, count, into=None):
+    _, rows, columns = sources[0].shape
+    many = own * len(sources)
+    shape = (many * rows, columns) if by_row else (rows, many * columns)
     kept = [] if into is None else near(into)
     return pl.pallas_call(
-        functools.partial(load_kernel, own - count if kept else count, count if kept else 0),
-        in_specs=[SMEM, ANY, ANY] + [VMEM] * len(kept),
+        functools.partial(load_kernel_into if kept else load_kernel, by_row, start, count),
+        in_specs=[SMEM] + [ANY] * len(sources) + [VMEM] * len(kept),
         out_specs=VMEM,
-        out_shape=pltpu.VMEM((d, own * 2 * ff), jnp.bfloat16),
+        out_shape=pltpu.VMEM(shape, jnp.bfloat16),
         scratch_shapes=[pltpu.SemaphoreType.DMA],
-        input_output_aliases={3: 0} if kept else {},
+        input_output_aliases={1 + len(sources): 0} if kept else {},
         compiler_params=pltpu.CompilerParams(vmem_limit_bytes=4 * MIB),
         cost_estimate=LIGHT,
         name="load_weights",
-    )(first, *far(w_gate, w_up), *kept)
-
-
-def forward_kernel(places, n_tensor, top, own, scalars, *refs):
-    count = len(places)
-    shards, (w_in, wd_ref) = refs[:count], refs[count : count + 2]
-    x_ref, og_ref, grads_ref, kept_ref, sent_ref, meta_ref, w_out, sem = refs[count + 2 :]
+    )(first, *far(*sources), *kept)
+
+
+def forward_kernel(places, n_tensor, top, own, scalars, own_ref, got_ref, w_in, wd_ref, *outs):
+    x_ref, og_ref, grads_ref, both_ref, inners_ref, kept_ref, sent_ref, w_out, sem = outs
     tensor = scalars[1]
     tokens, d = x_ref.shape
     wide, share = d // n_tensor, tokens // 2
@@ -126,20 +133,21 @@
     ]
     for copy in copies:
         copy.start()
-    for shard, held in zip(shards, places):
-        rows = shard.shape[0] // len(held)
-        for i, (row, side) in enumerate(held):
-            at = pl.ds(i * rows, rows)
+    rows = own_ref.shape[0] // len(places)
+    metas = []
+    for base, held in ((0, own_ref), (share, got_ref)):
+        for i, (row, side) in enumerate(places):
+            at, to = pl.ds(i * rows, rows), pl.ds(base + row, rows)
             columns = pl.ds(pl.multiple_of(lax.rem(tensor + side, n_tensor) * wide, wide), wide)
-            x_ref[pl.ds(row, rows), columns] = shard[at, :wide]
-            og_ref[pl.ds(row, rows), columns] = shard[at, wide : 2 * wide]
+            x_ref[to, columns] = held[at, :wide]
+            og_ref[to, columns] = held[at, wide : 2 * wide]
             if side == 0:
-                meta_ref[pl.ds(row, rows), :] = shard[at, 2 * wide :].astype(jnp.float32)
+                metas.append(held[at, 2 * wide :].astype(jnp.float32))
+    meta = jnp.concatenate(metas, axis=0)
     pre = jnp.dot(x_ref[...], w_in[...], preferred_element_type=jnp.float32)
     for copy in copies:
         copy.wait()
     hidden_grads = lax.dot_general(og_ref[...], w_out[...], NT, preferred_element_type=jnp.float32)
-    meta = meta_ref[...]
     lane = lax.broadcasted_iota(jnp.int32, meta.shape, 1)
     inners = jnp.zeros(meta.shape, jnp.float32)
     both = []
@@ -162,40 +170,65 @@
         grads_ref[i, :, 2 * ff :] = (prob * hidden).astype(jnp.bfloat16)
         both += [gate_grad, up_grad]
     both = jnp.concatenate(both, axis=1)
-    for side in range(n_tensor):
-        at = pl.ds(pl.multiple_of(lax.rem(tensor + side, n_tensor) * wide, wide), wide)
-        total = lax.dot_general(both, w_in[at, :], NT, preferred_element_type=jnp.float32)
-        kept_ref[side, :, :wide] = total[:share]
-        kept_ref[side, :, wide:] = inners[:share]
-        sent_ref[side, :, :wide] = total[share:].astype(jnp.bfloat16)
-        sent_ref[side, :, wide:] = inners[share:].astype(jnp.bfloat16)
-
-
-def forward(shards, places, scalars, w_in, w_down, own, tokens, n_tensor, top):
+    both_ref[...] = both
+    inners_ref[...] = inners
+    row_pass(tensor + 1, n_tensor, both, inners, w_in, kept_ref, sent_ref)
+
+
+def row_pass(side, n_tensor, both, inners, w_in, kept_ref, sent_ref):
+    wide = w_in.shape[0] // n_tensor
+    share = both.shape[0] // 2
+    at = pl.ds(pl.multiple_of(lax.rem(side, n_tensor) * wide, wide), wide)
+    total = lax.dot_general(both, w_in[at, :], NT, preferred_element_type=jnp.float32)
+    kept_ref[:, :wide] = total[:share]
+    kept_ref[:, wide:] = inners[:share]
+    sent_ref[:, :wide] = total[share:].astype(jnp.bfloat16)
+    sent_ref[:, wide:] = inners[share:].astype(jnp.bfloat16)
+
+
+def rows_kernel(n_tensor, scalars, both_ref, inners_ref, w_in, kept_ref, sent_ref):
+    row_pass(scalars[1], n_tensor, both_ref[...], inners_ref[...], w_in, kept_ref, sent_ref)
+
+
+def forward_call(kernel, name, scalars, inputs, out_shape, flops, distant=(), scratch=()):
+    return pl.pallas_call(
+        kernel,
+        in_specs=[SMEM] + [VMEM] * len(inputs) + [ANY] * len(distant),
+        out_specs=[VMEM] * len(out_shape),
+        out_shape=out_shape,
+        scratch_shapes=scratch,
+        compiler_params=pltpu.CompilerParams(vmem_limit_bytes=20 * MIB),
+        cost_estimate=pl.CostEstimate(flops=flops, bytes_accessed=1024, transcendentals=0),
+        name=name,
+    )(scalars, *near(*inputs), *far(*distant))
+
+
+def forward(held, got, places, scalars, w_in, w_down, own, n_tensor, top):
     _, ff, d = w_down.shape
-    sums = (n_tensor, tokens // 2, d // n_tensor + META)
-    return pl.pallas_call(
-        functools.partial(forward_kernel, places, n_tensor, top, own),
-        in_specs=[SMEM] + [VMEM] * (len(shards) + 1) + [ANY],
-        out_specs=[VMEM] * 5,
-        out_shape=[
-            pltpu.VMEM((tokens, d), jnp.bfloat16),
-            pltpu.VMEM((tokens, d), jnp.bfloat16),
-            pltpu.VMEM((own, tokens, 3 * ff), jnp.bfloat16),
-            pltpu.VMEM(sums, jnp.float32),
-            pltpu.VMEM(sums, jnp.bfloat16),
-        ],
-        scratch_shapes=[
-            pltpu.VMEM((tokens, META), jnp.float32),
-            pltpu.VMEM((own * ff, d), jnp.bfloat16),
-            pltpu.SemaphoreType.DMA,
-        ],
-        compiler_params=pltpu.CompilerParams(vmem_limit_bytes=22 * MIB),
-        cost_estimate=pl.CostEstimate(
-            flops=10 * own * tokens * d * ff, bytes_accessed=16 * tokens * d, transcendentals=0
-        ),
-        name="routed_forward",
-    )(scalars, *near(*shards, w_in), *far(w_down))
+    share = held.shape[0] // n_tensor
+    tokens = 2 * share
+    sums = (share, d // n_tensor + META)
+    shapes = [
+        pltpu.VMEM((tokens, d), jnp.bfloat16),
+        pltpu.VMEM((tokens, d), jnp.bfloat16),
+        pltpu.VMEM((own, tokens, 3 * ff), jnp.bfloat16),
+        pltpu.VMEM((tokens, own * 2 * ff), jnp.bfloat16),
+        pltpu.VMEM((tokens, META), jnp.float32),
+        pltpu.VMEM(sums, jnp.float32),
+        pltpu.VMEM(sums, jnp.bfloat16),
+    ]
+    kernel = functools.partial(forward_kernel, places, n_tensor, top, own)
+    scratch = [pltpu.VMEM((own * ff, d), jnp.bfloat16), pltpu.SemaphoreType.DMA]
+    flops = 8 * own * tokens * d * ff
+    return forward_call(kernel, "routed_forward", scalars, [held, got, w_in], shapes, flops, [w_down], scratch)
+
+
+def row_sums(scalars, both, inners, w_in, n_tensor):
+    tokens, d = both.shape[0], w_in.shape[0]
+    sums = (tokens // 2, d // n_tensor + META)
+    shapes = [pltpu.VMEM(sums, jnp.float32), pltpu.VMEM(sums, jnp.bfloat16)]
+    kernel = functools.partial(rows_kernel, n_tensor)
+    return forward_call(kernel, "row_sums", scalars, [both, inners, w_in], shapes, 2 * tokens * d * w_in.shape[1])
 
 
 def weight_kernel(swap, first_ref, x_ref, og_ref, grads_ref, *refs):
@@ -248,16 +281,16 @@
     )(first, *near(x, og, grads), *kept)
 
 
-def dp_sum_kernel(kept_ref, got_ref, here_ref, there_ref):
-    here_ref[...] = kept_ref[0] + got_ref[0].astype(jnp.float32)
-    there_ref[...] = (kept_ref[1] + got_ref[1].astype(jnp.float32)).astype(jnp.bfloat16)
-
-
-def tensor_sum_kernel(here_ref, got_ref, own_ref, *out_refs):
+def dp_sum_kernel(kept_ref, got_ref, there_ref):
+    there_ref[...] = (kept_ref[...] + got_ref[...].astype(jnp.float32)).astype(jnp.bfloat16)
+
+
+def tensor_sum_kernel(kept_ref, core_ref, got_ref, own_ref, *out_refs):
     rows = own_ref.shape[0]
     for block, target in enumerate((own_ref, *out_refs)):
         at = pl.ds(block * rows, rows)
-        target[...] = (here_ref[at, :] + got_ref[at, :].astype(jnp.float32)).astype(target.dtype)
+        total = kept_ref[at, :] + core_ref[at, :].astype(jnp.float32) + got_ref[at, :].astype(jnp.float32)
+        target[...] = total.astype(target.dtype)
 
 
 def finish_kernel(top, ids_ref, own_ref, *refs):
@@ -401,42 +434,44 @@
     packed = pack(activations, out_grad, ids, gate_probs.T)
     along = [packed] + [shift(packed, "expert", k) for k in range(1, n_expert)]
     across = {k: shift(along[k], "tensor", 1) for k in (0, 3, 1)}
-    along[2], across, then = lax.optimization_barrier((along[2], across, scalars))
+    along[2], across[0], across[3], then = lax.optimization_barrier((along[2], across[0], across[3], scalars))
     across[2] = shift(along[2], "tensor", 1)
-    w_in = load_weights(then, w_gate, w_up, own, own // 2)
-    across[2], w_in, then = lax.optimization_barrier((across[2], w_in, scalars))
-    w_in = load_weights(then, w_gate, w_up, own, own // 2, w_in)
+    w_in = load_weights(then, (w_gate, w_up), False, own, 0, own // 2)
+    across[1], across[2], w_in, then = lax.optimization_barrier((across[1], across[2], w_in, scalars))
+    w_in = load_weights(then, (w_gate, w_up), False, own, own // 2, own - own // 2, w_in)
     held = collect(along + [across[k] for k in range(n_expert)])
     places = [(k * rows, side) for side in range(n_tensor) for k in range(n_expert)]
-    places = [places, [(tokens // 2 + row, side) for row, side in places]]
-    shards = [held, shift(held, "dp", 1)]
-    x, og, grads, kept, sent = forward(
-        shards, places, scalars, w_in, w_down, own, tokens, n_tensor, top
+    swapped = shift(held, "dp", 1)
+    x, og, grads, both, inners, kept, sent = forward(
+        held, swapped, places, scalars, w_in, w_down, own, n_tensor, top
     )
     got = shift(sent, "dp", 1)
-    got, grads = lax.optimization_barrier((got, grads))
-    got_grads = shift(grads, "dp", 1)
+    kept_here, sent_here = row_sums(scalars, both, inners, w_in, n_tensor)
+    got, sent_here, grads = lax.optimization_barrier((got, sent_here, grads))
     half = (tokens // 2, wide + META)
-    here, there = pl.pallas_call(
+    there = pl.pallas_call(
         dp_sum_kernel,
         in_specs=[VMEM] * 2,
-        out_specs=[VMEM] * 2,
-        out_shape=[pltpu.VMEM(half, jnp.float32), pltpu.VMEM(half, jnp.bfloat16)],
+        out_specs=VMEM,
+        out_shape=pltpu.VMEM(half, jnp.bfloat16),
         compiler_params=pltpu.CompilerParams(vmem_limit_bytes=4 * MIB),
+        cost_estimate=LIGHT,
         name="sum_over_cores",
-    )(kept, *near(got))
+    )(*near(kept, got))
     crossed = shift(there, "tensor", 1)
+    got_here = shift(sent_here, "dp", 1)
+    got_grads = shift(grads, "dp", 1)
     outputs = weight_grads(scalars, x, og, grads, local_count)
-    crossed, outputs = lax.optimization_barrier((crossed, outputs))
+    crossed, got_here, outputs = lax.optimization_barrier((crossed, got_here, outputs))
     piece = (rows, wide + META)
     pieces = pl.pallas_call(
         tensor_sum_kernel,
-        in_specs=[VMEM] * 2,
+        in_specs=[VMEM] * 3,
         out_specs=[VMEM] * n_expert,
         out_shape=[pltpu.VMEM(piece, jnp.float32)] + [pltpu.VMEM(piece, jnp.bfloat16)] * (n_expert - 1),
         compiler_params=pltpu.CompilerParams(vmem_limit_bytes=4 * MIB),
         name="sum_over_tensor",
-    )(here, *near(crossed))
+    )(*near(kept_here, got_here, crossed))
     received = [shift(pieces[k], "expert", -k) for k in range(1, n_expert)]
     outputs = weight_grads(scalars[3:], x, og, got_grads, local_count, outputs)
     received, outputs = lax.optimization_barrier((received, outputs))

time: 61.8 us -> 59.8 us (0.968)
  starting transfers between devices: 17.7 us -> 14.8 us
    ppermute x14 -> x15, starting transfers between devices: 17.7 us -> 14.8 us  [shift(): return lax.ppermute(x, axis, [(i, (i + by) % count) for i in range(count)])]
    pallas_call x5 -> x6, Pallas kernels: 16.9 us -> 17.6 us  [the longest x2 10.6 us: forward_call(): pl.pallas_call(kernel, in_specs=[SMEM] + [VMEM] * len(inputs) + [ANY] * l...]
    ppermute x14 -> x15, waiting for transfers between devices: 9.99 us -> 10.1 us  [shift(): return lax.ppermute(x, axis, [(i, (i + by) % count) for i in range(count)])]
  transfers between devices with their start and end apart: 14 -> 15, of which waited for: 7 -> 5; matrix products, arithmetic and copies ran while one was open for 0% -> 0% of each run, Pallas kernels for 35% -> 40%
where the time goes in v5:
time: 59.8 us; the launch traced here: 59.6 us
  Pallas kernels  33.8 us (57%)
  starting transfers between devices  14.8 us (25%)
  waiting for transfers between devices  10.1 us (17%)
  between operations  0.75 us (1%)
    ppermute x15, starting transfers between devices, shift(): return lax.ppermute(x, axis, [(i, (i + by) % count) for i in range(count)])  14.8 us
    pallas_call x2, Pallas kernels, weight_grads(): pl.pallas_call(functools.partial(weight_kernel, into is not None), in_spe...  14.5 us
    pallas_call x2, Pallas kernels, forward_call(): pl.pallas_call(kernel, in_specs=[SMEM] + [VMEM] * len(inputs) + [ANY] * l...  10.6 us
    ppermute x15, waiting for transfers between devices, shift(): return lax.ppermute(x, axis, [(i, (i + by) % count) for i in range(count)])  10.1 us
    pallas_call x2, Pallas kernels, load_weights(): pl.pallas_call(functools.partial(load_kernel_into if kept else load_kerne...  6.77 us
  transfers between devices with their start and end apart: 15, of which 5 were waited for; matrix products, arithmetic and copies ran while one was open for 0% of the time, Pallas kernels for 40%

profile of v5, /device:TPU:0, one launch (start us, length us, event | category | flops | bytes accessed | tf_op | source)
XLA Modules:
  0.0 59.6 jit_solution(468453145173380395)
XLA Ops:
  0.6 0.9 %pack_tokens.1.refs_0_ = bf16[32,2176]{1,0:T(8,128)(2,1)S(1)} custom-call(bf16[32,1024]{1,0:T(8,128)(2,1)} %act_hbm.1, bf16[32,1024]{1,0:T(8,128)(2,1)} %og_hbm.1, s32[8,32]{1,0:T(8,128)} %bitcast.7, bf16[8,32]{1,0:T(8,128)(2,1)} %bitcast.9), custom_call_target="tpu_custom_call" | custom-call | tf_op jit(solution)/shard_map/pack_tokens/pallas_call | solution.py:51
  1.5 5.1 %collective-permute-start.3 = (bf16[32,2176]{1,0:T(8,128)(2,1)S(1)}, bf16[32,2176]{1,0:T(8,128)(2,1)S(1)}, u32[]{:S(2)}, u32[]{:S(2)}) collective-permute-start(bf16[32,2176]{1,0:T(8,128)(2,1)S(1)} %pack_tokens.1.refs_0_), channel_id=1, source_target_pairs={{0,12},{4,0},{8,4},{12,8},{1,13},{5,1},{9,5},{13,9},{2,14},{6,2},{... | collective-permute-start | bytes 417800 | tf_op jit(solution)/shard_map/ppermute | solution.py:313
  6.6 0.0 collective-permute-start
  6.7 1.5 %collective-permute-start.2 = (bf16[32,2176]{1,0:T(8,128)(2,1)S(1)}, bf16[32,2176]{1,0:T(8,128)(2,1)S(1)}, u32[]{:S(2)}, u32[]{:S(2)}) collective-permute-start(bf16[32,2176]{1,0:T(8,128)(2,1)S(1)} %pack_tokens.1.refs_0_), channel_id=1, source_target_pairs={{0,2},{2,0},{1,3},{3,1},{4,6},{6,4},{5,7},{7,5},{8,10},{10,8},{9,1... | collective-permute-start | bytes 417800 | tf_op jit(solution)/shard_map/ppermute | solution.py:313
  8.1 1.0 %collective-permute-start.1 = (bf16[32,2176]{1,0:T(8,128)(2,1)S(1)}, bf16[32,2176]{1,0:T(8,128)(2,1)S(1)}, u32[]{:S(2)}, u32[]{:S(2)}) collective-permute-start(bf16[32,2176]{1,0:T(8,128)(2,1)S(1)} %pack_tokens.1.refs_0_), channel_id=1, source_target_pairs={{0,8},{4,12},{8,0},{12,4},{1,9},{5,13},{9,1},{13,5},{2,10},{6,14},... | collective-permute-start | bytes 417800 | tf_op jit(solution)/shard_map/ppermute | solution.py:313
  9.2 1.6 %collective-permute-done.3.refs_3_ = bf16[32,2176]{1,0:T(8,128)(2,1)S(1)} collective-permute-done((bf16[32,2176]{1,0:T(8,128)(2,1)S(1)}, bf16[32,2176]{1,0:T(8,128)(2,1)S(1)}, u32[]{:S(2)}, u32[]{:S(2)}) %collective-permute-start.3) | collective-permute-done | bytes 139296 | tf_op jit(solution)/shard_map/ppermute | solution.py:313
  10.7 1.5 %collective-permute-start.4 = (bf16[32,2176]{1,0:T(8,128)(2,1)S(1)}, bf16[32,2176]{1,0:T(8,128)(2,1)S(1)}, u32[]{:S(2)}, u32[]{:S(2)}) collective-permute-start(bf16[32,2176]{1,0:T(8,128)(2,1)S(1)} %collective-permute-done.3.refs_3_), channel_id=1, source_target_pairs={{0,2},{2,0},{1,3},{3,1},{4,6},{6,4},{5,7},{7,5},{8,10},{10,8},{9,1... | collective-permute-start | bytes 417800 | tf_op jit(solution)/shard_map/ppermute | solution.py:313
  12.2 0.1 pad_add_fusion.first_ref.scalars
  12.3 2.8 %collective-permute-done.refs_1_ = bf16[32,2176]{1,0:T(8,128)(2,1)S(1)} collective-permute-done((bf16[32,2176]{1,0:T(8,128)(2,1)S(1)}, bf16[32,2176]{1,0:T(8,128)(2,1)S(1)}, u32[]{:S(2)}, u32[]{:S(2)}) %collective-permute-start) | collective-permute-done | bytes 139296 | tf_op jit(solution)/shard_map/ppermute | solution.py:313
  15.1 1.4 %collective-permute-start.5 = (bf16[32,2176]{1,0:T(8,128)(2,1)S(1)}, bf16[32,2176]{1,0:T(8,128)(2,1)S(1)}, u32[]{:S(2)}, u32[]{:S(2)}) collective-permute-start(bf16[32,2176]{1,0:T(8,128)(2,1)S(1)} %collective-permute-done.refs_1_), channel_id=1, source_target_pairs={{0,2},{2,0},{1,3},{3,1},{4,6},{6,4},{5,7},{7,5},{8,10},{10,8},{9,1... | collective-permute-start | bytes 417800 | tf_op jit(solution)/shard_map/ppermute | solution.py:313
  16.6 0.0 collective-permute-done.2.refs_4_
  16.6 3.0 %collective-permute-done.1.refs_2_ = bf16[32,2176]{1,0:T(8,128)(2,1)S(1)} collective-permute-done((bf16[32,2176]{1,0:T(8,128)(2,1)S(1)}, bf16[32,2176]{1,0:T(8,128)(2,1)S(1)}, u32[]{:S(2)}, u32[]{:S(2)}) %collective-permute-start.1) | collective-permute-done | bytes 139296 | tf_op jit(solution)/shard_map/ppermute | solution.py:313
  19.5 0.0 collective-permute-done.4.refs_7_
  19.6 0.9 %collective-permute-start.6 = (bf16[32,2176]{1,0:T(8,128)(2,1)S(1)}, bf16[32,2176]{1,0:T(8,128)(2,1)S(1)}, u32[]{:S(2)}, u32[]{:S(2)}) collective-permute-start(bf16[32,2176]{1,0:T(8,128)(2,1)S(1)} %collective-permute-done.1.refs_2_), channel_id=1, source_target_pairs={{0,2},{2,0},{1,3},{3,1},{4,6},{6,4},{5,7},{7,5},{8,10},{10,8},{9,1... | collective-permute-start | bytes 417800 | tf_op jit(solution)/shard_map/ppermute | solution.py:313
  20.4 3.4 %load_weights.2.refs_2_ = bf16[2048,3072]{1,0:T(8,128)(2,1)S(1)} custom-call(s32[4]{0:T(128)S(1)} %pad_add_fusion.first_ref.scalars, bf16[8,2048,384]{2,1,0:T(8,128)(2,1)} %refs_0_.3, bf16[8,2048,384]{2,1,0:T(8,128)(2,1)} %refs_1_.3), custom_call_target="tpu_custom_call" | custom-call | bytes 1024 | tf_op jit(solution)/shard_map/load_weights/pallas_call | solution.py:112
  23.8 0.0 collective-permute-done.5.refs_5_
  23.8 1.3 %collective-permute-done.6.refs_6_ = bf16[32,2176]{1,0:T(8,128)(2,1)S(1)} collective-permute-done((bf16[32,2176]{1,0:T(8,128)(2,1)S(1)}, bf16[32,2176]{1,0:T(8,128)(2,1)S(1)}, u32[]{:S(2)}, u32[]{:S(2)}) %collective-permute-start.6) | collective-permute-done | bytes 139296 | tf_op jit(solution)/shard_map/ppermute | solution.py:313
  25.1 0.1 collect.1.own_ref
  25.2 0.1 collective-permute-start.7
  25.3 3.4 %load_weights.3.w_in = bf16[2048,3072]{1,0:T(8,128)(2,1)S(1)} custom-call(s32[4]{0:T(128)S(1)} %pad_add_fusion.first_ref.scalars, bf16[8,2048,384]{2,1,0:T(8,128)(2,1)} %refs_0_.3, bf16[8,2048,384]{2,1,0:T(8,128)(2,1)} %refs_1_.3, bf16[2048,3072]{1,0:T(8,128)(2,1)S(1)} %load_weights.2.refs_2_), custom_call_target="tpu_custom_call", output_to_operand_aliasing={{}: (3, {})} | custom-call | bytes 1024 | tf_op jit(solution)/shard_map/load_weights/pallas_call | solution.py:112
  28.7 0.0 collective-permute-done.7.got_ref
  28.7 8.3 %routed_forward.1 = (bf16[256,2048]{1,0:T(8,128)(2,1)S(1)}, bf16[256,2048]{1,0:T(8,128)(2,1)S(1)}, bf16[4,256,1152]{2,1,0:T(8,128)(2,1)S(1)}, bf16[256,3072]{1,0...) custom-call(s32[4]{0:T(128)S(1)} %pad_add_fusion.first_ref.scalars, ...), custom_call_target="tpu_custom_call" | custom-call | flops 6442450944 | bytes 1024 | tf_op jit(solution)/shard_map/routed_forward/pallas_call | solution.py:194
  37.0 0.6 collective-permute-start.8
  37.6 2.4 %row_sums.1 = (f32[128,1152]{1,0:T(8,128)S(1)}, bf16[128,1152]{1,0:T(8,128)(2,1)S(1)}) custom-call(s32[4]{0:T(128)S(1)} %pad_add_fusion.first_ref.scalars, bf16[256,3072]{1,0:T(8,128)(2,1)S(1)} %get-tuple-element.56.both_ref, f32[256,128]{1,0:T(8,128)S(1)} %get-tuple-element.57.inners_ref, bf16[2048,3072]{1,0:T(8,128)(2,1)S(1)} %load_weights.3.w_in), custom_call_target="tpu_custom_call" | custom-call | flops 3221225472 | bytes 1024 | tf_op jit(solution)/shard_map/row_sums/pallas_call | solution.py:194
  39.9 0.0 collective-permute-done.8.got_ref
  39.9 0.1 collective-permute-start.14
  40.0 0.1 sum_over_cores.1
  40.1 0.4 collective-permute-start.9
  40.5 0.3 collective-permute-start.10
  40.7 7.5 %weight_grads.2 = (bf16[8,2048,384]{2,1,0:T(8,128)(2,1)}, bf16[8,2048,384]{2,1,0:T(8,128)(2,1)}, bf16[8,384,2048]{2,1,0:T(8,128)(2,1)}) custom-call(s32[4]{0:T(128)S(1)} %pad_add_fusion.first_ref.scalars, bf16[256,2048]{1,0:T(8,128)(2,1)S(1)} %get-tuple-element.65.x_ref, bf16[256,2048]{1,0:T(8,128)(2,1)S(1)} %get-tuple-element.66.og_ref, ...), custom_call_target="tpu_custom_call" | custom-call | flops 4831838208 | bytes 18874368 | tf_op jit(solution)/shard_map/weight_grads/pallas_call | solution.py:269
  48.2 1.3 %collective-permute-done.9.got_ref = bf16[128,1152]{1,0:T(8,128)(2,1)S(1)} collective-permute-done((bf16[128,1152]{1,0:T(8,128)(2,1)S(1)}, bf16[128,1152]{1,0:T(8,128)(2,1)S(1)}, u32[]{:S(2)}, u32[]{:S(2)}) %collective-permute-start.9) | collective-permute-done | bytes 294944 | tf_op jit(solution)/shard_map/ppermute | solution.py:313
  49.6 0.0 collective-permute-done.10.core_ref
  49.6 0.1 sum_over_tensor.1
  49.6 1.0 %collective-permute-start.11 = (bf16[32,1152]{1,0:T(8,128)(2,1)S(1)}, bf16[32,1152]{1,0:T(8,128)(2,1)S(1)}, u32[]{:S(2)}, u32[]{:S(2)}) collective-permute-start(bf16[32,1152]{1,0:T(8,128)(2,1)S(1)} %get-tuple-element.74), channel_id=1, source_target_pairs={{0,12},{4,0},{8,4},{12,8},{1,13},{5,1},{9,5},{13,9},{2,14},{6,2},{... | collective-permute-start | bytes 221192 | tf_op jit(solution)/shard_map/ppermute | solution.py:313
  50.7 0.0 collective-permute-start.12
  50.7 0.0 copy-start
  50.7 1.0 %collective-permute-start.13 = (bf16[32,1152]{1,0:T(8,128)(2,1)S(1)}, bf16[32,1152]{1,0:T(8,128)(2,1)S(1)}, u32[]{:S(2)}, u32[]{:S(2)}) collective-permute-start(bf16[32,1152]{1,0:T(8,128)(2,1)S(1)} %get-tuple-element.76), channel_id=1, source_target_pairs={{0,4},{4,8},{8,12},{12,0},{1,5},{5,9},{9,13},{13,1},{2,6},{6,10},{... | collective-permute-start | bytes 221192 | tf_op jit(solution)/shard_map/ppermute | solution.py:313
  51.7 0.0 collective-permute-done.14.grads_ref
  51.7 7.0 %weight_grads.3 = (bf16[8,2048,384]{2,1,0:T(8,128)(2,1)}, bf16[8,2048,384]{2,1,0:T(8,128)(2,1)}, bf16[8,384,2048]{2,1,0:T(8,128)(2,1)}) custom-call(s32[1]{0:T(128)} %bitcast.4.first_ref, bf16[256,2048]{1,0:T(8,128)(2,1)S(1)} %get-tuple-element.65.x_ref, ...), custom_call_target="tpu_custom_call", output_to_operand_aliasing={{0}: (4, {}), {1}: (5, {}), {2}: (6, {})} | custom-call | flops 4831838208 | bytes 18874368 | tf_op jit(solution)/shard_map/weight_grads/pallas_call | solution.py:269
  58.7 0.0 collective-permute-done.11.refs_0_
  58.7 0.1 collective-permute-done.12.refs_1_
  58.8 0.0 collective-permute-done.13.refs_2_
  58.8 0.0 copy-done
  58.8 0.8 %sum_over_experts.1 = (bf16[32,1024]{1,0:T(8,128)(2,1)}, f32[8,32]{1,0:T(8,128)}) custom-call(s32[8,32]{1,0:T(8,128)S(1)} %bitcast.8, f32[32,1152]{1,0:T(8,128)S(1)} %get-tuple-element.73.own_ref, bf16[32,1152]{1,0:T(8,128)(2,1)S(1)} %collective-permute-done.11.refs_0_, bf16[32,1152]{1,0:T(8,128)(2,1)S(1)} %collective-permute-done.12.refs_1_, ...), custom_call_target="tpu_custom_call" | custom-call | tf_op jit(solution)/shard_map/sum_over_experts/pallas_call | solution.py:478
Async XLA Ops:
  1.5 9.2 %collective-permute-start.3 = (bf16[32,2176]{1,0:T(8,128)(2,1)S(1)}, bf16[32,2176]{1,0:T(8,128)(2,1)S(1)}, u32[]{:S(2)}, u32[]{:S(2)}) collective-permute-start(bf16[32,2176]{1,0:T(8,128)(2,1)S(1)} %pack_tokens.1.refs_0_), channel_id=1, source_target_pairs={{0,12},{4,0},{8,4},{12,8},{1,13},{5,1},{9,5},{13,9},{2,14},{6,2},{... | collective-permute-start | bytes 417800 | tf_op jit(solution)/shard_map/ppermute | solution.py:313
  6.6 8.5 %collective-permute-start = (bf16[32,2176]{1,0:T(8,128)(2,1)S(1)}, bf16[32,2176]{1,0:T(8,128)(2,1)S(1)}, u32[]{:S(2)}, u32[]{:S(2)}) collective-permute-start(bf16[32,2176]{1,0:T(8,128)(2,1)S(1)} %pack_tokens.1.refs_0_), channel_id=1, source_target_pairs={{0,4},{4,8},{8,12},{12,0},{1,5},{5,9},{9,13},{13,1},{2,6},{6,10},{... | collective-permute-start | bytes 417800 | tf_op jit(solution)/shard_map/ppermute | solution.py:313
  6.7 9.9 %collective-permute-start.2 = (bf16[32,2176]{1,0:T(8,128)(2,1)S(1)}, bf16[32,2176]{1,0:T(8,128)(2,1)S(1)}, u32[]{:S(2)}, u32[]{:S(2)}) collective-permute-start(bf16[32,2176]{1,0:T(8,128)(2,1)S(1)} %pack_tokens.1.refs_0_), channel_id=1, source_target_pairs={{0,2},{2,0},{1,3},{3,1},{4,6},{6,4},{5,7},{7,5},{8,10},{10,8},{9,1... | collective-permute-start | bytes 417800 | tf_op jit(solution)/shard_map/ppermute | solution.py:313
  8.1 11.4 %collective-permute-start.1 = (bf16[32,2176]{1,0:T(8,128)(2,1)S(1)}, bf16[32,2176]{1,0:T(8,128)(2,1)S(1)}, u32[]{:S(2)}, u32[]{:S(2)}) collective-permute-start(bf16[32,2176]{1,0:T(8,128)(2,1)S(1)} %pack_tokens.1.refs_0_), channel_id=1, source_target_pairs={{0,8},{4,12},{8,0},{12,4},{1,9},{5,13},{9,1},{13,5},{2,10},{6,14},... | collective-permute-start | bytes 417800 | tf_op jit(solution)/shard_map/ppermute | solution.py:313
  10.7 8.8 %collective-permute-start.4 = (bf16[32,2176]{1,0:T(8,128)(2,1)S(1)}, bf16[32,2176]{1,0:T(8,128)(2,1)S(1)}, u32[]{:S(2)}, u32[]{:S(2)}) collective-permute-start(bf16[32,2176]{1,0:T(8,128)(2,1)S(1)} %collective-permute-done.3.refs_3_), channel_id=1, source_target_pairs={{0,2},{2,0},{1,3},{3,1},{4,6},{6,4},{5,7},{7,5},{8,10},{10,8},{9,1... | collective-permute-start | bytes 417800 | tf_op jit(solution)/shard_map/ppermute | solution.py:313
  15.1 8.7 %collective-permute-start.5 = (bf16[32,2176]{1,0:T(8,128)(2,1)S(1)}, bf16[32,2176]{1,0:T(8,128)(2,1)S(1)}, u32[]{:S(2)}, u32[]{:S(2)}) collective-permute-start(bf16[32,2176]{1,0:T(8,128)(2,1)S(1)} %collective-permute-done.refs_1_), channel_id=1, source_target_pairs={{0,2},{2,0},{1,3},{3,1},{4,6},{6,4},{5,7},{7,5},{8,10},{10,8},{9,1... | collective-permute-start | bytes 417800 | tf_op jit(solution)/shard_map/ppermute | solution.py:313
  19.6 5.6 %collective-permute-start.6 = (bf16[32,2176]{1,0:T(8,128)(2,1)S(1)}, bf16[32,2176]{1,0:T(8,128)(2,1)S(1)}, u32[]{:S(2)}, u32[]{:S(2)}) collective-permute-start(bf16[32,2176]{1,0:T(8,128)(2,1)S(1)} %collective-permute-done.1.refs_2_), channel_id=1, source_target_pairs={{0,2},{2,0},{1,3},{3,1},{4,6},{6,4},{5,7},{7,5},{8,10},{10,8},{9,1... | collective-permute-start | bytes 417800 | tf_op jit(solution)/shard_map/ppermute | solution.py:313
  25.2 3.5 %collective-permute-start.7 = (bf16[256,2176]{1,0:T(8,128)(2,1)S(1)}, bf16[256,2176]{1,0:T(8,128)(2,1)S(1)}, u32[]{:S(2)}, u32[]{:S(2)}) collective-permute-start(bf16[256,2176]{1,0:T(8,128)(2,1)S(1)} %collect.1.own_ref), channel_id=1, source_target_pairs={{0,1},{1,0},{2,3},{3,2},{4,5},{5,4},{6,7},{7,6},{8,9},{9,8},{10,11... | collective-permute-start | bytes 3342344 | tf_op jit(solution)/shard_map/ppermute | solution.py:313
  37.0 2.9 %collective-permute-start.8 = (bf16[128,1152]{1,0:T(8,128)(2,1)S(1)}, bf16[128,1152]{1,0:T(8,128)(2,1)S(1)}, u32[]{:S(2)}, u32[]{:S(2)}) collective-permute-start(bf16[128,1152]{1,0:T(8,128)(2,1)S(1)} %get-tuple-element.60), channel_id=1, source_target_pairs={{0,1},{1,0},{2,3},{3,2},{4,5},{5,4},{6,7},{7,6},{8,9},{9,8},{10,11... | collective-permute-start | bytes 884744 | tf_op jit(solution)/shard_map/ppermute | solution.py:313
  39.9 11.8 %collective-permute-start.14 = (bf16[4,256,1152]{2,1,0:T(8,128)(2,1)S(1)}, bf16[4,256,1152]{2,1,0:T(8,128)(2,1)S(1)}, u32[]{:S(2)}, u32[]{:S(2)}) collective-permute-start(bf16[4,256,1152]{2,1,0:T(8,128)(2,1)S(1)} %get-tuple-element.67.grads_ref), channel_id=1, source_target_pairs={{0,1},{1,0},{2,3},{3,2},{4,5},{5,4},{6,7},{7,6},{8,9},{9,8},{10,11... | collective-permute-start | bytes 7077896 | tf_op jit(solution)/shard_map/ppermute | solution.py:313
  40.1 9.5 %collective-permute-start.9 = (bf16[128,1152]{1,0:T(8,128)(2,1)S(1)}, bf16[128,1152]{1,0:T(8,128)(2,1)S(1)}, u32[]{:S(2)}, u32[]{:S(2)}) collective-permute-start(bf16[128,1152]{1,0:T(8,128)(2,1)S(1)} %sum_over_cores.1), channel_id=1, source_target_pairs={{0,2},{2,0},{1,3},{3,1},{4,6},{6,4},{5,7},{7,5},{8,10},{10,8},{9,1... | collective-permute-start | bytes 884744 | tf_op jit(solution)/shard_map/ppermute | solution.py:313
  40.5 9.1 %collective-permute-start.10 = (bf16[128,1152]{1,0:T(8,128)(2,1)S(1)}, bf16[128,1152]{1,0:T(8,128)(2,1)S(1)}, u32[]{:S(2)}, u32[]{:S(2)}) collective-permute-start(bf16[128,1152]{1,0:T(8,128)(2,1)S(1)} %get-tuple-element.64), channel_id=1, source_target_pairs={{0,1},{1,0},{2,3},{3,2},{4,5},{5,4},{6,7},{7,6},{8,9},{9,8},{10,11... | collective-permute-start | bytes 884744 | tf_op jit(solution)/shard_map/ppermute | solution.py:313
  49.6 9.1 %collective-permute-start.11 = (bf16[32,1152]{1,0:T(8,128)(2,1)S(1)}, bf16[32,1152]{1,0:T(8,128)(2,1)S(1)}, u32[]{:S(2)}, u32[]{:S(2)}) collective-permute-start(bf16[32,1152]{1,0:T(8,128)(2,1)S(1)} %get-tuple-element.74), channel_id=1, source_target_pairs={{0,12},{4,0},{8,4},{12,8},{1,13},{5,1},{9,5},{13,9},{2,14},{6,2},{... | collective-permute-start | bytes 221192 | tf_op jit(solution)/shard_map/ppermute | solution.py:313
  50.7 8.1 %collective-permute-start.12 = (bf16[32,1152]{1,0:T(8,128)(2,1)S(1)}, bf16[32,1152]{1,0:T(8,128)(2,1)S(1)}, u32[]{:S(2)}, u32[]{:S(2)}) collective-permute-start(bf16[32,1152]{1,0:T(8,128)(2,1)S(1)} %get-tuple-element.75), channel_id=1, source_target_pairs={{0,8},{4,12},{8,0},{12,4},{1,9},{5,13},{9,1},{13,5},{2,10},{6,14},... | collective-permute-start | bytes 221192 | tf_op jit(solution)/shard_map/ppermute | solution.py:313
  50.7 8.1 %copy-start = (s32[32,8]{0,1:T(8,128)S(1)}, s32[32,8]{0,1:T(8,128)}, u32[]{:S(2)}) copy-start(s32[32,8]{0,1:T(8,128)} %param.9) | copy-start | bytes 3076
  50.7 8.1 %collective-permute-start.13 = (bf16[32,1152]{1,0:T(8,128)(2,1)S(1)}, bf16[32,1152]{1,0:T(8,128)(2,1)S(1)}, u32[]{:S(2)}, u32[]{:S(2)}) collective-permute-start(bf16[32,1152]{1,0:T(8,128)(2,1)S(1)} %get-tuple-element.76), channel_id=1, source_target_pairs={{0,4},{4,8},{8,12},{12,0},{1,5},{5,9},{9,13},{13,1},{2,6},{6,10},{... | collective-permute-start | bytes 221192 | tf_op jit(solution)/shard_map/ppermute | solution.py:313

commit v6 on v5

--- a/solution.py
+++ b/solution.py
@@ -14,7 +14,6 @@
 NT = (((1,), (1,)), ((), ()))
 TN = (((0,), (0,)), ((), ()))
 ANY = pl.BlockSpec(memory_space=pl.ANY)
-SMEM = pl.BlockSpec(memory_space=pltpu.SMEM)
 VMEM = pl.BlockSpec(memory_space=pltpu.VMEM)
 LIGHT = pl.CostEstimate(flops=0, bytes_accessed=1024, transcendentals=0)
 
@@ -63,55 +62,65 @@
     )(*far(activations, out_grad, ids, probs))
 
 
-def collect_kernel(*refs):
+def collect_kernel(n_tensor, *refs):
     *shards, out_ref = refs
     rows = shards[0].shape[0]
+    wide = (shards[0].shape[1] - META) // 2
+    d = n_tensor * wide
+    blocks = len(shards) // n_tensor
     for i, shard in enumerate(shards):
-        out_ref[pl.ds(i * rows, rows), :] = shard[...]
-
-
-def collect(shards):
+        side, at = i // blocks, pl.ds(i % blocks * rows, rows)
+        begin = pl.multiple_of(lax.rem(lax.axis_index("tensor") + side, n_tensor) * wide, wide)
+        out_ref[at, pl.ds(begin, wide)] = shard[:, :wide]
+        out_ref[at, pl.ds(d + begin, wide)] = shard[:, wide : 2 * wide]
+        if side == 0:
+            out_ref[at, 2 * d :] = shard[:, 2 * wide :]
+
+
+def collect(shards, n_tensor):
     rows, columns = shards[0].shape
+    shape = (len(shards) // n_tensor * rows, n_tensor * (columns - META) + META)
     return pl.pallas_call(
-        collect_kernel,
+        functools.partial(collect_kernel, n_tensor),
         in_specs=[VMEM] * len(shards),
         out_specs=VMEM,
-        out_shape=pltpu.VMEM((len(shards) * rows, columns), shards[0].dtype),
+        out_shape=pltpu.VMEM(shape, shards[0].dtype),
         compiler_params=pltpu.CompilerParams(vmem_limit_bytes=4 * MIB),
         cost_estimate=LIGHT,
         name="collect",
     )(*near(*shards))
 
 
-def load_kernel(by_row, start, count, first_ref, *refs):
+def load_kernel(by_row, own, start, count, after_ref, *refs):
     *sources, target_ref, sem = refs
     step = sources[0].shape[1 if by_row else 2]
     many = len(sources)
+    first = lax.axis_index("dp") * own
     copies = []
     for i in range(start, start + count):
         for j, source in enumerate(sources):
             at = pl.ds((many * i + j) * step, step)
             target = target_ref.at[at, :] if by_row else target_ref.at[:, at]
-            copies.append(pltpu.make_async_copy(source.at[first_ref[0] + i], target, sem))
+            copies.append(pltpu.make_async_copy(source.at[first + i], target, sem))
     for copy in copies:
         copy.start()
     for copy in copies:
         copy.wait()
 
 
-def load_kernel_into(by_row, start, count, first_ref, *refs):
+def load_kernel_into(by_row, own, start, count, after_ref, *refs):
     *refs, _, target_ref, sem = refs
-    load_kernel(by_row, start, count, first_ref, *refs, target_ref, sem)
-
-
-def load_weights(first, sources, by_row, own, start, count, into=None):
+    load_kernel(by_row, own, start, count, after_ref, *refs, target_ref, sem)
+
+
+def load_weights(after, sources, by_row, own, start, count, into=None):
     _, rows, columns = sources[0].shape
     many = own * len(sources)
     shape = (many * rows, columns) if by_row else (rows, many * columns)
     kept = [] if into is None else near(into)
     return pl.pallas_call(
-        functools.partial(load_kernel_into if kept else load_kernel, by_row, start, count),
-        in_specs=[SMEM] + [ANY] * len(sources) + [VMEM] * len(kept),
+        functools.partial(load_kernel_into if kept else load_kernel, by_row, own, start, count),
+        in_specs=[VMEM] + [ANY] * len(sources) + [VMEM] * len(kept),
         out_specs=VMEM,
         out_shape=pltpu.VMEM(shape, jnp.bfloat16),
         scratch_shapes=[pltpu.SemaphoreType.DMA],
@@ -119,42 +128,32 @@
         compiler_params=pltpu.CompilerParams(vmem_limit_bytes=4 * MIB),
         cost_estimate=LIGHT,
         name="load_weights",
-    )(first, *far(*sources), *kept)
-
-
-def forward_kernel(places, n_tensor, top, own, scalars, own_ref, got_ref, w_in, wd_ref, *outs):
-    x_ref, og_ref, grads_ref, both_ref, inners_ref, kept_ref, sent_ref, w_out, sem = outs
-    tensor = scalars[1]
-    tokens, d = x_ref.shape
-    wide, share = d // n_tensor, tokens // 2
-    ff = wd_ref.shape[1]
+    )(*near(after), *far(*sources), *kept)
+
+
+def forward_kernel(n_tensor, top, own, held_ref, got_ref, w_in, wd_ref, *outs):
+    grads_ref, both_ref, inners_ref, kept_ref, sent_ref, w_out, sem = outs
+    local_count, ff, d = wd_ref.shape
+    first = lax.axis_index("dp") * own
+    first_expert = lax.axis_index("expert") * local_count + first
+    every = lambda at: jnp.concatenate([held_ref[:, at], got_ref[:, at]], axis=0)
     copies = [
-        pltpu.make_async_copy(wd_ref.at[scalars[0] + i], w_out.at[pl.ds(i * ff, ff), :], sem) for i in range(own)
+        pltpu.make_async_copy(wd_ref.at[first + i], w_out.at[pl.ds(i * ff, ff), :], sem) for i in range(own)
     ]
     for copy in copies:
         copy.start()
-    rows = own_ref.shape[0] // len(places)
-    metas = []
-    for base, held in ((0, own_ref), (share, got_ref)):
-        for i, (row, side) in enumerate(places):
-            at, to = pl.ds(i * rows, rows), pl.ds(base + row, rows)
-            columns = pl.ds(pl.multiple_of(lax.rem(tensor + side, n_tensor) * wide, wide), wide)
-            x_ref[to, columns] = held[at, :wide]
-            og_ref[to, columns] = held[at, wide : 2 * wide]
-            if side == 0:
-                metas.append(held[at, 2 * wide :].astype(jnp.float32))
-    meta = jnp.concatenate(metas, axis=0)
-    pre = jnp.dot(x_ref[...], w_in[...], preferred_element_type=jnp.float32)
+    pre = jnp.dot(every(slice(0, d)), w_in[...], preferred_element_type=jnp.float32)
     for copy in copies:
         copy.wait()
-    hidden_grads = lax.dot_general(og_ref[...], w_out[...], NT, preferred_element_type=jnp.float32)
+    hidden_grads = lax.dot_general(every(slice(d, 2 * d)), w_out[...], NT, preferred_element_type=jnp.float32)
+    meta = every(slice(2 * d, None)).astype(jnp.float32)
     lane = lax.broadcasted_iota(jnp.int32, meta.shape, 1)
     inners = jnp.zeros(meta.shape, jnp.float32)
     both = []
     for i in range(own):
         gate_pre, up_pre = pre[:, 2 * i * ff : (2 * i + 1) * ff], pre[:, (2 * i + 1) * ff : (2 * i + 2) * ff]
         hidden_grad = hidden_grads[:, i * ff : (i + 1) * ff]
-        expert = scalars[2] + i
+        expert = first_expert + i
         hit = meta[:, :top] == expert.astype(jnp.float32)
         prob = jnp.sum(jnp.where(hit, meta[:, top : 2 * top], 0.0), axis=1, keepdims=True)
         sigma = jax.nn.sigmoid(gate_pre)
@@ -172,13 +171,13 @@
     both = jnp.concatenate(both, axis=1)
     both_ref[...] = both
     inners_ref[...] = inners
-    row_pass(tensor + 1, n_tensor, both, inners, w_in, kept_ref, sent_ref)
+    row_pass(1, n_tensor, both, inners, w_in, kept_ref, sent_ref)
 
 
 def row_pass(side, n_tensor, both, inners, w_in, kept_ref, sent_ref):
     wide = w_in.shape[0] // n_tensor
     share = both.shape[0] // 2
-    at = pl.ds(pl.multiple_of(lax.rem(side, n_tensor) * wide, wide), wide)
+    at = pl.ds(pl.multiple_of(lax.rem(lax.axis_index("tensor") + side, n_tensor) * wide, wide), wide)
     total = lax.dot_general(both, w_in[at, :], NT, preferred_element_type=jnp.float32)
     kept_ref[:, :wide] = total[:share]
     kept_ref[:, wide:] = inners[:share]
@@ -186,59 +185,60 @@
     sent_ref[:, wide:] = inners[share:].astype(jnp.bfloat16)
 
 
-def rows_kernel(n_tensor, scalars, both_ref, inners_ref, w_in, kept_ref, sent_ref):
-    row_pass(scalars[1], n_tensor, both_ref[...], inners_ref[...], w_in, kept_ref, sent_ref)
-
-
-def forward_call(kernel, name, scalars, inputs, out_shape, flops, distant=(), scratch=()):
+def rows_kernel(n_tensor, both_ref, inners_ref, w_in, kept_ref, sent_ref):
+    row_pass(0, n_tensor, both_ref[...], inners_ref[...], w_in, kept_ref, sent_ref)
+
+
+def forward_call(kernel, name, inputs, out_shape, flops, distant=(), scratch=()):
     return pl.pallas_call(
         kernel,
-        in_specs=[SMEM] + [VMEM] * len(inputs) + [ANY] * len(distant),
+        in_specs=[VMEM] * len(inputs) + [ANY] * len(distant),
         out_specs=[VMEM] * len(out_shape),
         out_shape=out_shape,
         scratch_shapes=scratch,
         compiler_params=pltpu.CompilerParams(vmem_limit_bytes=20 * MIB),
         cost_estimate=pl.CostEstimate(flops=flops, bytes_accessed=1024, transcendentals=0),
         name=name,
-    )(scalars, *near(*inputs), *far(*distant))
-
-
-def forward(held, got, places, scalars, w_in, w_down, own, n_tensor, top):
+    )(*near(*inputs), *far(*distant))
+
+
+def forward(held, got, w_in, w_down, own, n_tensor, top):
     _, ff, d = w_down.shape
-    share = held.shape[0] // n_tensor
+    share = held.shape[0]
     tokens = 2 * share
     sums = (share, d // n_tensor + META)
     shapes = [
-        pltpu.VMEM((tokens, d), jnp.bfloat16),
-        pltpu.VMEM((tokens, d), jnp.bfloat16),
         pltpu.VMEM((own, tokens, 3 * ff), jnp.bfloat16),
         pltpu.VMEM((tokens, own * 2 * ff), jnp.bfloat16),
         pltpu.VMEM((tokens, META), jnp.float32),
         pltpu.VMEM(sums, jnp.float32),
         pltpu.VMEM(sums, jnp.bfloat16),
     ]
-    kernel = functools.partial(forward_kernel, places, n_tensor, top, own)
+    kernel = functools.partial(forward_kernel, n_tensor, top, own)
     scratch = [pltpu.VMEM((own * ff, d), jnp.bfloat16), pltpu.SemaphoreType.DMA]
     flops = 8 * own * tokens * d * ff
-    return forward_call(kernel, "routed_forward", scalars, [held, got, w_in], shapes, flops, [w_down], scratch)
-
-
-def row_sums(scalars, both, inners, w_in, n_tensor):
+    return forward_call(kernel, "routed_forward", [held, got, w_in], shapes, flops, [w_down], scratch)
+
+
+def row_sums(both, inners, w_in, n_tensor):
     tokens, d = both.shape[0], w_in.shape[0]
     sums = (tokens // 2, d // n_tensor + META)
     shapes = [pltpu.VMEM(sums, jnp.float32), pltpu.VMEM(sums, jnp.bfloat16)]
     kernel = functools.partial(rows_kernel, n_tensor)
-    return forward_call(kernel, "row_sums", scalars, [both, inners, w_in], shapes, 2 * tokens * d * w_in.shape[1])
-
-
-def weight_kernel(swap, first_ref, x_ref, og_ref, grads_ref, *refs):
+    return forward_call(kernel, "row_sums", [both, inners, w_in], shapes, 2 * tokens * d * w_in.shape[1])
+
+
+def weight_kernel(swap, held_ref, got_ref, grads_ref, *refs):
     *targets, gate_ref, up_ref, down_ref, sem = refs[-7:]
     own, d, ff = gate_ref.shape
     half, step = grads_ref.shape[1] // 2, d // PARTS
+    core = lax.axis_index("dp")
+    first = (1 - core if swap else core) * own
+    both = lambda at: jnp.concatenate([held_ref[:, at], got_ref[:, at]], axis=0)
     copies = []
 
     def send(ref, target, i, at):
-        copies.append(pltpu.make_async_copy(ref.at[(i, *at)], target.at[(first_ref[0] + i, *at)], sem))
+        copies.append(pltpu.make_async_copy(ref.at[(i, *at)], target.at[(first + i, *at)], sem))
         copies[-1].start()
 
     for i in range(own):
@@ -247,38 +247,39 @@
             grads = jnp.concatenate([grads[half:], grads[:half]], axis=0)
         for part in range(PARTS):
             at, every = pl.ds(part * step, step), pl.ds(0, ff)
-            total = lax.dot_general(x_ref[:, at], grads[:, : 2 * ff], TN, preferred_element_type=jnp.float32)
+            total = lax.dot_general(both(at), grads[:, : 2 * ff], TN, preferred_element_type=jnp.float32)
             gate_ref[i, at, :] = total[:, :ff].astype(jnp.bfloat16)
             up_ref[i, at, :] = total[:, ff:].astype(jnp.bfloat16)
             send(gate_ref, targets[0], i, (at, every))
             send(up_ref, targets[1], i, (at, every))
         for part in range(PARTS):
             at, every = pl.ds(part * step, step), pl.ds(0, ff)
-            total = lax.dot_general(grads[:, 2 * ff :], og_ref[:, at], TN, preferred_element_type=jnp.float32)
+            after = pl.ds(d + part * step, step)
+            total = lax.dot_general(grads[:, 2 * ff :], both(after), TN, preferred_element_type=jnp.float32)
             down_ref[i, :, at] = total.astype(jnp.bfloat16)
             send(down_ref, targets[2], i, (every, at))
     for copy in copies:
         copy.wait()
 
 
-def weight_grads(first, x, og, grads, local_count, into=None):
+def weight_grads(held, got, grads, local_count, into=None):
     own, tokens, ff = grads.shape[0], grads.shape[1], grads.shape[2] // 3
-    d = x.shape[1]
+    d = (held.shape[1] - META) // 2
     kept = [] if into is None else list(into)
     shapes = [(d, ff), (d, ff), (ff, d)]
     return pl.pallas_call(
         functools.partial(weight_kernel, into is not None),
-        in_specs=[SMEM] + [VMEM] * 3 + [ANY] * len(kept),
+        in_specs=[VMEM] * 3 + [ANY] * len(kept),
         out_specs=[ANY] * 3,
         out_shape=[pltpu.HBM((local_count, *s), jnp.bfloat16) for s in shapes],
         scratch_shapes=[pltpu.VMEM((own, *s), jnp.bfloat16) for s in shapes] + [pltpu.SemaphoreType.DMA],
-        input_output_aliases={4 + i: i for i in range(len(kept))},
+        input_output_aliases={3 + i: i for i in range(len(kept))},
         compiler_params=pltpu.CompilerParams(vmem_limit_bytes=26 * MIB),
         cost_estimate=pl.CostEstimate(
             flops=6 * own * tokens * d * ff, bytes_accessed=6 * own * d * ff, transcendentals=0
         ),
         name="weight_grads",
-    )(first, *near(x, og, grads), *kept)
+    )(*near(held, got, grads), *kept)
 
 
 def dp_sum_kernel(kept_ref, got_ref, there_ref):
@@ -427,26 +428,20 @@
     tokens = rows * n_expert * n_dp
     wide = d // n_tensor
     own = local_count // n_dp
-    e, t, p = (lax.axis_index(a) for a in ("expert", "tensor", "dp"))
-    first = p * own
-    scalars = jnp.stack([first, t, e * local_count + first, own - first]).astype(jnp.int32)
     ids = expert_ids.T
     packed = pack(activations, out_grad, ids, gate_probs.T)
     along = [packed] + [shift(packed, "expert", k) for k in range(1, n_expert)]
     across = {k: shift(along[k], "tensor", 1) for k in (0, 3, 1)}
-    along[2], across[0], across[3], then = lax.optimization_barrier((along[2], across[0], across[3], scalars))
+    along[2], across[0], across[3] = lax.optimization_barrier((along[2], across[0], across[3]))
     across[2] = shift(along[2], "tensor", 1)
-    w_in = load_weights(then, (w_gate, w_up), False, own, 0, own // 2)
-    across[1], across[2], w_in, then = lax.optimization_barrier((across[1], across[2], w_in, scalars))
-    w_in = load_weights(then, (w_gate, w_up), False, own, own // 2, own - own // 2, w_in)
-    held = collect(along + [across[k] for k in range(n_expert)])
-    places = [(k * rows, side) for side in range(n_tensor) for k in range(n_expert)]
+    w_in = load_weights(along[2], (w_gate, w_up), False, own, 0, own // 2)
+    across[1], across[2], w_in = lax.optimization_barrier((across[1], across[2], w_in))
+    w_in = load_weights(across[2], (w_gate, w_up), False, own, own // 2, own - own // 2, w_in)
+    held = collect(along + [across[k] for k in range(n_expert)], n_tensor)
     swapped = shift(held, "dp", 1)
-    x, og, grads, both, inners, kept, sent = forward(
-        held, swapped, places, scalars, w_in, w_down, own, n_tensor, top
-    )
+    grads, both, inners, kept, sent = forward(held, swapped, w_in, w_down, own, n_tensor, top)
     got = shift(sent, "dp", 1)
-    kept_here, sent_here = row_sums(scalars, both, inners, w_in, n_tensor)
+    kept_here, sent_here = row_sums(both, inners, w_in, n_tensor)
     got, sent_here, grads = lax.optimization_barrier((got, sent_here, grads))
     half = (tokens // 2, wide + META)
     there = pl.pallas_call(
@@ -461,7 +456,7 @@
     crossed = shift(there, "tensor", 1)
     got_here = shift(sent_here, "dp", 1)
     got_grads = shift(grads, "dp", 1)
-    outputs = weight_grads(scalars, x, og, grads, local_count)
+    outputs = weight_grads(held, swapped, grads, local_count)
     crossed, got_here, outputs = lax.optimization_barrier((crossed, got_here, outputs))
     piece = (rows, wide + META)
     pieces = pl.pallas_call(
@@ -473,7 +468,7 @@
         name="sum_over_tensor",
     )(*near(kept_here, got_here, crossed))
     received = [shift(pieces[k], "expert", -k) for k in range(1, n_expert)]
-    outputs = weight_grads(scalars[3:], x, og, got_grads, local_count, outputs)
+    outputs = weight_grads(held, swapped, got_grads, local_count, outputs)
     received, outputs = lax.optimization_barrier((received, outputs))
     grad, probs = pl.pallas_call(
         functools.partial(finish_kernel, top),

time: 59.8 us -> 57.9 us (0.968)
  Pallas kernels: 33.8 us -> 30.9 us
  waiting for transfers between devices: 10.1 us -> 11.2 us
    pallas_call x3, Pallas kernels: 10.7 us -> 9.39 us  [the longest x2 9.3 us: forward_call(): pl.pallas_call(kernel, in_specs=[VMEM] * len(inputs) + [ANY] * len(distan...]
    ppermute x15, waiting for transfers between devices: 10.1 us -> 11.2 us  [shift(): return lax.ppermute(x, axis, [(i, (i + by) % count) for i in range(count)])]
    pallas_call x2, Pallas kernels: 6.77 us -> 5.69 us  [load_weights(): pl.pallas_call(functools.partial(load_kernel_into if kept else load_kerne...]
  transfers between devices with their start and end apart: 15 -> 15, of which waited for: 5 -> 5; matrix products, arithmetic and copies ran while one was open for 0% -> 0% of each run, Pallas kernels for 40% -> 37%
where the time goes in v6:
time: 57.9 us; the launch traced here: 57.7 us
  Pallas kernels  30.9 us (53%)
  starting transfers between devices  14.8 us (26%)
  waiting for transfers between devices  11.2 us (19%)
  between operations  0.77 us (1%)
    ppermute x15, starting transfers between devices, shift(): return lax.ppermute(x, axis, [(i, (i + by) % count) for i in range(count)])  14.8 us
    pallas_call x2, Pallas kernels, weight_grads(): pl.pallas_call(functools.partial(weight_kernel, into is not None), in_spe...  13.9 us
    ppermute x15, waiting for transfers between devices, shift(): return lax.ppermute(x, axis, [(i, (i + by) % count) for i in range(count)])  11.2 us
    pallas_call x2, Pallas kernels, forward_call(): pl.pallas_call(kernel, in_specs=[VMEM] * len(inputs) + [ANY] * len(distan...  9.3 us
    pallas_call x2, Pallas kernels, load_weights(): pl.pallas_call(functools.partial(load_kernel_into if kept else load_kerne...  5.69 us
  transfers between devices with their start and end apart: 15, of which 5 were waited for; matrix products, arithmetic and copies ran while one was open for 0% of the time, Pallas kernels for 37%

profile of v6, /device:TPU:0, one launch (start us, length us, event | category | flops | bytes accessed | tf_op | source)
XLA Modules:
  0.0 57.7 jit_solution(14559915538676002205)
XLA Ops:
  0.6 0.9 %pack_tokens.1.refs_0_ = bf16[32,2176]{1,0:T(8,128)(2,1)S(1)} custom-call(bf16[32,1024]{1,0:T(8,128)(2,1)} %act_hbm.1, bf16[32,1024]{1,0:T(8,128)(2,1)} %og_hbm.1, s32[8,32]{1,0:T(8,128)} %bitcast.3, bf16[8,32]{1,0:T(8,128)(2,1)} %bitcast.5), custom_call_target="tpu_custom_call" | custom-call | tf_op jit(solution)/shard_map/pack_tokens/pallas_call | solution.py:50
  1.5 5.1 %collective-permute-start.3 = (bf16[32,2176]{1,0:T(8,128)(2,1)S(1)}, bf16[32,2176]{1,0:T(8,128)(2,1)S(1)}, u32[]{:S(2)}, u32[]{:S(2)}) collective-permute-start(bf16[32,2176]{1,0:T(8,128)(2,1)S(1)} %pack_tokens.1.refs_0_), channel_id=1, source_target_pairs={{0,12},{4,0},{8,4},{12,8},{1,13},{5,1},{9,5},{13,9},{2,14},{6,2},{... | collective-permute-start | bytes 417800 | tf_op jit(solution)/shard_map/ppermute | solution.py:314
  6.6 0.0 collective-permute-start
  6.7 1.5 %collective-permute-start.2 = (bf16[32,2176]{1,0:T(8,128)(2,1)S(1)}, bf16[32,2176]{1,0:T(8,128)(2,1)S(1)}, u32[]{:S(2)}, u32[]{:S(2)}) collective-permute-start(bf16[32,2176]{1,0:T(8,128)(2,1)S(1)} %pack_tokens.1.refs_0_), channel_id=1, source_target_pairs={{0,2},{2,0},{1,3},{3,1},{4,6},{6,4},{5,7},{7,5},{8,10},{10,8},{9,1... | collective-permute-start | bytes 417800 | tf_op jit(solution)/shard_map/ppermute | solution.py:314
  8.1 1.0 %collective-permute-start.1 = (bf16[32,2176]{1,0:T(8,128)(2,1)S(1)}, bf16[32,2176]{1,0:T(8,128)(2,1)S(1)}, u32[]{:S(2)}, u32[]{:S(2)}) collective-permute-start(bf16[32,2176]{1,0:T(8,128)(2,1)S(1)} %pack_tokens.1.refs_0_), channel_id=1, source_target_pairs={{0,8},{4,12},{8,0},{12,4},{1,9},{5,13},{9,1},{13,5},{2,10},{6,14},... | collective-permute-start | bytes 417800 | tf_op jit(solution)/shard_map/ppermute | solution.py:314
  9.2 1.6 %collective-permute-done.3.refs_3_ = bf16[32,2176]{1,0:T(8,128)(2,1)S(1)} collective-permute-done((bf16[32,2176]{1,0:T(8,128)(2,1)S(1)}, bf16[32,2176]{1,0:T(8,128)(2,1)S(1)}, u32[]{:S(2)}, u32[]{:S(2)}) %collective-permute-start.3) | collective-permute-done | bytes 139296 | tf_op jit(solution)/shard_map/ppermute | solution.py:314
  10.7 1.5 %collective-permute-start.4 = (bf16[32,2176]{1,0:T(8,128)(2,1)S(1)}, bf16[32,2176]{1,0:T(8,128)(2,1)S(1)}, u32[]{:S(2)}, u32[]{:S(2)}) collective-permute-start(bf16[32,2176]{1,0:T(8,128)(2,1)S(1)} %collective-permute-done.3.refs_3_), channel_id=1, source_target_pairs={{0,2},{2,0},{1,3},{3,1},{4,6},{6,4},{5,7},{7,5},{8,10},{10,8},{9,1... | collective-permute-start | bytes 417800 | tf_op jit(solution)/shard_map/ppermute | solution.py:314
  12.2 2.9 %collective-permute-done.refs_1_ = bf16[32,2176]{1,0:T(8,128)(2,1)S(1)} collective-permute-done((bf16[32,2176]{1,0:T(8,128)(2,1)S(1)}, bf16[32,2176]{1,0:T(8,128)(2,1)S(1)}, u32[]{:S(2)}, u32[]{:S(2)}) %collective-permute-start) | collective-permute-done | bytes 139296 | tf_op jit(solution)/shard_map/ppermute | solution.py:314
  15.1 1.4 %collective-permute-start.5 = (bf16[32,2176]{1,0:T(8,128)(2,1)S(1)}, bf16[32,2176]{1,0:T(8,128)(2,1)S(1)}, u32[]{:S(2)}, u32[]{:S(2)}) collective-permute-start(bf16[32,2176]{1,0:T(8,128)(2,1)S(1)} %collective-permute-done.refs_1_), channel_id=1, source_target_pairs={{0,2},{2,0},{1,3},{3,1},{4,6},{6,4},{5,7},{7,5},{8,10},{10,8},{9,1... | collective-permute-start | bytes 417800 | tf_op jit(solution)/shard_map/ppermute | solution.py:314
  16.6 0.0 collective-permute-done.2.refs_4_
  16.6 3.0 %collective-permute-done.1.after_ref.refs_2_ = bf16[32,2176]{1,0:T(8,128)(2,1)S(1)} collective-permute-done((bf16[32,2176]{1,0:T(8,128)(2,1)S(1)}, bf16[32,2176]{1,0:T(8,128)(2,1)S(1)}, u32[]{:S(2)}, u32[]{:S(2)}) %collective-permute-start.1) | collective-permute-done | bytes 139296 | tf_op jit(solution)/shard_map/ppermute | solution.py:314
  19.5 0.0 collective-permute-done.4.refs_7_
  19.6 0.9 %collective-permute-start.6 = (bf16[32,2176]{1,0:T(8,128)(2,1)S(1)}, bf16[32,2176]{1,0:T(8,128)(2,1)S(1)}, u32[]{:S(2)}, u32[]{:S(2)}) collective-permute-start(bf16[32,2176]{1,0:T(8,128)(2,1)S(1)} %collective-permute-done.1.after_ref.refs_2_), channel_id=1, source_target_pairs={{0,2},{2,0},{1,3},{3,1},{4,6},{6,4},{5,7},{7,5},{8,10},{10,8},{9,1... | collective-permute-start | bytes 417800 | tf_op jit(solution)/shard_map/ppermute | solution.py:314
  20.4 2.8 %load_weights.2.refs_2_ = bf16[2048,3072]{1,0:T(8,128)(2,1)S(1)} custom-call(bf16[32,2176]{1,0:T(8,128)(2,1)S(1)} %collective-permute-done.1.after_ref.refs_2_, bf16[8,2048,384]{2,1,0:T(8,128)(2,1)} %refs_0_.3, bf16[8,2048,384]{2,1,0:T(8,128)(2,1)} %refs_1_.3), custom_call_target="tpu_custom_call" | custom-call | bytes 1024 | tf_op jit(solution)/shard_map/load_weights/pallas_call | solution.py:121
  23.2 0.0 collective-permute-done.5.refs_5_
  23.3 1.9 %collective-permute-done.6.refs_6_.after_ref = bf16[32,2176]{1,0:T(8,128)(2,1)S(1)} collective-permute-done((bf16[32,2176]{1,0:T(8,128)(2,1)S(1)}, bf16[32,2176]{1,0:T(8,128)(2,1)S(1)}, u32[]{:S(2)}, u32[]{:S(2)}) %collective-permute-start.6) | collective-permute-done | bytes 139296 | tf_op jit(solution)/shard_map/ppermute | solution.py:314
  25.1 0.1 collect.1.held_ref
  25.2 0.1 collective-permute-start.7
  25.3 2.8 %load_weights.3.w_in = bf16[2048,3072]{1,0:T(8,128)(2,1)S(1)} custom-call(bf16[32,2176]{1,0:T(8,128)(2,1)S(1)} %collective-permute-done.6.refs_6_.after_ref, bf16[8,2048,384]{2,1,0:T(8,128)(2,1)} %refs_0_.3, bf16[8,2048,384]{2,1,0:T(8,128)(2,1)} %refs_1_.3, bf16[2048,3072]{1,0:T(8,128)(2,1)S(1)} %load_weights.2.refs_2_), custom_call_target="tpu_custom_call", output_to_operand_aliasing={{}: (3, {})} | custom-call | bytes 1024 | tf_op jit(solution)/shard_map/load_weights/pallas_call | solution.py:121
  28.2 0.0 collective-permute-done.7.got_ref
  28.2 7.5 %routed_forward.1 = (bf16[4,256,1152]{2,1,0:T(8,128)(2,1)S(1)}, bf16[256,3072]{1,0:T(8,128)(2,1)S(1)}, f32[256,128]{1,0:T(8,128)S(1)}, f32[128,1152]{1,0:T(8,128)S(1)}, bf16[128,1152]{1,0:T(8,128)(2,1)S(1)}) custom-call(bf16[128,4224]{1,0:T(8,128)(2,1)S(1)} %collect.1.held_ref, bf16[128,4224]{1,0:T(8,128)(2,1)S(1)} %collective-permute-done.7.got_ref, ...), custom_call_target="tpu_custom_call" | custom-call | flops 6442450944 | bytes 1024 | tf_op jit(solution)/shard_map/routed_forward/pallas_call | solution.py:193
  35.7 0.6 collective-permute-start.8
  36.2 1.8 %row_sums.1 = (f32[128,1152]{1,0:T(8,128)S(1)}, bf16[128,1152]{1,0:T(8,128)(2,1)S(1)}) custom-call(bf16[256,3072]{1,0:T(8,128)(2,1)S(1)} %get-tuple-element.50.both_ref, f32[256,128]{1,0:T(8,128)S(1)} %get-tuple-element.51.inners_ref, bf16[2048,3072]{1,0:T(8,128)(2,1)S(1)} %load_weights.3.w_in), custom_call_target="tpu_custom_call" | custom-call | flops 3221225472 | bytes 1024 | tf_op jit(solution)/shard_map/row_sums/pallas_call | solution.py:193
  38.1 0.0 collective-permute-done.8.got_ref
  38.1 0.1 collective-permute-start.14
  38.2 0.1 sum_over_cores.1
  38.2 0.4 collective-permute-start.9
  38.6 0.2 collective-permute-start.10
  38.8 7.0 %weight_grads.2 = (bf16[8,2048,384]{2,1,0:T(8,128)(2,1)}, bf16[8,2048,384]{2,1,0:T(8,128)(2,1)}, bf16[8,384,2048]{2,1,0:T(8,128)(2,1)}) custom-call(bf16[128,4224]{1,0:T(8,128)(2,1)S(1)} %collect.1.held_ref, bf16[128,4224]{1,0:T(8,128)(2,1)S(1)} %collective-permute-done.7.got_ref, bf16[4,256,1152]{2,1,0:T(8,128)(2,1)S(1)} %get-tuple-element.59.grads_ref), custom_call_target="tpu_custom_call" | custom-call | flops 4831838208 | bytes 18874368 | tf_op jit(solution)/shard_map/weight_grads/pallas_call | solution.py:270
  45.8 1.9 %collective-permute-done.9.got_ref = bf16[128,1152]{1,0:T(8,128)(2,1)S(1)} collective-permute-done((bf16[128,1152]{1,0:T(8,128)(2,1)S(1)}, bf16[128,1152]{1,0:T(8,128)(2,1)S(1)}, u32[]{:S(2)}, u32[]{:S(2)}) %collective-permute-start.9) | collective-permute-done | bytes 294944 | tf_op jit(solution)/shard_map/ppermute | solution.py:314
  47.7 0.0 collective-permute-done.10.core_ref
  47.7 0.1 sum_over_tensor.1
  47.8 1.0 %collective-permute-start.11 = (bf16[32,1152]{1,0:T(8,128)(2,1)S(1)}, bf16[32,1152]{1,0:T(8,128)(2,1)S(1)}, u32[]{:S(2)}, u32[]{:S(2)}) collective-permute-start(bf16[32,1152]{1,0:T(8,128)(2,1)S(1)} %get-tuple-element.66), channel_id=1, source_target_pairs={{0,12},{4,0},{8,4},{12,8},{1,13},{5,1},{9,5},{13,9},{2,14},{6,2},{... | collective-permute-start | bytes 221192 | tf_op jit(solution)/shard_map/ppermute | solution.py:314
  48.8 0.0 collective-permute-start.12
  48.8 0.0 copy-start
  48.8 1.0 %collective-permute-start.13 = (bf16[32,1152]{1,0:T(8,128)(2,1)S(1)}, bf16[32,1152]{1,0:T(8,128)(2,1)S(1)}, u32[]{:S(2)}, u32[]{:S(2)}) collective-permute-start(bf16[32,1152]{1,0:T(8,128)(2,1)S(1)} %get-tuple-element.68), channel_id=1, source_target_pairs={{0,4},{4,8},{8,12},{12,0},{1,5},{5,9},{9,13},{13,1},{2,6},{6,10},{... | collective-permute-start | bytes 221192 | tf_op jit(solution)/shard_map/ppermute | solution.py:314
  49.9 0.0 collective-permute-done.14.grads_ref
  49.9 7.0 %weight_grads.3 = (bf16[8,2048,384]{2,1,0:T(8,128)(2,1)}, bf16[8,2048,384]{2,1,0:T(8,128)(2,1)}, bf16[8,384,2048]{2,1,0:T(8,128)(2,1)}) custom-call(bf16[128,4224]{1,0:T(8,128)(2,1)S(1)} %collect.1.held_ref, bf16[128,4224]{1,0:T(8,128)(2,1)S(1)} %collective-permute-done.7.got_ref, ...), custom_call_target="tpu_custom_call", output_to_operand_aliasing={{0}: (3, {}), {1}: (4, {}), {2}: (5, {})} | custom-call | flops 4831838208 | bytes 18874368 | tf_op jit(solution)/shard_map/weight_grads/pallas_call | solution.py:270
  56.8 0.0 collective-permute-done.11.refs_0_
  56.8 0.0 collective-permute-done.12.refs_1_
  56.8 0.0 collective-permute-done.13.refs_2_
  56.9 0.0 copy-done
  56.9 0.8 %sum_over_experts.1 = (bf16[32,1024]{1,0:T(8,128)(2,1)}, f32[8,32]{1,0:T(8,128)}) custom-call(s32[8,32]{1,0:T(8,128)S(1)} %bitcast.4, f32[32,1152]{1,0:T(8,128)S(1)} %get-tuple-element.65.own_ref, bf16[32,1152]{1,0:T(8,128)(2,1)S(1)} %collective-permute-done.11.refs_0_, bf16[32,1152]{1,0:T(8,128)(2,1)S(1)} %collective-permute-done.12.refs_1_, ...), custom_call_target="tpu_custom_call" | custom-call | tf_op jit(solution)/shard_map/sum_over_experts/pallas_call | solution.py:473
Async XLA Ops:
  1.5 9.2 %collective-permute-start.3 = (bf16[32,2176]{1,0:T(8,128)(2,1)S(1)}, bf16[32,2176]{1,0:T(8,128)(2,1)S(1)}, u32[]{:S(2)}, u32[]{:S(2)}) collective-permute-start(bf16[32,2176]{1,0:T(8,128)(2,1)S(1)} %pack_tokens.1.refs_0_), channel_id=1, source_target_pairs={{0,12},{4,0},{8,4},{12,8},{1,13},{5,1},{9,5},{13,9},{2,14},{6,2},{... | collective-permute-start | bytes 417800 | tf_op jit(solution)/shard_map/ppermute | solution.py:314
  6.6 8.5 %collective-permute-start = (bf16[32,2176]{1,0:T(8,128)(2,1)S(1)}, bf16[32,2176]{1,0:T(8,128)(2,1)S(1)}, u32[]{:S(2)}, u32[]{:S(2)}) collective-permute-start(bf16[32,2176]{1,0:T(8,128)(2,1)S(1)} %pack_tokens.1.refs_0_), channel_id=1, source_target_pairs={{0,4},{4,8},{8,12},{12,0},{1,5},{5,9},{9,13},{13,1},{2,6},{6,10},{... | collective-permute-start | bytes 417800 | tf_op jit(solution)/shard_map/ppermute | solution.py:314
  6.7 9.9 %collective-permute-start.2 = (bf16[32,2176]{1,0:T(8,128)(2,1)S(1)}, bf16[32,2176]{1,0:T(8,128)(2,1)S(1)}, u32[]{:S(2)}, u32[]{:S(2)}) collective-permute-start(bf16[32,2176]{1,0:T(8,128)(2,1)S(1)} %pack_tokens.1.refs_0_), channel_id=1, source_target_pairs={{0,2},{2,0},{1,3},{3,1},{4,6},{6,4},{5,7},{7,5},{8,10},{10,8},{9,1... | collective-permute-start | bytes 417800 | tf_op jit(solution)/shard_map/ppermute | solution.py:314
  8.1 11.4 %collective-permute-start.1 = (bf16[32,2176]{1,0:T(8,128)(2,1)S(1)}, bf16[32,2176]{1,0:T(8,128)(2,1)S(1)}, u32[]{:S(2)}, u32[]{:S(2)}) collective-permute-start(bf16[32,2176]{1,0:T(8,128)(2,1)S(1)} %pack_tokens.1.refs_0_), channel_id=1, source_target_pairs={{0,8},{4,12},{8,0},{12,4},{1,9},{5,13},{9,1},{13,5},{2,10},{6,14},... | collective-permute-start | bytes 417800 | tf_op jit(solution)/shard_map/ppermute | solution.py:314
  10.7 8.8 %collective-permute-start.4 = (bf16[32,2176]{1,0:T(8,128)(2,1)S(1)}, bf16[32,2176]{1,0:T(8,128)(2,1)S(1)}, u32[]{:S(2)}, u32[]{:S(2)}) collective-permute-start(bf16[32,2176]{1,0:T(8,128)(2,1)S(1)} %collective-permute-done.3.refs_3_), channel_id=1, source_target_pairs={{0,2},{2,0},{1,3},{3,1},{4,6},{6,4},{5,7},{7,5},{8,10},{10,8},{9,1... | collective-permute-start | bytes 417800 | tf_op jit(solution)/shard_map/ppermute | solution.py:314
  15.1 8.1 %collective-permute-start.5 = (bf16[32,2176]{1,0:T(8,128)(2,1)S(1)}, bf16[32,2176]{1,0:T(8,128)(2,1)S(1)}, u32[]{:S(2)}, u32[]{:S(2)}) collective-permute-start(bf16[32,2176]{1,0:T(8,128)(2,1)S(1)} %collective-permute-done.refs_1_), channel_id=1, source_target_pairs={{0,2},{2,0},{1,3},{3,1},{4,6},{6,4},{5,7},{7,5},{8,10},{10,8},{9,1... | collective-permute-start | bytes 417800 | tf_op jit(solution)/shard_map/ppermute | solution.py:314
  19.6 5.6 %collective-permute-start.6 = (bf16[32,2176]{1,0:T(8,128)(2,1)S(1)}, bf16[32,2176]{1,0:T(8,128)(2,1)S(1)}, u32[]{:S(2)}, u32[]{:S(2)}) collective-permute-start(bf16[32,2176]{1,0:T(8,128)(2,1)S(1)} %collective-permute-done.1.after_ref.refs_2_), channel_id=1, source_target_pairs={{0,2},{2,0},{1,3},{3,1},{4,6},{6,4},{5,7},{7,5},{8,10},{10,8},{9,1... | collective-permute-start | bytes 417800 | tf_op jit(solution)/shard_map/ppermute | solution.py:314
  25.2 2.9 %collective-permute-start.7 = (bf16[128,4224]{1,0:T(8,128)(2,1)S(1)}, bf16[128,4224]{1,0:T(8,128)(2,1)S(1)}, u32[]{:S(2)}, u32[]{:S(2)}) collective-permute-start(bf16[128,4224]{1,0:T(8,128)(2,1)S(1)} %collect.1.held_ref), channel_id=1, source_target_pairs={{0,1},{1,0},{2,3},{3,2},{4,5},{5,4},{6,7},{7,6},{8,9},{9,8},{10,11... | collective-permute-start | bytes 3244040 | tf_op jit(solution)/shard_map/ppermute | solution.py:314
  35.7 2.4 %collective-permute-start.8 = (bf16[128,1152]{1,0:T(8,128)(2,1)S(1)}, bf16[128,1152]{1,0:T(8,128)(2,1)S(1)}, u32[]{:S(2)}, u32[]{:S(2)}) collective-permute-start(bf16[128,1152]{1,0:T(8,128)(2,1)S(1)} %get-tuple-element.54), channel_id=1, source_target_pairs={{0,1},{1,0},{2,3},{3,2},{4,5},{5,4},{6,7},{7,6},{8,9},{9,8},{10,11... | collective-permute-start | bytes 884744 | tf_op jit(solution)/shard_map/ppermute | solution.py:314
  38.1 11.8 %collective-permute-start.14 = (bf16[4,256,1152]{2,1,0:T(8,128)(2,1)S(1)}, bf16[4,256,1152]{2,1,0:T(8,128)(2,1)S(1)}, u32[]{:S(2)}, u32[]{:S(2)}) collective-permute-start(bf16[4,256,1152]{2,1,0:T(8,128)(2,1)S(1)} %get-tuple-element.59.grads_ref), channel_id=1, source_target_pairs={{0,1},{1,0},{2,3},{3,2},{4,5},{5,4},{6,7},{7,6},{8,9},{9,8},{10,11... | collective-permute-start | bytes 7077896 | tf_op jit(solution)/shard_map/ppermute | solution.py:314
  38.2 9.5 %collective-permute-start.9 = (bf16[128,1152]{1,0:T(8,128)(2,1)S(1)}, bf16[128,1152]{1,0:T(8,128)(2,1)S(1)}, u32[]{:S(2)}, u32[]{:S(2)}) collective-permute-start(bf16[128,1152]{1,0:T(8,128)(2,1)S(1)} %sum_over_cores.1), channel_id=1, source_target_pairs={{0,2},{2,0},{1,3},{3,1},{4,6},{6,4},{5,7},{7,5},{8,10},{10,8},{9,1... | collective-permute-start | bytes 884744 | tf_op jit(solution)/shard_map/ppermute | solution.py:314
  38.6 9.1 %collective-permute-start.10 = (bf16[128,1152]{1,0:T(8,128)(2,1)S(1)}, bf16[128,1152]{1,0:T(8,128)(2,1)S(1)}, u32[]{:S(2)}, u32[]{:S(2)}) collective-permute-start(bf16[128,1152]{1,0:T(8,128)(2,1)S(1)} %get-tuple-element.58), channel_id=1, source_target_pairs={{0,1},{1,0},{2,3},{3,2},{4,5},{5,4},{6,7},{7,6},{8,9},{9,8},{10,11... | collective-permute-start | bytes 884744 | tf_op jit(solution)/shard_map/ppermute | solution.py:314
  47.8 9.1 %collective-permute-start.11 = (bf16[32,1152]{1,0:T(8,128)(2,1)S(1)}, bf16[32,1152]{1,0:T(8,128)(2,1)S(1)}, u32[]{:S(2)}, u32[]{:S(2)}) collective-permute-start(bf16[32,1152]{1,0:T(8,128)(2,1)S(1)} %get-tuple-element.66), channel_id=1, source_target_pairs={{0,12},{4,0},{8,4},{12,8},{1,13},{5,1},{9,5},{13,9},{2,14},{6,2},{... | collective-permute-start | bytes 221192 | tf_op jit(solution)/shard_map/ppermute | solution.py:314
  48.8 8.0 %collective-permute-start.12 = (bf16[32,1152]{1,0:T(8,128)(2,1)S(1)}, bf16[32,1152]{1,0:T(8,128)(2,1)S(1)}, u32[]{:S(2)}, u32[]{:S(2)}) collective-permute-start(bf16[32,1152]{1,0:T(8,128)(2,1)S(1)} %get-tuple-element.67), channel_id=1, source_target_pairs={{0,8},{4,12},{8,0},{12,4},{1,9},{5,13},{9,1},{13,5},{2,10},{6,14},... | collective-permute-start | bytes 221192 | tf_op jit(solution)/shard_map/ppermute | solution.py:314
  48.8 8.0 %copy-start = (s32[32,8]{0,1:T(8,128)S(1)}, s32[32,8]{0,1:T(8,128)}, u32[]{:S(2)}) copy-start(s32[32,8]{0,1:T(8,128)} %param.9) | copy-start | bytes 3076
  48.8 8.0 %collective-permute-start.13 = (bf16[32,1152]{1,0:T(8,128)(2,1)S(1)}, bf16[32,1152]{1,0:T(8,128)(2,1)S(1)}, u32[]{:S(2)}, u32[]{:S(2)}) collective-permute-start(bf16[32,1152]{1,0:T(8,128)(2,1)S(1)} %get-tuple-element.68), channel_id=1, source_target_pairs={{0,4},{4,8},{8,12},{12,0},{1,5},{5,9},{9,13},{13,1},{2,6},{6,10},{... | collective-permute-start | bytes 221192 | tf_op jit(solution)/shard_map/ppermute | solution.py:314

commit v7 on v6

--- a/solution.py
+++ b/solution.py
@@ -185,17 +185,28 @@
     sent_ref[:, wide:] = inners[share:].astype(jnp.bfloat16)
 
 
-def rows_kernel(n_tensor, both_ref, inners_ref, w_in, kept_ref, sent_ref):
-    row_pass(0, n_tensor, both_ref[...], inners_ref[...], w_in, kept_ref, sent_ref)
-
-
-def forward_call(kernel, name, inputs, out_shape, flops, distant=(), scratch=()):
+def rows_kernel(n_tensor, part, both_ref, inners_ref, w_in, *refs):
+    kept_ref, sent_ref = refs[-2:]
+    wide = w_in.shape[0] // n_tensor
+    step, share = wide // 2, both_ref.shape[0] // 2
+    at = pl.ds(pl.multiple_of(lax.axis_index("tensor") * wide + part * step, step), step)
+    here = pl.ds(part * step, step)
+    total = lax.dot_general(both_ref[...], w_in[at, :], NT, preferred_element_type=jnp.float32)
+    kept_ref[:, here] = total[:share]
+    sent_ref[:, here] = total[share:].astype(jnp.bfloat16)
+    if part == 0:
+        kept_ref[:, wide:] = inners_ref[:share, :]
+        sent_ref[:, wide:] = inners_ref[share:, :].astype(jnp.bfloat16)
+
+
+def forward_call(kernel, name, inputs, out_shape, flops, distant=(), scratch=(), aliases={}):
     return pl.pallas_call(
         kernel,
         in_specs=[VMEM] * len(inputs) + [ANY] * len(distant),
         out_specs=[VMEM] * len(out_shape),
         out_shape=out_shape,
         scratch_shapes=scratch,
+        input_output_aliases=aliases,
         compiler_params=pltpu.CompilerParams(vmem_limit_bytes=20 * MIB),
         cost_estimate=pl.CostEstimate(flops=flops, bytes_accessed=1024, transcendentals=0),
         name=name,
@@ -220,12 +231,14 @@
     return forward_call(kernel, "routed_forward", [held, got, w_in], shapes, flops, [w_down], scratch)
 
 
-def row_sums(both, inners, w_in, n_tensor):
+def row_sums(both, inners, w_in, n_tensor, part, into=()):
     tokens, d = both.shape[0], w_in.shape[0]
     sums = (tokens // 2, d // n_tensor + META)
     shapes = [pltpu.VMEM(sums, jnp.float32), pltpu.VMEM(sums, jnp.bfloat16)]
-    kernel = functools.partial(rows_kernel, n_tensor)
-    return forward_call(kernel, "row_sums", [both, inners, w_in], shapes, 2 * tokens * d * w_in.shape[1])
+    kernel = functools.partial(rows_kernel, n_tensor, part)
+    flops = tokens * d * w_in.shape[1]
+    aliases = {3 + i: i for i in range(len(into))}
+    return forward_call(kernel, "row_sums", [both, inners, w_in, *into], shapes, flops, aliases=aliases)
 
 
 def weight_kernel(swap, held_ref, got_ref, grads_ref, *refs):
@@ -441,7 +454,7 @@
     swapped = shift(held, "dp", 1)
     grads, both, inners, kept, sent = forward(held, swapped, w_in, w_down, own, n_tensor, top)
     got = shift(sent, "dp", 1)
-    kept_here, sent_here = row_sums(both, inners, w_in, n_tensor)
+    kept_here, sent_here = row_sums(both, inners, w_in, n_tensor, 0)
     got, sent_here, grads = lax.optimization_barrier((got, sent_here, grads))
     half = (tokens // 2, wide + META)
     there = pl.pallas_call(
@@ -454,6 +467,8 @@
         name="sum_over_cores",
     )(*near(kept, got))
     crossed = shift(there, "tensor", 1)
+    both, there = lax.optimization_barrier((both, there))
+    kept_here, sent_here = row_sums(both, inners, w_in, n_tensor, 1, (kept_here, sent_here))
     got_here = shift(sent_here, "dp", 1)
     got_grads = shift(grads, "dp", 1)
     outputs = weight_grads(held, swapped, grads, local_count)

time: 57.9 us -> 57.4 us (level)
  waiting for transfers between devices: 11.2 us -> 10.3 us
    ppermute x15, waiting for transfers between devices: 11.2 us -> 10.3 us  [shift(): return lax.ppermute(x, axis, [(i, (i + by) % count) for i in range(count)])]
    pallas_call x2 -> x3, Pallas kernels: 9.3 us -> 9.5 us  [forward_call(): pl.pallas_call(kernel, in_specs=[VMEM] * len(inputs) + [ANY] * len(distan...]
  transfers between devices with their start and end apart: 15 -> 15, of which waited for: 5 -> 7; matrix products, arithmetic and copies ran while one was open for 0% -> 0% of each run, Pallas kernels for 37% -> 38%
where the time goes in v7:
time: 57.4 us; the launch traced here: 57.2 us
  Pallas kernels  31.1 us (54%)
  starting transfers between devices  15 us (26%)
  waiting for transfers between devices  10.3 us (18%)
  between operations  0.77 us (1%)
    ppermute x15, starting transfers between devices, shift(): return lax.ppermute(x, axis, [(i, (i + by) % count) for i in range(count)])  15 us
    pallas_call x2, Pallas kernels, weight_grads(): pl.pallas_call(functools.partial(weight_kernel, into is not None), in_spe...  13.9 us
    ppermute x15, waiting for transfers between devices, shift(): return lax.ppermute(x, axis, [(i, (i + by) % count) for i in range(count)])  10.3 us
    pallas_call x3, Pallas kernels, forward_call(): pl.pallas_call(kernel, in_specs=[VMEM] * len(inputs) + [ANY] * len(distan...  9.5 us
    pallas_call x2, Pallas kernels, load_weights(): pl.pallas_call(functools.partial(load_kernel_into if kept else load_kerne...  5.69 us
  transfers between devices with their start and end apart: 15, of which 7 were waited for; matrix products, arithmetic and copies ran while one was open for 0% of the time, Pallas kernels for 38%

profile of v7, /device:TPU:0, one launch (start us, length us, event | category | flops | bytes accessed | tf_op | source)
XLA Modules:
  0.0 57.2 jit_solution(5743493129841755011)
XLA Ops:
  0.6 0.9 %pack_tokens.1.refs_0_ = bf16[32,2176]{1,0:T(8,128)(2,1)S(1)} custom-call(bf16[32,1024]{1,0:T(8,128)(2,1)} %act_hbm.1, bf16[32,1024]{1,0:T(8,128)(2,1)} %og_hbm.1, s32[8,32]{1,0:T(8,128)} %bitcast.3, bf16[8,32]{1,0:T(8,128)(2,1)} %bitcast.5), custom_call_target="tpu_custom_call" | custom-call | tf_op jit(solution)/shard_map/pack_tokens/pallas_call | solution.py:50
  1.5 5.1 %collective-permute-start.3 = (bf16[32,2176]{1,0:T(8,128)(2,1)S(1)}, bf16[32,2176]{1,0:T(8,128)(2,1)S(1)}, u32[]{:S(2)}, u32[]{:S(2)}) collective-permute-start(bf16[32,2176]{1,0:T(8,128)(2,1)S(1)} %pack_tokens.1.refs_0_), channel_id=1, source_target_pairs={{0,12},{4,0},{8,4},{12,8},{1,13},{5,1},{9,5},{13,9},{2,14},{6,2},{... | collective-permute-start | bytes 417800 | tf_op jit(solution)/shard_map/ppermute | solution.py:327
  6.6 0.0 collective-permute-start
  6.7 1.5 %collective-permute-start.2 = (bf16[32,2176]{1,0:T(8,128)(2,1)S(1)}, bf16[32,2176]{1,0:T(8,128)(2,1)S(1)}, u32[]{:S(2)}, u32[]{:S(2)}) collective-permute-start(bf16[32,2176]{1,0:T(8,128)(2,1)S(1)} %pack_tokens.1.refs_0_), channel_id=1, source_target_pairs={{0,2},{2,0},{1,3},{3,1},{4,6},{6,4},{5,7},{7,5},{8,10},{10,8},{9,1... | collective-permute-start | bytes 417800 | tf_op jit(solution)/shard_map/ppermute | solution.py:327
  8.1 1.0 %collective-permute-start.1 = (bf16[32,2176]{1,0:T(8,128)(2,1)S(1)}, bf16[32,2176]{1,0:T(8,128)(2,1)S(1)}, u32[]{:S(2)}, u32[]{:S(2)}) collective-permute-start(bf16[32,2176]{1,0:T(8,128)(2,1)S(1)} %pack_tokens.1.refs_0_), channel_id=1, source_target_pairs={{0,8},{4,12},{8,0},{12,4},{1,9},{5,13},{9,1},{13,5},{2,10},{6,14},... | collective-permute-start | bytes 417800 | tf_op jit(solution)/shard_map/ppermute | solution.py:327
  9.2 1.6 %collective-permute-done.3.refs_3_ = bf16[32,2176]{1,0:T(8,128)(2,1)S(1)} collective-permute-done((bf16[32,2176]{1,0:T(8,128)(2,1)S(1)}, bf16[32,2176]{1,0:T(8,128)(2,1)S(1)}, u32[]{:S(2)}, u32[]{:S(2)}) %collective-permute-start.3) | collective-permute-done | bytes 139296 | tf_op jit(solution)/shard_map/ppermute | solution.py:327
  10.7 1.5 %collective-permute-start.4 = (bf16[32,2176]{1,0:T(8,128)(2,1)S(1)}, bf16[32,2176]{1,0:T(8,128)(2,1)S(1)}, u32[]{:S(2)}, u32[]{:S(2)}) collective-permute-start(bf16[32,2176]{1,0:T(8,128)(2,1)S(1)} %collective-permute-done.3.refs_3_), channel_id=1, source_target_pairs={{0,2},{2,0},{1,3},{3,1},{4,6},{6,4},{5,7},{7,5},{8,10},{10,8},{9,1... | collective-permute-start | bytes 417800 | tf_op jit(solution)/shard_map/ppermute | solution.py:327
  12.2 2.9 %collective-permute-done.refs_1_ = bf16[32,2176]{1,0:T(8,128)(2,1)S(1)} collective-permute-done((bf16[32,2176]{1,0:T(8,128)(2,1)S(1)}, bf16[32,2176]{1,0:T(8,128)(2,1)S(1)}, u32[]{:S(2)}, u32[]{:S(2)}) %collective-permute-start) | collective-permute-done | bytes 139296 | tf_op jit(solution)/shard_map/ppermute | solution.py:327
  15.1 1.4 %collective-permute-start.5 = (bf16[32,2176]{1,0:T(8,128)(2,1)S(1)}, bf16[32,2176]{1,0:T(8,128)(2,1)S(1)}, u32[]{:S(2)}, u32[]{:S(2)}) collective-permute-start(bf16[32,2176]{1,0:T(8,128)(2,1)S(1)} %collective-permute-done.refs_1_), channel_id=1, source_target_pairs={{0,2},{2,0},{1,3},{3,1},{4,6},{6,4},{5,7},{7,5},{8,10},{10,8},{9,1... | collective-permute-start | bytes 417800 | tf_op jit(solution)/shard_map/ppermute | solution.py:327
  16.6 0.0 collective-permute-done.2.refs_4_
  16.6 3.0 %collective-permute-done.1.after_ref.refs_2_ = bf16[32,2176]{1,0:T(8,128)(2,1)S(1)} collective-permute-done((bf16[32,2176]{1,0:T(8,128)(2,1)S(1)}, bf16[32,2176]{1,0:T(8,128)(2,1)S(1)}, u32[]{:S(2)}, u32[]{:S(2)}) %collective-permute-start.1) | collective-permute-done | bytes 139296 | tf_op jit(solution)/shard_map/ppermute | solution.py:327
  19.5 0.0 collective-permute-done.4.refs_7_
  19.6 0.9 %collective-permute-start.6 = (bf16[32,2176]{1,0:T(8,128)(2,1)S(1)}, bf16[32,2176]{1,0:T(8,128)(2,1)S(1)}, u32[]{:S(2)}, u32[]{:S(2)}) collective-permute-start(bf16[32,2176]{1,0:T(8,128)(2,1)S(1)} %collective-permute-done.1.after_ref.refs_2_), channel_id=1, source_target_pairs={{0,2},{2,0},{1,3},{3,1},{4,6},{6,4},{5,7},{7,5},{8,10},{10,8},{9,1... | collective-permute-start | bytes 417800 | tf_op jit(solution)/shard_map/ppermute | solution.py:327
  20.4 2.8 %load_weights.2.refs_2_ = bf16[2048,3072]{1,0:T(8,128)(2,1)S(1)} custom-call(bf16[32,2176]{1,0:T(8,128)(2,1)S(1)} %collective-permute-done.1.after_ref.refs_2_, bf16[8,2048,384]{2,1,0:T(8,128)(2,1)} %refs_0_.3, bf16[8,2048,384]{2,1,0:T(8,128)(2,1)} %refs_1_.3), custom_call_target="tpu_custom_call" | custom-call | bytes 1024 | tf_op jit(solution)/shard_map/load_weights/pallas_call | solution.py:121
  23.2 0.0 collective-permute-done.5.refs_5_
  23.3 1.9 %collective-permute-done.6.refs_6_.after_ref = bf16[32,2176]{1,0:T(8,128)(2,1)S(1)} collective-permute-done((bf16[32,2176]{1,0:T(8,128)(2,1)S(1)}, bf16[32,2176]{1,0:T(8,128)(2,1)S(1)}, u32[]{:S(2)}, u32[]{:S(2)}) %collective-permute-start.6) | collective-permute-done | bytes 139296 | tf_op jit(solution)/shard_map/ppermute | solution.py:327
  25.1 0.1 collect.1.held_ref
  25.2 0.1 collective-permute-start.7
  25.3 2.8 %load_weights.3.w_in = bf16[2048,3072]{1,0:T(8,128)(2,1)S(1)} custom-call(bf16[32,2176]{1,0:T(8,128)(2,1)S(1)} %collective-permute-done.6.refs_6_.after_ref, bf16[8,2048,384]{2,1,0:T(8,128)(2,1)} %refs_0_.3, bf16[8,2048,384]{2,1,0:T(8,128)(2,1)} %refs_1_.3, bf16[2048,3072]{1,0:T(8,128)(2,1)S(1)} %load_weights.2.refs_2_), custom_call_target="tpu_custom_call", output_to_operand_aliasing={{}: (3, {})} | custom-call | bytes 1024 | tf_op jit(solution)/shard_map/load_weights/pallas_call | solution.py:121
  28.2 0.0 collective-permute-done.7.got_ref
  28.2 7.5 %routed_forward.1 = (bf16[4,256,1152]{2,1,0:T(8,128)(2,1)S(1)}, bf16[256,3072]{1,0:T(8,128)(2,1)S(1)}, f32[256,128]{1,0:T(8,128)S(1)}, f32[128,1152]{1,0:T(8,128)S(1)}, bf16[128,1152]{1,0:T(8,128)(2,1)S(1)}) custom-call(bf16[128,4224]{1,0:T(8,128)(2,1)S(1)} %collect.1.held_ref, bf16[128,4224]{1,0:T(8,128)(2,1)S(1)} %collective-permute-done.7.got_ref, ...), custom_call_target="tpu_custom_call" | custom-call | flops 6442450944 | bytes 1024 | tf_op jit(solution)/shard_map/routed_forward/pallas_call | solution.py:203
  35.7 0.6 collective-permute-start.8
  36.2 1.0 %row_sums.2 = (f32[128,1152]{1,0:T(8,128)S(1)}, bf16[128,1152]{1,0:T(8,128)(2,1)S(1)}) custom-call(bf16[256,3072]{1,0:T(8,128)(2,1)S(1)} %get-tuple-element.60.both_ref, f32[256,128]{1,0:T(8,128)S(1)} %get-tuple-element.56.inners_ref, bf16[2048,3072]{1,0:T(8,128)(2,1)S(1)} %load_weights.3.w_in), custom_call_target="tpu_custom_call" | custom-call | flops 1610612736 | bytes 1024 | tf_op jit(solution)/shard_map/row_sums/pallas_call | solution.py:203
  37.2 0.2 collective-permute-done.8.got_ref
  37.4 0.4 collective-permute-start.14
  37.8 0.1 sum_over_cores.1
  37.9 0.4 collective-permute-start.9
  38.2 1.0 %row_sums.3 = (f32[128,1152]{1,0:T(8,128)S(1)}, bf16[128,1152]{1,0:T(8,128)(2,1)S(1)}) custom-call(bf16[256,3072]{1,0:T(8,128)(2,1)S(1)} %get-tuple-element.60.both_ref, f32[256,128]{1,0:T(8,128)S(1)} %get-tuple-element.56.inners_ref, bf16[2048,3072]{1,0:T(8,128)(2,1)S(1)} %load_weights.3.w_in, ...), custom_call_target="tpu_custom_call", output_to_operand_aliasing={{0}: (3, {}), {1}: (4, {})} | custom-call | flops 1610612736 | bytes 1024 | tf_op jit(solution)/shard_map/row_sums/pallas_call | solution.py:203
  39.3 0.1 collective-permute-start.10
  39.3 7.0 %weight_grads.2 = (bf16[8,2048,384]{2,1,0:T(8,128)(2,1)}, bf16[8,2048,384]{2,1,0:T(8,128)(2,1)}, bf16[8,384,2048]{2,1,0:T(8,128)(2,1)}) custom-call(bf16[128,4224]{1,0:T(8,128)(2,1)S(1)} %collect.1.held_ref, bf16[128,4224]{1,0:T(8,128)(2,1)S(1)} %collective-permute-done.7.got_ref, bf16[4,256,1152]{2,1,0:T(8,128)(2,1)S(1)} %get-tuple-element.65.grads_ref), custom_call_target="tpu_custom_call" | custom-call | flops 4831838208 | bytes 18874368 | tf_op jit(solution)/shard_map/weight_grads/pallas_call | solution.py:283
  46.3 0.0 collective-permute-done.10.core_ref
  46.3 0.7 %collective-permute-done.9.got_ref = bf16[128,1152]{1,0:T(8,128)(2,1)S(1)} collective-permute-done((bf16[128,1152]{1,0:T(8,128)(2,1)S(1)}, bf16[128,1152]{1,0:T(8,128)(2,1)S(1)}, u32[]{:S(2)}, u32[]{:S(2)}) %collective-permute-start.9) | collective-permute-done | bytes 294944 | tf_op jit(solution)/shard_map/ppermute | solution.py:327
  47.0 0.1 sum_over_tensor.1
  47.1 1.6 %collective-permute-start.11 = (bf16[32,1152]{1,0:T(8,128)(2,1)S(1)}, bf16[32,1152]{1,0:T(8,128)(2,1)S(1)}, u32[]{:S(2)}, u32[]{:S(2)}) collective-permute-start(bf16[32,1152]{1,0:T(8,128)(2,1)S(1)} %get-tuple-element.72), channel_id=1, source_target_pairs={{0,12},{4,0},{8,4},{12,8},{1,13},{5,1},{9,5},{13,9},{2,14},{6,2},{... | collective-permute-start | bytes 221192 | tf_op jit(solution)/shard_map/ppermute | solution.py:327
  48.6 0.0 collective-permute-start.12
  48.6 0.0 copy-start
  48.6 0.6 %collective-permute-start.13 = (bf16[32,1152]{1,0:T(8,128)(2,1)S(1)}, bf16[32,1152]{1,0:T(8,128)(2,1)S(1)}, u32[]{:S(2)}, u32[]{:S(2)}) collective-permute-start(bf16[32,1152]{1,0:T(8,128)(2,1)S(1)} %get-tuple-element.74), channel_id=1, source_target_pairs={{0,4},{4,8},{8,12},{12,0},{1,5},{5,9},{9,13},{13,1},{2,6},{6,10},{... | collective-permute-start | bytes 221192 | tf_op jit(solution)/shard_map/ppermute | solution.py:327
  49.3 0.0 collective-permute-done.14.grads_ref
  49.3 7.0 %weight_grads.3 = (bf16[8,2048,384]{2,1,0:T(8,128)(2,1)}, bf16[8,2048,384]{2,1,0:T(8,128)(2,1)}, bf16[8,384,2048]{2,1,0:T(8,128)(2,1)}) custom-call(bf16[128,4224]{1,0:T(8,128)(2,1)S(1)} %collect.1.held_ref, bf16[128,4224]{1,0:T(8,128)(2,1)S(1)} %collective-permute-done.7.got_ref, ...), custom_call_target="tpu_custom_call", output_to_operand_aliasing={{0}: (3, {}), {1}: (4, {}), {2}: (5, {})} | custom-call | flops 4831838208 | bytes 18874368 | tf_op jit(solution)/shard_map/weight_grads/pallas_call | solution.py:283
  56.3 0.0 collective-permute-done.11.refs_0_
  56.3 0.1 collective-permute-done.12.refs_1_
  56.4 0.0 collective-permute-done.13.refs_2_
  56.4 0.0 copy-done
  56.4 0.8 %sum_over_experts.1 = (bf16[32,1024]{1,0:T(8,128)(2,1)}, f32[8,32]{1,0:T(8,128)}) custom-call(s32[8,32]{1,0:T(8,128)S(1)} %bitcast.4, f32[32,1152]{1,0:T(8,128)S(1)} %get-tuple-element.71.own_ref, bf16[32,1152]{1,0:T(8,128)(2,1)S(1)} %collective-permute-done.11.refs_0_, bf16[32,1152]{1,0:T(8,128)(2,1)S(1)} %collective-permute-done.12.refs_1_, ...), custom_call_target="tpu_custom_call" | custom-call | tf_op jit(solution)/shard_map/sum_over_experts/pallas_call | solution.py:488
Async XLA Ops:
  1.5 9.2 %collective-permute-start.3 = (bf16[32,2176]{1,0:T(8,128)(2,1)S(1)}, bf16[32,2176]{1,0:T(8,128)(2,1)S(1)}, u32[]{:S(2)}, u32[]{:S(2)}) collective-permute-start(bf16[32,2176]{1,0:T(8,128)(2,1)S(1)} %pack_tokens.1.refs_0_), channel_id=1, source_target_pairs={{0,12},{4,0},{8,4},{12,8},{1,13},{5,1},{9,5},{13,9},{2,14},{6,2},{... | collective-permute-start | bytes 417800 | tf_op jit(solution)/shard_map/ppermute | solution.py:327
  6.6 8.5 %collective-permute-start = (bf16[32,2176]{1,0:T(8,128)(2,1)S(1)}, bf16[32,2176]{1,0:T(8,128)(2,1)S(1)}, u32[]{:S(2)}, u32[]{:S(2)}) collective-permute-start(bf16[32,2176]{1,0:T(8,128)(2,1)S(1)} %pack_tokens.1.refs_0_), channel_id=1, source_target_pairs={{0,4},{4,8},{8,12},{12,0},{1,5},{5,9},{9,13},{13,1},{2,6},{6,10},{... | collective-permute-start | bytes 417800 | tf_op jit(solution)/shard_map/ppermute | solution.py:327
  6.7 9.9 %collective-permute-start.2 = (bf16[32,2176]{1,0:T(8,128)(2,1)S(1)}, bf16[32,2176]{1,0:T(8,128)(2,1)S(1)}, u32[]{:S(2)}, u32[]{:S(2)}) collective-permute-start(bf16[32,2176]{1,0:T(8,128)(2,1)S(1)} %pack_tokens.1.refs_0_), channel_id=1, source_target_pairs={{0,2},{2,0},{1,3},{3,1},{4,6},{6,4},{5,7},{7,5},{8,10},{10,8},{9,1... | collective-permute-start | bytes 417800 | tf_op jit(solution)/shard_map/ppermute | solution.py:327
  8.1 11.4 %collective-permute-start.1 = (bf16[32,2176]{1,0:T(8,128)(2,1)S(1)}, bf16[32,2176]{1,0:T(8,128)(2,1)S(1)}, u32[]{:S(2)}, u32[]{:S(2)}) collective-permute-start(bf16[32,2176]{1,0:T(8,128)(2,1)S(1)} %pack_tokens.1.refs_0_), channel_id=1, source_target_pairs={{0,8},{4,12},{8,0},{12,4},{1,9},{5,13},{9,1},{13,5},{2,10},{6,14},... | collective-permute-start | bytes 417800 | tf_op jit(solution)/shard_map/ppermute | solution.py:327
  10.7 8.8 %collective-permute-start.4 = (bf16[32,2176]{1,0:T(8,128)(2,1)S(1)}, bf16[32,2176]{1,0:T(8,128)(2,1)S(1)}, u32[]{:S(2)}, u32[]{:S(2)}) collective-permute-start(bf16[32,2176]{1,0:T(8,128)(2,1)S(1)} %collective-permute-done.3.refs_3_), channel_id=1, source_target_pairs={{0,2},{2,0},{1,3},{3,1},{4,6},{6,4},{5,7},{7,5},{8,10},{10,8},{9,1... | collective-permute-start | bytes 417800 | tf_op jit(solution)/shard_map/ppermute | solution.py:327
  15.1 8.1 %collective-permute-start.5 = (bf16[32,2176]{1,0:T(8,128)(2,1)S(1)}, bf16[32,2176]{1,0:T(8,128)(2,1)S(1)}, u32[]{:S(2)}, u32[]{:S(2)}) collective-permute-start(bf16[32,2176]{1,0:T(8,128)(2,1)S(1)} %collective-permute-done.refs_1_), channel_id=1, source_target_pairs={{0,2},{2,0},{1,3},{3,1},{4,6},{6,4},{5,7},{7,5},{8,10},{10,8},{9,1... | collective-permute-start | bytes 417800 | tf_op jit(solution)/shard_map/ppermute | solution.py:327
  19.6 5.6 %collective-permute-start.6 = (bf16[32,2176]{1,0:T(8,128)(2,1)S(1)}, bf16[32,2176]{1,0:T(8,128)(2,1)S(1)}, u32[]{:S(2)}, u32[]{:S(2)}) collective-permute-start(bf16[32,2176]{1,0:T(8,128)(2,1)S(1)} %collective-permute-done.1.after_ref.refs_2_), channel_id=1, source_target_pairs={{0,2},{2,0},{1,3},{3,1},{4,6},{6,4},{5,7},{7,5},{8,10},{10,8},{9,1... | collective-permute-start | bytes 417800 | tf_op jit(solution)/shard_map/ppermute | solution.py:327
  25.2 2.9 %collective-permute-start.7 = (bf16[128,4224]{1,0:T(8,128)(2,1)S(1)}, bf16[128,4224]{1,0:T(8,128)(2,1)S(1)}, u32[]{:S(2)}, u32[]{:S(2)}) collective-permute-start(bf16[128,4224]{1,0:T(8,128)(2,1)S(1)} %collect.1.held_ref), channel_id=1, source_target_pairs={{0,1},{1,0},{2,3},{3,2},{4,5},{5,4},{6,7},{7,6},{8,9},{9,8},{10,11... | collective-permute-start | bytes 3244040 | tf_op jit(solution)/shard_map/ppermute | solution.py:327
  35.7 1.8 %collective-permute-start.8 = (bf16[128,1152]{1,0:T(8,128)(2,1)S(1)}, bf16[128,1152]{1,0:T(8,128)(2,1)S(1)}, u32[]{:S(2)}, u32[]{:S(2)}) collective-permute-start(bf16[128,1152]{1,0:T(8,128)(2,1)S(1)} %get-tuple-element.55), channel_id=1, source_target_pairs={{0,1},{1,0},{2,3},{3,2},{4,5},{5,4},{6,7},{7,6},{8,9},{9,8},{10,11... | collective-permute-start | bytes 884744 | tf_op jit(solution)/shard_map/ppermute | solution.py:327
  37.4 11.8 %collective-permute-start.14 = (bf16[4,256,1152]{2,1,0:T(8,128)(2,1)S(1)}, bf16[4,256,1152]{2,1,0:T(8,128)(2,1)S(1)}, u32[]{:S(2)}, u32[]{:S(2)}) collective-permute-start(bf16[4,256,1152]{2,1,0:T(8,128)(2,1)S(1)} %get-tuple-element.65.grads_ref), channel_id=1, source_target_pairs={{0,1},{1,0},{2,3},{3,2},{4,5},{5,4},{6,7},{7,6},{8,9},{9,8},{10,11... | collective-permute-start | bytes 7077896 | tf_op jit(solution)/shard_map/ppermute | solution.py:327
  37.9 9.1 %collective-permute-start.9 = (bf16[128,1152]{1,0:T(8,128)(2,1)S(1)}, bf16[128,1152]{1,0:T(8,128)(2,1)S(1)}, u32[]{:S(2)}, u32[]{:S(2)}) collective-permute-start(bf16[128,1152]{1,0:T(8,128)(2,1)S(1)} %sum_over_cores.1), channel_id=1, source_target_pairs={{0,2},{2,0},{1,3},{3,1},{4,6},{6,4},{5,7},{7,5},{8,10},{10,8},{9,1... | collective-permute-start | bytes 884744 | tf_op jit(solution)/shard_map/ppermute | solution.py:327
  39.3 7.0 %collective-permute-start.10 = (bf16[128,1152]{1,0:T(8,128)(2,1)S(1)}, bf16[128,1152]{1,0:T(8,128)(2,1)S(1)}, u32[]{:S(2)}, u32[]{:S(2)}) collective-permute-start(bf16[128,1152]{1,0:T(8,128)(2,1)S(1)} %get-tuple-element.64), channel_id=1, source_target_pairs={{0,1},{1,0},{2,3},{3,2},{4,5},{5,4},{6,7},{7,6},{8,9},{9,8},{10,11... | collective-permute-start | bytes 884744 | tf_op jit(solution)/shard_map/ppermute | solution.py:327
  47.1 9.2 %collective-permute-start.11 = (bf16[32,1152]{1,0:T(8,128)(2,1)S(1)}, bf16[32,1152]{1,0:T(8,128)(2,1)S(1)}, u32[]{:S(2)}, u32[]{:S(2)}) collective-permute-start(bf16[32,1152]{1,0:T(8,128)(2,1)S(1)} %get-tuple-element.72), channel_id=1, source_target_pairs={{0,12},{4,0},{8,4},{12,8},{1,13},{5,1},{9,5},{13,9},{2,14},{6,2},{... | collective-permute-start | bytes 221192 | tf_op jit(solution)/shard_map/ppermute | solution.py:327
  48.6 7.7 %collective-permute-start.12 = (bf16[32,1152]{1,0:T(8,128)(2,1)S(1)}, bf16[32,1152]{1,0:T(8,128)(2,1)S(1)}, u32[]{:S(2)}, u32[]{:S(2)}) collective-permute-start(bf16[32,1152]{1,0:T(8,128)(2,1)S(1)} %get-tuple-element.73), channel_id=1, source_target_pairs={{0,8},{4,12},{8,0},{12,4},{1,9},{5,13},{9,1},{13,5},{2,10},{6,14},... | collective-permute-start | bytes 221192 | tf_op jit(solution)/shard_map/ppermute | solution.py:327
  48.6 7.7 %copy-start = (s32[32,8]{0,1:T(8,128)S(1)}, s32[32,8]{0,1:T(8,128)}, u32[]{:S(2)}) copy-start(s32[32,8]{0,1:T(8,128)} %param.9) | copy-start | bytes 3076
  48.6 7.7 %collective-permute-start.13 = (bf16[32,1152]{1,0:T(8,128)(2,1)S(1)}, bf16[32,1152]{1,0:T(8,128)(2,1)S(1)}, u32[]{:S(2)}, u32[]{:S(2)}) collective-permute-start(bf16[32,1152]{1,0:T(8,128)(2,1)S(1)} %get-tuple-element.74), channel_id=1, source_target_pairs={{0,4},{4,8},{8,12},{12,0},{1,5},{5,9},{9,13},{13,1},{2,6},{6,10},{... | collective-permute-start | bytes 221192 | tf_op jit(solution)/shard_map/ppermute | solution.py:327
